TPU v7x, 256 devices: a whole 4x4x8 slice. The times are simulated.
256 devices in a mesh: chain: 16 (over y, x), group: 16 (over z, core).
Axes of the slice: x: 4, y: 4, z: 8, core: 2. Of those that a mesh axis runs over, the one named last changes fastest.
Arguments:
- train_emb: bfloat16 [4096, 1024], P(('chain', 'group')), may hold values from -6 to 6
- cand_emb: bfloat16 [16384, 1024], P('group'), may hold values from -6 to 6
- factor: float32 [4096, 4096], P('chain'), may hold values from -0.09375 to 0.09375
- diag_inverse: float32 [4096, 256], P('chain'), as said below
- targets: float32 [4096], P('chain'), may hold values from -0.09375 to 0.09375
Outputs:
- whitened: float32 [4096, 16384], P('chain', 'group')
- post_mean: float32 [16384], P('group')
Inputs may be any that keep to these rules, and one draw needn't show every extreme that they name: Each block of 256 rows of diag_inverse is lower triangular with a positive diagonal.
All inputs are finite; a program needn't handle non-finite values.
Results may differ from a plain program's by a relative error of at most 0.0003.
Values may be sent and summed in bfloat16 or wider, within the bound.
No kernel may reach another device: no remote copies, remote signals or barrier semaphores. Data moves between devices by JAX's collectives and lax.ppermute only.
A program may use at most 64 MiB of HBM per device.

v0:
```python
import math

import jax
import jax.numpy as jnp
from jax import lax
from jax.sharding import PartitionSpec as P

EPS = 1e-06


def from_root(x, axis, root):
    mine = lax.axis_index(axis) == root
    return lax.psum(jnp.where(mine, x, jnp.zeros_like(x)), axis)


def chain_solve(panel, diag_inverse, factor, position, length):
    block_rows = panel.shape[0]
    width = panel.shape[1]

    def advance(section, carry):
        resid, solved, running = carry

        def finish():
            return jnp.dot(
                diag_inverse,
                resid,
                precision=lax.Precision.HIGHEST,
                preferred_element_type=jnp.float32,
            )

        def nothing():
            return jnp.zeros_like(resid)

        fresh = lax.cond(position == section, finish, nothing)
        arrived = from_root(fresh, "chain", section)
        solved = jnp.where(position == section, arrived, solved)
        columns = lax.dynamic_slice_in_dim(factor, section * block_rows, block_rows, 1)

        def subtract():
            return resid - jnp.dot(
                columns,
                arrived,
                precision=lax.Precision.HIGHEST,
                preferred_element_type=jnp.float32,
            )

        def keep():
            return resid

        resid = lax.cond(section < position, subtract, keep)
        return (resid, solved, running)

    start = (panel, jnp.zeros_like(panel), jnp.zeros((width,), jnp.float32))
    resid, solved, running = lax.fori_loop(0, length, advance, start)
    return (solved, running)


def shards(train_emb, cand_emb, factor, diag_inverse, targets):
    beta = 0.5 * math.sqrt(cand_emb.shape[1])
    cand_f = cand_emb.astype(jnp.float32)
    cand_scale = lax.rsqrt(jnp.sum(cand_f * cand_f, axis=1) + EPS)
    piece = lax.all_gather(train_emb, "group", axis=0, tiled=True)
    piece_f = piece.astype(jnp.float32)
    row_scale = lax.rsqrt(jnp.sum(piece_f * piece_f, axis=1) + EPS)
    cross = lax.dot_general(
        piece, cand_emb, (((1,), (1,)), ((), ())), preferred_element_type=jnp.float32
    )
    panel = jnp.exp(beta * cross * row_scale[:, None] * cand_scale[None, :])
    position = lax.axis_index("chain")
    length = lax.axis_size("chain")
    mean_parts = []
    solved, running = chain_solve(panel, diag_inverse, factor, position, length)
    mean_parts.append(running)
    local_mean = jnp.sum(solved * targets[:, None], axis=0)
    post_mean = lax.psum(local_mean, "chain")
    return (solved, post_mean)


def solution(mesh):
    in_specs = (
        P(("chain", "group"), None),
        P("group", None),
        P("chain", None),
        P("chain", None),
        P("chain"),
    )
    out_specs = (P("chain", "group"), P("group"))
    return jax.shard_map(shards, mesh=mesh, in_specs=in_specs, out_specs=out_specs, check_vma=False)
```

profile of v0, /device:TPU:1, one launch (start us, length us, event | category | flops | bytes accessed | tf_op | source)
XLA Modules:
  0.0 1728.3 jit_solution(12346194877566181147)
XLA Ops:
  7.2 23.1 %all_gather.3 = bf16[256,1024]{1,0:T(8,128)(2,1)S(1)} all-gather(bf16[16,1024]{1,0:T(8,128)(2,1)} %param.11), channel_id=1, replica_groups=mesh['chain'=16,'group'=16] {'group'}, dimensions={0}, use_global_device_ids=true | all-gather | bytes 557056 | tf_op jit(solution)/shard_map/all_gather | solution.py:62
  30.5 2.1 multiply_reduce_fusion
  32.6 2.4 fusion.3
  35.0 1653.8 %while.19 = (s32[]{:T(128)}, f32[256,1024]{1,0:T(8,128)S(1)}, f32[256,1024]{1,0:T(8,128)S(1)}, s32[]{:T(128)}, f32[256,256]{1,0:T(8,128)S(1)}, /*index=5*/f32[25...) while((s32[]{:T(128)}, f32[256,1024]{1,0:T(8,128)S(1)}, f32[256,1024]{1,0:T(8,128)S(1)}, ...), condition=%wide.region_8.9_spmd.clone, body=%wide.region_2.8_spmd.clone.sunk | while | flops 1611923456 | bytes 17301848 | solution.py:54
  35.1 1.1 conditional.6
  35.1 1.0 fusion.4
  36.1 1.0 broadcast_select_fusion.2
  37.2 95.8 %all-reduce.2.cloned.1.call-done = f32[256,1024]{1,0:T(8,128)} async-done(((f32[256,1024]{1,0:T(8,128)}), f32[256,1024]{1,0:T(8,128)}) %all-reduce.2.cloned.1.call-update) | async-done | bytes 1048592 | tf_op jit(solution)/shard_map/while/body/eval_jaxpr/psum | solution.py:13
  133.0 1.5 select_select_fusion.2
  134.7 1.0 broadcast_select_fusion.2
  135.8 101.1 %all-reduce.2.cloned.1.call-done = f32[256,1024]{1,0:T(8,128)} async-done(((f32[256,1024]{1,0:T(8,128)}), f32[256,1024]{1,0:T(8,128)}) %all-reduce.2.cloned.1.call-update) | async-done | bytes 1048592 | tf_op jit(solution)/shard_map/while/body/eval_jaxpr/psum | solution.py:13
  236.9 0.3 select_select_fusion.2
  237.5 1.0 broadcast_select_fusion.2
  238.6 102.3 %all-reduce.2.cloned.1.call-done = f32[256,1024]{1,0:T(8,128)} async-done(((f32[256,1024]{1,0:T(8,128)}), f32[256,1024]{1,0:T(8,128)}) %all-reduce.2.cloned.1.call-update) | async-done | bytes 1048592 | tf_op jit(solution)/shard_map/while/body/eval_jaxpr/psum | solution.py:13
  340.9 0.3 select_select_fusion.2
  341.4 1.0 broadcast_select_fusion.2
  342.5 102.0 %all-reduce.2.cloned.1.call-done = f32[256,1024]{1,0:T(8,128)} async-done(((f32[256,1024]{1,0:T(8,128)}), f32[256,1024]{1,0:T(8,128)}) %all-reduce.2.cloned.1.call-update) | async-done | bytes 1048592 | tf_op jit(solution)/shard_map/while/body/eval_jaxpr/psum | solution.py:13
  444.5 0.3 select_select_fusion.2
  445.1 1.0 broadcast_select_fusion.2
  446.2 102.0 %all-reduce.2.cloned.1.call-done = f32[256,1024]{1,0:T(8,128)} async-done(((f32[256,1024]{1,0:T(8,128)}), f32[256,1024]{1,0:T(8,128)}) %all-reduce.2.cloned.1.call-update) | async-done | bytes 1048592 | tf_op jit(solution)/shard_map/while/body/eval_jaxpr/psum | solution.py:13
  548.7 1.0 broadcast_select_fusion.2
  549.8 102.0 %all-reduce.2.cloned.1.call-done = f32[256,1024]{1,0:T(8,128)} async-done(((f32[256,1024]{1,0:T(8,128)}), f32[256,1024]{1,0:T(8,128)}) %all-reduce.2.cloned.1.call-update) | async-done | bytes 1048592 | tf_op jit(solution)/shard_map/while/body/eval_jaxpr/psum | solution.py:13
  652.4 1.0 broadcast_select_fusion.2
  653.5 102.4 %all-reduce.2.cloned.1.call-done = f32[256,1024]{1,0:T(8,128)} async-done(((f32[256,1024]{1,0:T(8,128)}), f32[256,1024]{1,0:T(8,128)}) %all-reduce.2.cloned.1.call-update) | async-done | bytes 1048592 | tf_op jit(solution)/shard_map/while/body/eval_jaxpr/psum | solution.py:13
  756.4 1.0 broadcast_select_fusion.2
  757.5 102.4 %all-reduce.2.cloned.1.call-done = f32[256,1024]{1,0:T(8,128)} async-done(((f32[256,1024]{1,0:T(8,128)}), f32[256,1024]{1,0:T(8,128)}) %all-reduce.2.cloned.1.call-update) | async-done | bytes 1048592 | tf_op jit(solution)/shard_map/while/body/eval_jaxpr/psum | solution.py:13
  859.9 0.3 select_select_fusion.2
  860.4 1.0 broadcast_select_fusion.2
  861.5 102.4 %all-reduce.2.cloned.1.call-done = f32[256,1024]{1,0:T(8,128)} async-done(((f32[256,1024]{1,0:T(8,128)}), f32[256,1024]{1,0:T(8,128)}) %all-reduce.2.cloned.1.call-update) | async-done | bytes 1048592 | tf_op jit(solution)/shard_map/while/body/eval_jaxpr/psum | solution.py:13
  963.8 0.3 select_select_fusion.2
  964.4 1.0 broadcast_select_fusion.2
  965.5 102.0 %all-reduce.2.cloned.1.call-done = f32[256,1024]{1,0:T(8,128)} async-done(((f32[256,1024]{1,0:T(8,128)}), f32[256,1024]{1,0:T(8,128)}) %all-reduce.2.cloned.1.call-update) | async-done | bytes 1048592 | tf_op jit(solution)/shard_map/while/body/eval_jaxpr/psum | solution.py:13
  1068.0 1.0 broadcast_select_fusion.2
  1069.1 102.3 %all-reduce.2.cloned.1.call-done = f32[256,1024]{1,0:T(8,128)} async-done(((f32[256,1024]{1,0:T(8,128)}), f32[256,1024]{1,0:T(8,128)}) %all-reduce.2.cloned.1.call-update) | async-done | bytes 1048592 | tf_op jit(solution)/shard_map/while/body/eval_jaxpr/psum | solution.py:13
  1171.5 0.3 select_select_fusion.2
  1172.0 1.0 broadcast_select_fusion.2
  1173.1 101.8 %all-reduce.2.cloned.1.call-done = f32[256,1024]{1,0:T(8,128)} async-done(((f32[256,1024]{1,0:T(8,128)}), f32[256,1024]{1,0:T(8,128)}) %all-reduce.2.cloned.1.call-update) | async-done | bytes 1048592 | tf_op jit(solution)/shard_map/while/body/eval_jaxpr/psum | solution.py:13
  1275.4 1.0 broadcast_select_fusion.2
  1276.5 102.1 %all-reduce.2.cloned.1.call-done = f32[256,1024]{1,0:T(8,128)} async-done(((f32[256,1024]{1,0:T(8,128)}), f32[256,1024]{1,0:T(8,128)}) %all-reduce.2.cloned.1.call-update) | async-done | bytes 1048592 | tf_op jit(solution)/shard_map/while/body/eval_jaxpr/psum | solution.py:13
  1378.6 0.3 select_select_fusion.2
  1379.2 1.0 broadcast_select_fusion.2
  1380.2 101.8 %all-reduce.2.cloned.1.call-done = f32[256,1024]{1,0:T(8,128)} async-done(((f32[256,1024]{1,0:T(8,128)}), f32[256,1024]{1,0:T(8,128)}) %all-reduce.2.cloned.1.call-update) | async-done | bytes 1048592 | tf_op jit(solution)/shard_map/while/body/eval_jaxpr/psum | solution.py:13
  1482.6 1.0 broadcast_select_fusion.2
  1483.7 101.8 %all-reduce.2.cloned.1.call-done = f32[256,1024]{1,0:T(8,128)} async-done(((f32[256,1024]{1,0:T(8,128)}), f32[256,1024]{1,0:T(8,128)}) %all-reduce.2.cloned.1.call-update) | async-done | bytes 1048592 | tf_op jit(solution)/shard_map/while/body/eval_jaxpr/psum | solution.py:13
  1586.0 1.0 broadcast_select_fusion.2
  1587.1 101.4 %all-reduce.2.cloned.1.call-done = f32[256,1024]{1,0:T(8,128)} async-done(((f32[256,1024]{1,0:T(8,128)}), f32[256,1024]{1,0:T(8,128)}) %all-reduce.2.cloned.1.call-update) | async-done | bytes 1048592 | tf_op jit(solution)/shard_map/while/body/eval_jaxpr/psum | solution.py:13
  1688.5 0.3 select_select_fusion.2
  1689.0 32.8 %psum.18 = f32[1024]{0:T(1024)} all-reduce(f32[1024]{0:T(1024)S(1)} %multiply_reduce_fusion.1), channel_id=1, replica_groups=mesh['chain'=16,'group'=16] {'chain'}, use_global_device_ids=true, to_apply=%region_10.11 | all-reduce | flops 1024 | bytes 8192 | tf_op jit(solution)/shard_map/psum | solution.py:75
  (96 shorter events, 7.1 us)
Async XLA Ops:
  7.2 27.8 %copy-start.1 = (f32[256,256]{1,0:T(8,128)S(1)}, f32[256,256]{1,0:T(8,128)}, u32[]{:S(2)}) copy-start(f32[256,256]{1,0:T(8,128)} %param.14) | copy-start | bytes 786436
  35.0 1653.9 %copy-start.2 = (f32[256]{0:T(256)S(1)}, f32[256]{0:T(256)}, u32[]{:S(2)}) copy-start(f32[256]{0:T(256)} %param.15) | copy-start | bytes 3076
  35.0 98.0 %all-reduce.2.cloned.1.call-start = ((), (), s32[]{:S(2)}) async-start(), calls=%async_computation | async-start | bytes 2097152 | tf_op jit(solution)/shard_map/while/body/eval_jaxpr/psum | solution.py:13
  134.5 102.4 %all-reduce.2.cloned.1.call-start = ((), (), s32[]{:S(2)}) async-start(), calls=%async_computation | async-start | bytes 2097152 | tf_op jit(solution)/shard_map/while/body/eval_jaxpr/psum | solution.py:13
  237.3 103.6 %all-reduce.2.cloned.1.call-start = ((), (), s32[]{:S(2)}) async-start(), calls=%async_computation | async-start | bytes 2097152 | tf_op jit(solution)/shard_map/while/body/eval_jaxpr/psum | solution.py:13
  341.2 103.3 %all-reduce.2.cloned.1.call-start = ((), (), s32[]{:S(2)}) async-start(), calls=%async_computation | async-start | bytes 2097152 | tf_op jit(solution)/shard_map/while/body/eval_jaxpr/psum | solution.py:13
  444.9 103.3 %all-reduce.2.cloned.1.call-start = ((), (), s32[]{:S(2)}) async-start(), calls=%async_computation | async-start | bytes 2097152 | tf_op jit(solution)/shard_map/while/body/eval_jaxpr/psum | solution.py:13
  548.5 103.3 %all-reduce.2.cloned.1.call-start = ((), (), s32[]{:S(2)}) async-start(), calls=%async_computation | async-start | bytes 2097152 | tf_op jit(solution)/shard_map/while/body/eval_jaxpr/psum | solution.py:13
  652.2 103.6 %all-reduce.2.cloned.1.call-start = ((), (), s32[]{:S(2)}) async-start(), calls=%async_computation | async-start | bytes 2097152 | tf_op jit(solution)/shard_map/while/body/eval_jaxpr/psum | solution.py:13
  756.2 103.6 %all-reduce.2.cloned.1.call-start = ((), (), s32[]{:S(2)}) async-start(), calls=%async_computation | async-start | bytes 2097152 | tf_op jit(solution)/shard_map/while/body/eval_jaxpr/psum | solution.py:13
  860.2 103.6 %all-reduce.2.cloned.1.call-start = ((), (), s32[]{:S(2)}) async-start(), calls=%async_computation | async-start | bytes 2097152 | tf_op jit(solution)/shard_map/while/body/eval_jaxpr/psum | solution.py:13
  964.2 103.3 %all-reduce.2.cloned.1.call-start = ((), (), s32[]{:S(2)}) async-start(), calls=%async_computation | async-start | bytes 2097152 | tf_op jit(solution)/shard_map/while/body/eval_jaxpr/psum | solution.py:13
  1067.8 103.6 %all-reduce.2.cloned.1.call-start = ((), (), s32[]{:S(2)}) async-start(), calls=%async_computation | async-start | bytes 2097152 | tf_op jit(solution)/shard_map/while/body/eval_jaxpr/psum | solution.py:13
  1171.8 103.1 %all-reduce.2.cloned.1.call-start = ((), (), s32[]{:S(2)}) async-start(), calls=%async_computation | async-start | bytes 2097152 | tf_op jit(solution)/shard_map/while/body/eval_jaxpr/psum | solution.py:13
  1275.2 103.4 %all-reduce.2.cloned.1.call-start = ((), (), s32[]{:S(2)}) async-start(), calls=%async_computation | async-start | bytes 2097152 | tf_op jit(solution)/shard_map/while/body/eval_jaxpr/psum | solution.py:13
  1379.0 103.1 %all-reduce.2.cloned.1.call-start = ((), (), s32[]{:S(2)}) async-start(), calls=%async_computation | async-start | bytes 2097152 | tf_op jit(solution)/shard_map/while/body/eval_jaxpr/psum | solution.py:13
  1482.4 103.1 %all-reduce.2.cloned.1.call-start = ((), (), s32[]{:S(2)}) async-start(), calls=%async_computation | async-start | bytes 2097152 | tf_op jit(solution)/shard_map/while/body/eval_jaxpr/psum | solution.py:13
  1585.8 102.7 %all-reduce.2.cloned.1.call-start = ((), (), s32[]{:S(2)}) async-start(), calls=%async_computation | async-start | bytes 2097152 | tf_op jit(solution)/shard_map/while/body/eval_jaxpr/psum | solution.py:13
  1688.8 32.9 %copy-start = (f32[256,1024]{1,0:T(8,128)}, f32[256,1024]{1,0:T(8,128)S(1)}, u32[]{:S(2)}) copy-start(f32[256,1024]{1,0:T(8,128)S(1)} %get-tuple-element.176) | copy-start | bytes 3145732
Sparse Core Ops, SparseCore 0:
  39.7 93.2 all-reduce.1
  139.2 97.6 all-reduce.1
  241.9 98.9 all-reduce.1
  345.6 98.9 all-reduce.1
  449.2 98.9 all-reduce.1
  552.9 98.9 all-reduce.1
  656.9 98.9 all-reduce.1
  760.9 98.9 all-reduce.1
  864.9 98.9 all-reduce.1
  968.5 98.9 all-reduce.1
  1072.5 98.9 all-reduce.1
  1176.1 98.6 all-reduce.1
  1279.9 98.6 all-reduce.1
  1383.3 98.6 all-reduce.1
  1486.7 98.6 all-reduce.1
  1590.2 98.2 all-reduce.1
where the time goes:
time: 1740 us; the launch traced here: 1730 us
  waiting for transfers between devices  1630 us (94%)
  blocking collectives  55.9 us (3%)
  other arithmetic  25.6 us (1%)
    psum x16, waiting for transfers between devices, from_root(): return lax.psum(jnp.where(mine, x, jnp.zeros_like(x)), axis)  1630 us
  transfers between devices with their start and end apart: 16, of which 16 were waited for; matrix products, arithmetic and copies ran while one was open for 0% of the time, Pallas kernels for 0%

commit v1 on v0

v1 whole, which is shorter than its diff:
```python
import functools
import math

import jax
import jax.numpy as jnp
from jax import lax
from jax.experimental import pallas as pl
from jax.experimental.pallas import tpu as pltpu
from jax.sharding import PartitionSpec as P

EPS = 1e-06
BF16 = jnp.bfloat16
F32 = jnp.float32
AXES = ("chain", "group")
SIDE = 4
ZS = 8
VMEM = pl.BlockSpec(memory_space=pltpu.VMEM)
SMEM = pl.BlockSpec(memory_space=pltpu.SMEM)
PARAMS = pltpu.CompilerParams(vmem_limit_bytes=56 * 1024 * 1024)


def moves(target):
    pairs = []
    for y in range(SIDE):
        for x in range(SIDE):
            for z in range(ZS):
                for c in range(2):
                    to = target(y, x, z, c)
                    if to is not None:
                        ty, tx, tz, tc = to
                        source = ((y * SIDE + x) * ZS + z) * 2 + c
                        dest = ((ty * SIDE + tx) * ZS + tz) * 2 + tc
                        pairs.append((source, dest))
    return pairs


def send(value, target):
    return lax.ppermute(value, AXES, moves(target))


def swap_core(value):
    return send(value, lambda y, x, z, c: (y, x, z, 1 - c))


def split(a):
    hi = a.astype(BF16)
    return hi, (a - hi.astype(F32)).astype(BF16)


def mul(a, b, dims):
    return lax.dot_general(a, b, (dims, ((), ())), preferred_element_type=F32)


NT = ((1,), (1,))
NN = ((1,), (0,))


def mul3(a, b, dims):
    (ah, al), (bh, bl) = a, b
    return mul(ah, bh, dims) + (mul(ah, bl, dims) + mul(al, bh, dims))


def nt(a, b):
    return mul3(split(a), split(b), NT)


def prepare_kernel(index_ref, f_ref, hi_ref, lo_ref):
    hi, lo = split(f_ref[...])
    hi_ref[0] = hi
    lo_ref[0] = lo


def prepare(factor, index, bs):
    count = index.shape[0]
    spec = pl.BlockSpec((1, bs, bs), lambda i, idx: (i, 0, 0))
    shape = jax.ShapeDtypeStruct((count, bs, bs), BF16)
    return pl.pallas_call(
        prepare_kernel,
        grid_spec=pltpu.PrefetchScalarGridSpec(
            num_scalar_prefetch=1,
            grid=(count,),
            in_specs=[pl.BlockSpec((bs, bs), lambda i, idx: (0, idx[i]))],
            out_specs=[spec, spec],
        ),
        out_shape=[shape, shape],
        compiler_params=PARAMS,
    )(index, factor)


def diagonal_kernel(place, d_ref, p1, p2, p3, r1, r2, r3, s1, s2, s3, out_ref):
    bs = d_ref.shape[0]
    x, c = place[0], place[1]
    first = c == 0
    dc, db, da = (jnp.where(first, r[...], s[...]) for r, s in ((r1, s1), (r2, s2), (r3, s3)))
    fcb, fba, fca = (jnp.where(first, s[...], r[...]) for r, s in ((r1, s1), (r2, s2), (r3, s3)))
    own = d_ref[...]
    dct, dbt, dat = dc.T, db.T, da.T
    sba = -nt(nt(dat, fba), db)
    ab = nt(jnp.concatenate([dbt, sba], 0), fcb)
    both = jnp.concatenate([ab[:bs], ab[bs:] + nt(dat, fca)], 0)
    cc = -nt(both, dc)
    scb, sca = cc[:bs], cc[bs:]
    t1 = nt(jnp.concatenate([dct, scb, sca], 0), p1[...])
    t2 = nt(jnp.concatenate([dbt, sba], 0), p2[...])
    t3 = nt(dat, p3[...])
    rows = jnp.concatenate([t1[:bs], t1[bs : 2 * bs] + t2[:bs], t1[2 * bs :] + t2[bs:] + t3], 0)
    res = -nt(rows, own)
    out_ref[...] = jnp.zeros_like(out_ref)
    out_ref[pl.ds(pl.multiple_of(x * bs, bs), bs), :] = own.T
    for k in (1, 2, 3):

        @pl.when(x >= k)
        def _():
            at = pl.multiple_of(jnp.maximum(x - k, 0) * bs, bs)
            out_ref[pl.ds(at, bs), :] = res[(k - 1) * bs : k * bs]


def diagonal(place, d, prev, near, far):
    bs = d.shape[0]
    return pl.pallas_call(
        diagonal_kernel,
        in_specs=[SMEM] + [VMEM] * 10,
        out_specs=VMEM,
        out_shape=jax.ShapeDtypeStruct((SIDE * bs, bs), F32),
        compiler_params=PARAMS,
    )(place, d, *prev, *near, *far)


def times_factor_kernel(count, init, *refs):
    xs, (hi, lo), rest = refs[:count], refs[count : count + 2], refs[count + 2 :]
    total = rest[0][...] if init else None
    for i in range(count):
        part = mul3(split(xs[i][...]), (hi[i], lo[i]), NT)
        total = part if total is None else total + part
    rest[-1][...] = total


def times_factor(xs, weights, first, init=None):
    n, (m, bs) = len(xs), xs[0].shape
    wspec = pl.BlockSpec((n, bs, bs), lambda i: (first, 0, 0))
    small = pl.BlockSpec((m, bs), lambda i: (0, 0))
    extra = [] if init is None else [init]
    return pl.pallas_call(
        functools.partial(times_factor_kernel, n, init is not None),
        grid=(1,),
        in_specs=[small] * n + [wspec, wspec] + [small] * len(extra),
        out_specs=small,
        out_shape=jax.ShapeDtypeStruct((m, bs), F32),
        compiler_params=PARAMS,
    )(*xs, *weights, *extra)


def times_inverse_kernel(below, place, *refs):
    ts, st = refs[:SIDE], refs[SIDE]
    out = refs[-1]
    bs = st.shape[1]
    x, c = place[0], place[1]
    total = None
    for k in range(SIDE):
        at = pl.multiple_of(jnp.maximum(x - k, 0) * bs, bs)
        part = mul3(split(ts[k][...]), split(st[pl.ds(at, bs), :]), NN)
        total = part if total is None else total + part
    if below:
        qs, ma, mb = refs[SIDE + 1 : 2 * SIDE + 1], refs[2 * SIDE + 1], refs[2 * SIDE + 2]
        full = refs[2 * SIDE + 4]
        interleave(full, ma, mb, c)
        for k in range(SIDE):
            at = pl.multiple_of(lax.rem(x - k + SIDE, SIDE) * bs, bs)
            total = total + mul3(split(qs[k][...]), split(full[pl.ds(at, bs), :]), NN)
        out = refs[2 * SIDE + 3]
    out[...] = -total


def interleave(full, ma, mb, c):
    m = ma.shape[1]
    for z in range(ZS):
        full[pl.ds(pl.multiple_of((2 * z + c) * m, m), m), :] = ma[z]
        full[pl.ds(pl.multiple_of((2 * z + 1 - c) * m, m), m), :] = mb[z]


def times_inverse(place, ts, st, below=None):
    m, bs = ts[0].shape
    args, scratch = [*ts, st], []
    if below is not None:
        qs, ma, mb = below
        args += [*qs, ma, mb]
        scratch = [pltpu.VMEM((SIDE * bs, bs), F32)]
    return pl.pallas_call(
        functools.partial(times_inverse_kernel, below is not None),
        in_specs=[SMEM] + [VMEM] * len(args),
        out_specs=VMEM,
        out_shape=jax.ShapeDtypeStruct((m, bs), F32),
        scratch_shapes=scratch,
        compiler_params=PARAMS,
    )(place, *args)


def panel_kernel(beta, train_ref, cand_ref, scale_ref, hi_ref, lo_ref):
    rows = train_ref[...]
    rows_f = rows.astype(F32)
    row_scale = lax.rsqrt(jnp.sum(rows_f * rows_f, axis=1, keepdims=True) + EPS)
    cross = mul(rows, cand_ref[...], NT)
    hi, lo = split(jnp.exp(beta * cross * row_scale * scale_ref[...]))
    hi_ref[...] = hi
    lo_ref[...] = lo


def make_panel(train, cand, cand_scale, rows):
    total, e = train.shape
    n = cand.shape[0]
    spec = pl.BlockSpec((rows, n), lambda i: (i, 0))
    shape = jax.ShapeDtypeStruct((total, n), BF16)
    return pl.pallas_call(
        functools.partial(panel_kernel, 0.5 * math.sqrt(e)),
        grid=(total // rows,),
        in_specs=[
            pl.BlockSpec((rows, e), lambda i: (i, 0)),
            pl.BlockSpec((n, e), lambda i: (0, 0)),
            pl.BlockSpec((1, n), lambda i: (0, 0)),
        ],
        out_specs=[spec, spec],
        out_shape=[shape, shape],
        compiler_params=PARAMS,
    )(train, cand, cand_scale)


def arrange_kernel(place, *refs):
    z = place[2]
    out = refs[-1]
    for k in range(ZS):
        out[lax.rem(z - k + ZS, ZS)] = refs[k][...]


def z_gather(place, own):
    parts = [own]
    for k in range(1, ZS):
        parts.append(send(own, lambda y, x, z, c: (y, x, (z + k) % ZS, c)))
    mine = pl.pallas_call(
        arrange_kernel,
        in_specs=[SMEM] + [VMEM] * ZS,
        out_specs=VMEM,
        out_shape=jax.ShapeDtypeStruct((ZS,) + own.shape, own.dtype),
        compiler_params=PARAMS,
    )(place, *parts)
    return mine, swap_core(mine)


def apply_kernel(sliced, last, which, place, *refs):
    if sliced:
        ma, mb, refs = refs[0], refs[1], refs[2:]
    else:
        st, refs = refs[0], refs[1:]
    if sliced:
        win, refs = refs[0], refs[1:]
    hi, lo, refs = refs[0], refs[1], refs[2:]
    if last:
        targets, refs = refs[0], refs[1:]
    out, refs = refs[0], refs[1:]
    if last:
        mean, refs = refs[0], refs[1:]
    mh, ml = refs[-2], refs[-1]
    bs = mh.shape[0]
    step = pl.program_id(0)

    @pl.when(step == 0)
    def _():
        if sliced:
            full = refs[0]
            interleave(full, ma, mb, place[1])
            wide = full[...].T
            out[...] = win[...]
        else:
            wide = st[...].T
            out[...] = jnp.zeros_like(out)
        h, l = split(wide)
        mh[...] = h
        ml[...] = l

    at = pl.ds(pl.multiple_of(step * bs, bs), bs)
    out[...] += mul3((mh[:, at], ml[:, at]), (hi[...], lo[...]), NN)
    if last:

        @pl.when(step == pl.num_programs(0) - 1)
        def _():
            mean[...] = jnp.sum(out[...] * targets[...], axis=0, keepdims=True)


def apply(which, place, inverse, panel, win=None, targets=None):
    hi, lo = panel
    n = hi.shape[1]
    sliced, last = win is not None, targets is not None
    bs = inverse[0].shape[-1]
    steps = SIDE
    fixed = lambda shape: pl.BlockSpec(shape, lambda i, w, p: (0,) * len(shape))
    pspec = pl.BlockSpec((bs, n), lambda i, w, p: (w[0] * SIDE + i, 0))
    args = list(inverse)
    specs = [fixed(a.shape) for a in args]
    if sliced:
        args.append(win)
        specs.append(fixed(win.shape))
    args += [hi, lo]
    specs += [pspec, pspec]
    if last:
        args.append(targets)
        specs.append(fixed(targets.shape))
    shapes = [jax.ShapeDtypeStruct((bs, n), F32)]
    if last:
        shapes.append(jax.ShapeDtypeStruct((1, n), F32))
    scratch = [pltpu.VMEM((bs, SIDE * bs), BF16)] * 2
    if sliced:
        scratch = [pltpu.VMEM((SIDE * bs, bs), F32)] + scratch
    return pl.pallas_call(
        functools.partial(apply_kernel, sliced, last),
        grid_spec=pltpu.PrefetchScalarGridSpec(
            num_scalar_prefetch=2,
            grid=(steps,),
            in_specs=specs,
            out_specs=[fixed(s.shape) for s in shapes],
            scratch_shapes=scratch,
        ),
        out_shape=shapes,
        compiler_params=PARAMS,
    )(which, place, *args)


def up_x(k, value):
    return send(value, lambda y, x, z, c: (y, x + k, z, c) if x + k < SIDE else None)


def spread_y(value, rows):
    return [
        send(value, lambda y, x, z, c: (rows[y], (x + k) % SIDE, z, c) if y in rows else None)
        for k in range(SIDE)
    ]


def shards(train_emb, cand_emb, factor, diag_inverse, targets):
    bs = diag_inverse.shape[1]
    n = cand_emb.shape[0]
    p = lax.axis_index("chain")
    group = lax.axis_index("group")
    y, x, z, c = p // SIDE, p % SIDE, group // 2, group % 2
    place = jnp.stack([x, c, z, y]).astype(jnp.int32)

    def block(back):
        return lax.dynamic_slice(factor, (0, jnp.maximum(p - back, 0) * bs), (bs, bs))

    prev = [block(k) for k in (1, 2, 3)]
    even = c == 0
    pay = jnp.where(even, diag_inverse, prev[0])
    pay3 = jnp.where(even, diag_inverse, prev[1])

    def to1(y, x, z, c):
        return (y, x + 1, z, c) if x < 3 and (c == 0 or x >= 1) else None

    def to2(y, x, z, c):
        return (y, x + 2, z, c) if x < 2 and (c == 0 or x == 1) else None

    def to3(y, x, z, c):
        return (y, 3, z, c) if (c == 0 and x == 0) or (c == 1 and x == 2) else None

    near = [send(pay, to1), send(pay, to2), send(pay3, to3)]
    far = [swap_core(v) for v in near]
    index = jnp.stack(
        [jnp.maximum(y - dy, 0) * SIDE + lax.rem(x - dx + SIDE, SIDE) for dy in (1, 2, 3) for dx in range(SIDE)]
    ).astype(jnp.int32)
    weights = prepare(factor, index, bs)
    st = diagonal(place, diag_inverse, prev, near, far)

    m = SIDE * bs // (2 * ZS)
    sl = lax.dynamic_slice(st, (group * m, 0), (m, bs))
    s1 = spread_y(sl, {0: 1, 1: 2, 2: 3})
    t1 = times_factor(s1, weights, 0)
    t1_low = [t1] + [up_x(k, t1) for k in (1, 2, 3)]
    m1 = times_inverse(place, t1_low, st)

    s2 = spread_y(sl, {0: 2, 1: 3})
    s3 = spread_y(sl, {0: 3})
    t2 = times_factor(s2, weights, 1)
    t3 = times_factor(s3, weights, 2)

    m10_2 = spread_y(m1, {1: 2})
    m10_3 = spread_y(m1, {1: 3})
    m1_full = z_gather(place, m1)

    q1 = spread_y(t1, {2: 3})
    t31_low = [t2] + [up_x(k, t2) for k in (1, 2, 3)]
    m31 = times_inverse(place, t31_low, st, (q1, *m1_full))
    m31 = jnp.where(y == 3, m31, jnp.zeros_like(m31))
    ma_full = z_gather(place, m31)

    t20 = times_factor(m10_2, weights, 0, t2)
    t30 = times_factor(m10_3, weights, 1, t3)
    t0 = jnp.where(y == 3, t30, t20)
    q0 = spread_y(t0, {2: 3})
    t0_low = [t0] + [up_x(k, t0) for k in (1, 2, 3)]
    mb = times_inverse(place, t0_low, st, (q0, *m1_full))
    mb = jnp.where(y >= 2, mb, jnp.zeros_like(mb))
    mb_full = z_gather(place, mb)

    cand_f = cand_emb.astype(F32)
    cand_scale = lax.rsqrt(jnp.sum(cand_f * cand_f, axis=1) + EPS).reshape(1, n)
    train = lax.all_gather(train_emb, AXES, axis=0, tiled=True)
    panel = make_panel(train, cand_emb, cand_scale, 2 * bs)

    at = lambda v: jnp.full((1,), v, jnp.int32)
    (w,) = apply(at(y), place, (st,), panel)
    (w,) = apply(at(jnp.maximum(y - 1, 0)), place, m1_full, panel, w)
    (w,) = apply(at(1), place, ma_full, panel, w)
    w, mean = apply(at(0), place, mb_full, panel, w, targets.reshape(bs, 1))
    for axis in ("x", "y"):
        parts = [mean]
        for k in (1, 2, 3):
            if axis == "x":
                parts.append(send(mean, lambda y, x, z, c: (y, (x + k) % SIDE, z, c)))
            else:
                parts.append(send(mean, lambda y, x, z, c: ((y + k) % SIDE, x, z, c)))
        mean = (parts[0] + parts[1]) + (parts[2] + parts[3])
    return w, mean.reshape(n)


def solution(mesh):
    in_specs = (
        P(("chain", "group"), None),
        P("group", None),
        P("chain", None),
        P("chain", None),
        P("chain"),
    )
    out_specs = (P("chain", "group"), P("group"))
    return jax.shard_map(shards, mesh=mesh, in_specs=in_specs, out_specs=out_specs, check_vma=False)
```

time: 1740 us -> 393 us (0.23)
  waiting for transfers between devices: 1630 us -> 9.85 us
  starting transfers between devices: 0.65 us -> 260 us
  Pallas kernels: 0 us -> 87.5 us
  blocking collectives: 55.9 us -> 0 us
  other arithmetic: 25.6 us -> 6.1 us
    psum x16 -> x0, waiting for transfers between devices: 1630 us -> none  [from_root(): return lax.psum(jnp.where(mine, x, jnp.zeros_like(x)), axis)]
    ppermute x0 -> x73, starting transfers between devices: none -> 260 us  [send(): return lax.ppermute(value, AXES, moves(target))]
    pallas_call x0 -> x18, Pallas kernels: none -> 87.5 us  [the longest x4 28 us: apply(): pl.pallas_call(functools.partial(apply_kernel, sliced, last), grid_spec=p...]
    psum x1 -> x0, blocking collectives: 32.8 us -> none  [shards(): post_mean = lax.psum(local_mean, 'chain')]
    all_gather x1 -> x0, blocking collectives: 23.1 us -> none  [shards(): piece = lax.all_gather(train_emb, 'group', axis=0, tiled=True)]
    select_n x32 -> x4, other arithmetic: 23.2 us -> 3.12 us  [the longest x1 2.23 us: shards(): pay3 = jnp.where(even, diag_inverse, prev[1])]
  transfers between devices with their start and end apart: 16 -> 74, of which waited for: 16 -> 4; matrix products, arithmetic and copies ran while one was open for 0% -> 2% of each run, Pallas kernels for 0% -> 21%
where the time goes in v1:
time: 393 us; the launch traced here: 387 us
  starting transfers between devices  260 us (66%)
  Pallas kernels  87.5 us (22%)
  between operations  15.6 us (4%)
  waiting for transfers between devices  9.85 us (3%)
  local copies, waits for them, and re-layouts  7.45 us (2%)
  other arithmetic  6.1 us (2%)
    ppermute x73, starting transfers between devices, send(): return lax.ppermute(value, AXES, moves(target))  260 us
    pallas_call x4, Pallas kernels, apply(): pl.pallas_call(functools.partial(apply_kernel, sliced, last), grid_spec=p...  28 us
    pallas_call x1, Pallas kernels, make_panel(): pl.pallas_call(functools.partial(panel_kernel, 0.5 * math.sqrt(e)), grid=...  17.8 us
    pallas_call x5, Pallas kernels, times_factor(): pl.pallas_call(functools.partial(times_factor_kernel, n, init is not None...  12.8 us
    ppermute x73, waiting for transfers between devices, send(): return lax.ppermute(value, AXES, moves(target))  9.17 us
    pallas_call x1, Pallas kernels, prepare(): pl.pallas_call(prepare_kernel, grid_spec=pltpu.PrefetchScalarGridSpec(num...  8.66 us
    pallas_call x3, Pallas kernels, times_inverse(): pl.pallas_call(functools.partial(times_inverse_kernel, below is not None)...  8.56 us
  transfers between devices with their start and end apart: 74, of which 4 were waited for; matrix products, arithmetic and copies ran while one was open for 2% of the time, Pallas kernels for 21%

profile of v1, /device:TPU:1, one launch (start us, length us, event | category | flops | bytes accessed | tf_op | source)
XLA Modules:
  0.0 386.6 jit_solution(3928524173771225066)
XLA Ops:
  7.9 2.2 broadcast_select_fusion
  12.2 8.8 %collective-permute-start.3 = (f32[256,256]{1,0:T(8,128)S(1)}, f32[256,256]{1,0:T(8,128)S(1)}, u32[]{:S(2)}, u32[]{:S(2)}) collective-permute-start(f32[256,256]{1,0:T(8,128)S(1)} %collective-permute-done.r1), channel_id=1, source_target_pairs={{0,1},{1,0},{2,3},{3,2},{4,5},{5,4},{6,7},{7,6},{8,9},{9,8},{10,11... | collective-permute-start | bytes 786440 | tf_op jit(solution)/shard_map/ppermute | solution.py:38
  21.0 2.4 collective-permute-start.4
  23.5 15.6 %collective-permute-start.5 = (f32[256,256]{1,0:T(8,128)S(1)}, f32[256,256]{1,0:T(8,128)S(1)}, u32[]{:S(2)}, u32[]{:S(2)}) collective-permute-start(f32[256,256]{1,0:T(8,128)S(1)} %collective-permute-done.2.r3), channel_id=1, source_target_pairs={{0,1},{1,0},{2,3},{3,2},{4,5},{5,4},{6,7},{7,6},{8,9},{9,8},{10,11... | collective-permute-start | bytes 786440 | tf_op jit(solution)/shard_map/ppermute | solution.py:38
  39.7 2.4 collective-permute-done.5.s3
  42.9 5.9 %shard_map.68.refs_4_.refs_0_ = f32[1024,256]{1,0:T(8,128)} custom-call(s32[4]{0:T(128)} %pad_add_fusion.place, f32[256,256]{1,0:T(8,128)} %d_ref.1, f32[256,256]{1,0:T(8,128)} %get-tuple-element.19.p1, f32[256,256]{1,0:T(8,128)} %get-tuple-element.15.p2, f32[256,256]{1,0:T(8,128)} %get-tuple-element.20.p3, f32[256,256]{1,0:T(8,128)} %copy-done.6, ...), custom_call_target="tpu_custom_call" | custom-call | tf_op jit(solution)/shard_map/pallas_call | solution.py:120
  51.3 12.8 %collective-permute-start.7 = (f32[64,256]{1,0:T(8,128)S(1)}, f32[64,256]{1,0:T(8,128)S(1)}, u32[]{:S(2)}, u32[]{:S(2)}) collective-permute-start(f32[64,256]{1,0:T(8,128)S(1)} %constant_dynamic-slice_fusion), channel_id=1, source_target_pairs={{0,80},{1,81},{2,82},{3,83},{4,84},{5,85},{6,86},{7,87},{8,88},{9,... | collective-permute-start | bytes 196616 | tf_op jit(solution)/shard_map/ppermute | solution.py:38
  64.1 13.1 %collective-permute-start.8 = (f32[64,256]{1,0:T(8,128)S(1)}, f32[64,256]{1,0:T(8,128)S(1)}, u32[]{:S(2)}, u32[]{:S(2)}) collective-permute-start(f32[64,256]{1,0:T(8,128)S(1)} %constant_dynamic-slice_fusion), channel_id=1, source_target_pairs={{0,96},{1,97},{2,98},{3,99},{4,100},{5,101},{6,102},{7,103},{8,104... | collective-permute-start | bytes 196616 | tf_op jit(solution)/shard_map/ppermute | solution.py:38
  77.2 13.1 %collective-permute-start.9 = (f32[64,256]{1,0:T(8,128)S(1)}, f32[64,256]{1,0:T(8,128)S(1)}, u32[]{:S(2)}, u32[]{:S(2)}) collective-permute-start(f32[64,256]{1,0:T(8,128)S(1)} %constant_dynamic-slice_fusion), channel_id=1, source_target_pairs={{0,112},{1,113},{2,114},{3,115},{4,116},{5,117},{6,118},{7,119},{8... | collective-permute-start | bytes 196616 | tf_op jit(solution)/shard_map/ppermute | solution.py:38
  91.1 8.7 %shard_map.69 = (bf16[12,256,256]{2,1,0:T(8,128)(2,1)}, bf16[12,256,256]{2,1,0:T(8,128)(2,1)}) custom-call(s32[12]{0:T(128)} %stack.71.index_ref, f32[256,4096]{1,0:T(8,128)} %f_ref.1), custom_call_target="tpu_custom_call" | custom-call | tf_op jit(solution)/shard_map/pallas_call | solution.py:77
  100.5 2.6 shard_map.70.refs_0_
  103.0 3.3 collective-permute-start.10
  106.3 4.3 %collective-permute-start.11 = (f32[64,256]{1,0:T(8,128)}, f32[64,256]{1,0:T(8,128)S(1)}, u32[]{:S(2)}, u32[]{:S(2)}) collective-permute-start(f32[64,256]{1,0:T(8,128)} %shard_map.70.refs_0_), channel_id=1, source_target_pairs={{0,32},{1,33},{2,34},{3,35},{4,36},{5,37},{6,38},{7,39},{8,40},{9,... | collective-permute-start | bytes 196616 | tf_op jit(solution)/shard_map/ppermute | solution.py:38
  111.9 4.6 %collective-permute-start.25 = (f32[64,256]{1,0:T(8,128)S(1)}, f32[64,256]{1,0:T(8,128)S(1)}, u32[]{:S(2)}, u32[]{:S(2)}) collective-permute-start(f32[64,256]{1,0:T(8,128)S(1)} %constant_dynamic-slice_fusion), channel_id=1, source_target_pairs={{0,128},{1,129},{2,130},{3,131},{4,132},{5,133},{6,134},{7,135},{8... | collective-permute-start | bytes 196616 | tf_op jit(solution)/shard_map/ppermute | solution.py:38
  119.2 2.5 shard_map.71.refs_0_
  123.1 2.7 collective-permute-start.37
  125.8 3.5 collective-permute-start.38
  129.9 4.0 %collective-permute-start.40 = (f32[64,256]{1,0:T(8,128)}, f32[64,256]{1,0:T(8,128)S(1)}, u32[]{:S(2)}, u32[]{:S(2)}) collective-permute-start(f32[64,256]{1,0:T(8,128)} %shard_map.71.refs_0_), channel_id=1, source_target_pairs={{0,10},{1,11},{2,12},{3,13},{4,14},{5,15},{6,0},{7,1},{8,2},{9,3},... | collective-permute-start | bytes 196616 | tf_op jit(solution)/shard_map/ppermute | solution.py:38
  133.9 3.0 collective-permute-start.41
  137.6 3.9 %collective-permute-start.27 = (f32[64,256]{1,0:T(8,128)S(1)}, f32[64,256]{1,0:T(8,128)S(1)}, u32[]{:S(2)}, u32[]{:S(2)}) collective-permute-start(f32[64,256]{1,0:T(8,128)S(1)} %constant_dynamic-slice_fusion), channel_id=1, source_target_pairs={{0,160},{1,161},{2,162},{3,163},{4,164},{5,165},{6,166},{7,167},{8... | collective-permute-start | bytes 196616 | tf_op jit(solution)/shard_map/ppermute | solution.py:38
  145.9 3.1 collective-permute-start.19
  151.0 2.1 collective-permute-start.43
  160.2 2.6 shard_map.74.refs_6_.refs_0_
  162.8 2.4 collective-permute-start.52
  165.2 3.3 collective-permute-start.53
  169.9 2.6 shard_map.72.refs_6_
  172.5 2.5 shard_map.75
  175.8 2.5 shard_map.73
  186.9 3.0 shard_map.79
  193.6 4.7 %collective-permute-start.61 = (f32[64,256]{1,0:T(8,128)S(1)}, f32[64,256]{1,0:T(8,128)S(1)}, u32[]{:S(2)}, u32[]{:S(2)}) collective-permute-start(f32[64,256]{1,0:T(8,128)S(1)} %broadcast_select_fusion.2.refs_0_), channel_id=1, source_target_pairs={{0,6},{1,7},{2,8},{3,9},{4,10},{5,11},{6,12},{7,13},{8,14},{9,15},... | collective-permute-start | bytes 196616 | tf_op jit(solution)/shard_map/ppermute | solution.py:38
  198.6 4.1 %collective-permute-start.63 = (f32[64,256]{1,0:T(8,128)S(1)}, f32[64,256]{1,0:T(8,128)S(1)}, u32[]{:S(2)}, u32[]{:S(2)}) collective-permute-start(f32[64,256]{1,0:T(8,128)S(1)} %broadcast_select_fusion.2.refs_0_), channel_id=1, source_target_pairs={{0,10},{1,11},{2,12},{3,13},{4,14},{5,15},{6,0},{7,1},{8,2},{9,3},... | collective-permute-start | bytes 196616 | tf_op jit(solution)/shard_map/ppermute | solution.py:38
  202.7 3.0 shard_map.77
  211.3 12.7 %collective-permute-start.47 = (f32[64,256]{1,0:T(8,128)S(1)}, f32[64,256]{1,0:T(8,128)S(1)}, u32[]{:S(2)}, u32[]{:S(2)}) collective-permute-start(f32[64,256]{1,0:T(8,128)S(1)} %broadcast_select_fusion.3.refs_0_), channel_id=1, source_target_pairs={{0,8},{1,9},{2,10},{3,11},{4,12},{5,13},{6,14},{7,15},{8,0},{9,1},... | collective-permute-start | bytes 196616 | tf_op jit(solution)/shard_map/ppermute | solution.py:38
  224.9 3.1 collective-permute-start.49
  230.9 4.6 %collective-permute-start.66 = (f32[8,64,256]{2,1,0:T(8,128)}, f32[8,64,256]{2,1,0:T(8,128)S(1)}, u32[]{:S(2)}, u32[]{:S(2)}) collective-permute-start(f32[8,64,256]{2,1,0:T(8,128)} %shard_map.80.refs_0_), channel_id=1, source_target_pairs={{0,1},{1,0},{2,3},{3,2},{4,5},{5,4},{6,7},{7,6},{8,9},{9,8},{10,11... | collective-permute-start | bytes 1572872 | tf_op jit(solution)/shard_map/ppermute | solution.py:38
  243.3 17.8 %shard_map.81 = (bf16[4096,1024]{1,0:T(8,128)(2,1)}, bf16[4096,1024]{1,0:T(8,128)(2,1)}) custom-call(bf16[4096,1024]{1,0:T(8,128)(2,1)} %all-gather.2.cloned.1.call-done.train_ref, bf16[1024,1024]{1,0:T(8,128)(2,1)} %cand_ref.1, f32[1,1024]{1,0:T(1,128)} %bitcast.20), custom_call_target="tpu_custom_call" | custom-call | tf_op jit(solution)/shard_map/pallas_call | solution.py:213
  261.0 6.7 %shard_map.82.refs_2_ = f32[256,1024]{1,0:T(8,128)} custom-call(s32[1]{0:T(128)} %bitcast.3.which, s32[4]{0:T(128)} %pad_add_fusion.place, f32[1024,256]{1,0:T(8,128)} %shard_map.68.refs_4_.refs_0_, bf16[4096,1024]{1,0:T(8,128)(2,1)} %get-tuple-element.10.refs_1_.refs_3_, bf16[4096,1024]{1,0:T(8,128)(2,1)} %get-tuple-element.11.refs_2_.refs_4_), custom_call_target="tpu_custom_call" | custom-call | tf_op jit(solution)/shard_map/pallas_call | solution.py:312
  267.7 7.1 %shard_map.83.refs_2_ = f32[256,1024]{1,0:T(8,128)} custom-call(s32[1]{0:T(128)} %bitcast.16.which, s32[4]{0:T(128)} %pad_add_fusion.place, f32[8,64,256]{2,1,0:T(8,128)} %shard_map.76.refs_9_.refs_0_, f32[8,64,256]{2,1,0:T(8,128)} %copy-done.1, f32[256,1024]{1,0:T(8,128)} %shard_map.82.refs_2_, bf16[4096,1024]{1,0:T(8,128)(2,1)} %get-tuple-element.10.refs_1_.refs_3_, ...), custom_call_target="tpu_custom_call" | custom-call | tf_op jit(solution)/shard_map/pallas_call | solution.py:312
  275.6 7.1 %shard_map.84.refs_2_ = f32[256,1024]{1,0:T(8,128)} custom-call(s32[1]{0:T(128)} %constant.89.clone.1.which, s32[4]{0:T(128)} %pad_add_fusion.place, f32[8,64,256]{2,1,0:T(8,128)} %shard_map.80.refs_0_, f32[8,64,256]{2,1,0:T(8,128)} %copy-done.2, f32[256,1024]{1,0:T(8,128)} %shard_map.83.refs_2_, bf16[4096,1024]{1,0:T(8,128)(2,1)} %get-tuple-element.10.refs_1_.refs_3_, ...), custom_call_target="tpu_custom_call" | custom-call | tf_op jit(solution)/shard_map/pallas_call | solution.py:312
  283.5 7.2 %shard_map.85 = (f32[256,1024]{1,0:T(8,128)}, f32[1,1024]{1,0:T(1,128)}) custom-call(s32[1]{0:T(128)} %constant.73.clone.1.which, s32[4]{0:T(128)} %pad_add_fusion.place, f32[8,64,256]{2,1,0:T(8,128)} %shard_map.78.refs_0_, f32[8,64,256]{2,1,0:T(8,128)} %copy-done.3, f32[256,1024]{1,0:T(8,128)} %shard_map.84.refs_2_, ...), custom_call_target="tpu_custom_call" | custom-call | tf_op jit(solution)/shard_map/pallas_call | solution.py:312
  290.7 23.0 %collective-permute-start.67 = (f32[1,1024]{1,0:T(1,128)}, f32[1,1024]{1,0:T(1,128)S(1)}, u32[]{:S(2)}, u32[]{:S(2)}) collective-permute-start(f32[1,1024]{1,0:T(1,128)} %get-tuple-element.13), channel_id=1, source_target_pairs={{0,16},{1,17},{2,18},{3,19},{4,20},{5,21},{6,22},{7,23},{8,24},{9,... | collective-permute-start | bytes 12296 | tf_op jit(solution)/shard_map/ppermute | solution.py:38
  313.7 11.8 %collective-permute-start.68 = (f32[1,1024]{1,0:T(1,128)}, f32[1,1024]{1,0:T(1,128)S(1)}, u32[]{:S(2)}, u32[]{:S(2)}) collective-permute-start(f32[1,1024]{1,0:T(1,128)} %get-tuple-element.13), channel_id=1, source_target_pairs={{0,32},{1,33},{2,34},{3,35},{4,36},{5,37},{6,38},{7,39},{8,40},{9,... | collective-permute-start | bytes 12296 | tf_op jit(solution)/shard_map/ppermute | solution.py:38
  325.5 11.8 %collective-permute-start.69 = (f32[1,1024]{1,0:T(1,128)}, f32[1,1024]{1,0:T(1,128)S(1)}, u32[]{:S(2)}, u32[]{:S(2)}) collective-permute-start(f32[1,1024]{1,0:T(1,128)} %get-tuple-element.13), channel_id=1, source_target_pairs={{0,48},{1,49},{2,50},{3,51},{4,52},{5,53},{6,54},{7,55},{8,56},{9,... | collective-permute-start | bytes 12296 | tf_op jit(solution)/shard_map/ppermute | solution.py:38
  337.4 2.6 collective-permute-done.69
  340.6 12.3 %collective-permute-start.70 = (f32[1,1024]{1,0:T(1,128)S(1)}, f32[1,1024]{1,0:T(1,128)S(1)}, u32[]{:S(2)}, u32[]{:S(2)}) collective-permute-start(f32[1,1024]{1,0:T(1,128)S(1)} %add_add_fusion.1), channel_id=1, source_target_pairs={{0,64},{1,65},{2,66},{3,67},{4,68},{5,69},{6,70},{7,71},{8,72},{9,... | collective-permute-start | bytes 12296 | tf_op jit(solution)/shard_map/ppermute | solution.py:38
  352.9 11.8 %collective-permute-start.71 = (f32[1,1024]{1,0:T(1,128)S(1)}, f32[1,1024]{1,0:T(1,128)S(1)}, u32[]{:S(2)}, u32[]{:S(2)}) collective-permute-start(f32[1,1024]{1,0:T(1,128)S(1)} %add_add_fusion.1), channel_id=1, source_target_pairs={{0,128},{1,129},{2,130},{3,131},{4,132},{5,133},{6,134},{7,135},{8... | collective-permute-start | bytes 12296 | tf_op jit(solution)/shard_map/ppermute | solution.py:38
  364.8 11.8 %collective-permute-start.72 = (f32[1,1024]{1,0:T(1,128)S(1)}, f32[1,1024]{1,0:T(1,128)S(1)}, u32[]{:S(2)}, u32[]{:S(2)}) collective-permute-start(f32[1,1024]{1,0:T(1,128)S(1)} %add_add_fusion.1), channel_id=1, source_target_pairs={{0,192},{1,193},{2,194},{3,195},{4,196},{5,197},{6,198},{7,199},{8... | collective-permute-start | bytes 12296 | tf_op jit(solution)/shard_map/ppermute | solution.py:38
  376.6 2.4 collective-permute-done.72
  (277 shorter events, 61.8 us)
Async XLA Ops:
  7.2 236.1 %all-gather.2.cloned.1.call-start = ((), (), s32[]{:S(2)}) async-start(), calls=%async_computation | async-start | bytes 8421376 | tf_op jit(solution)/shard_map/all_gather | solution.py:403
  10.8 10.2 %collective-permute-start.1 = (f32[256,256]{1,0:T(8,128)S(1)}, f32[256,256]{1,0:T(8,128)S(1)}, u32[]{:S(2)}, u32[]{:S(2)}) collective-permute-start(f32[256,256]{1,0:T(8,128)S(1)} %get-tuple-element.18), channel_id=1, source_target_pairs={{0,32},{2,34},{4,36},{6,38},{8,40},{10,42},{12,44},{14,46},{16,48}... | collective-permute-start | bytes 786440 | tf_op jit(solution)/shard_map/ppermute | solution.py:38
  11.5 11.9 %collective-permute-start.2 = (f32[256,256]{1,0:T(8,128)S(1)}, f32[256,256]{1,0:T(8,128)S(1)}, u32[]{:S(2)}, u32[]{:S(2)}) collective-permute-start(f32[256,256]{1,0:T(8,128)S(1)} %get-tuple-element.14), channel_id=1, source_target_pairs={{0,48},{2,50},{4,52},{6,54},{8,56},{10,58},{12,60},{14,62},{33,49}... | collective-permute-start | bytes 786440 | tf_op jit(solution)/shard_map/ppermute | solution.py:38
  12.2 27.5 %collective-permute-start.3 = (f32[256,256]{1,0:T(8,128)S(1)}, f32[256,256]{1,0:T(8,128)S(1)}, u32[]{:S(2)}, u32[]{:S(2)}) collective-permute-start(f32[256,256]{1,0:T(8,128)S(1)} %collective-permute-done.r1), channel_id=1, source_target_pairs={{0,1},{1,0},{2,3},{3,2},{4,5},{5,4},{6,7},{7,6},{8,9},{9,8},{10,11... | collective-permute-start | bytes 786440 | tf_op jit(solution)/shard_map/ppermute | solution.py:38
  21.0 18.7 %collective-permute-start.4 = (f32[256,256]{1,0:T(8,128)S(1)}, f32[256,256]{1,0:T(8,128)S(1)}, u32[]{:S(2)}, u32[]{:S(2)}) collective-permute-start(f32[256,256]{1,0:T(8,128)S(1)} %collective-permute-done.1.r2), channel_id=1, source_target_pairs={{0,1},{1,0},{2,3},{3,2},{4,5},{5,4},{6,7},{7,6},{8,9},{9,8},{10,11... | collective-permute-start | bytes 786440 | tf_op jit(solution)/shard_map/ppermute | solution.py:38
  23.5 18.7 %collective-permute-start.5 = (f32[256,256]{1,0:T(8,128)S(1)}, f32[256,256]{1,0:T(8,128)S(1)}, u32[]{:S(2)}, u32[]{:S(2)}) collective-permute-start(f32[256,256]{1,0:T(8,128)S(1)} %collective-permute-done.2.r3), channel_id=1, source_target_pairs={{0,1},{1,0},{2,3},{3,2},{4,5},{5,4},{6,7},{7,6},{8,9},{9,8},{10,11... | collective-permute-start | bytes 786440 | tf_op jit(solution)/shard_map/ppermute | solution.py:38
  49.6 50.1 %collective-permute-start.6 = (f32[64,256]{1,0:T(8,128)S(1)}, f32[64,256]{1,0:T(8,128)S(1)}, u32[]{:S(2)}, u32[]{:S(2)}) collective-permute-start(f32[64,256]{1,0:T(8,128)S(1)} %constant_dynamic-slice_fusion), channel_id=1, source_target_pairs={{0,64},{1,65},{2,66},{3,67},{4,68},{5,69},{6,70},{7,71},{8,72},{9,... | collective-permute-start | bytes 196616 | tf_op jit(solution)/shard_map/ppermute | solution.py:38
  51.3 48.5 %collective-permute-start.7 = (f32[64,256]{1,0:T(8,128)S(1)}, f32[64,256]{1,0:T(8,128)S(1)}, u32[]{:S(2)}, u32[]{:S(2)}) collective-permute-start(f32[64,256]{1,0:T(8,128)S(1)} %constant_dynamic-slice_fusion), channel_id=1, source_target_pairs={{0,80},{1,81},{2,82},{3,83},{4,84},{5,85},{6,86},{7,87},{8,88},{9,... | collective-permute-start | bytes 196616 | tf_op jit(solution)/shard_map/ppermute | solution.py:38
  64.1 35.7 %collective-permute-start.8 = (f32[64,256]{1,0:T(8,128)S(1)}, f32[64,256]{1,0:T(8,128)S(1)}, u32[]{:S(2)}, u32[]{:S(2)}) collective-permute-start(f32[64,256]{1,0:T(8,128)S(1)} %constant_dynamic-slice_fusion), channel_id=1, source_target_pairs={{0,96},{1,97},{2,98},{3,99},{4,100},{5,101},{6,102},{7,103},{8,104... | collective-permute-start | bytes 196616 | tf_op jit(solution)/shard_map/ppermute | solution.py:38
  77.2 22.6 %collective-permute-start.9 = (f32[64,256]{1,0:T(8,128)S(1)}, f32[64,256]{1,0:T(8,128)S(1)}, u32[]{:S(2)}, u32[]{:S(2)}) collective-permute-start(f32[64,256]{1,0:T(8,128)S(1)} %constant_dynamic-slice_fusion), channel_id=1, source_target_pairs={{0,112},{1,113},{2,114},{3,115},{4,116},{5,117},{6,118},{7,119},{8... | collective-permute-start | bytes 196616 | tf_op jit(solution)/shard_map/ppermute | solution.py:38
  103.0 14.8 %collective-permute-start.10 = (f32[64,256]{1,0:T(8,128)}, f32[64,256]{1,0:T(8,128)S(1)}, u32[]{:S(2)}, u32[]{:S(2)}) collective-permute-start(f32[64,256]{1,0:T(8,128)} %shard_map.70.refs_0_), channel_id=1, source_target_pairs={{0,16},{1,17},{2,18},{3,19},{4,20},{5,21},{6,22},{7,23},{8,24},{9,... | collective-permute-start | bytes 196616 | tf_op jit(solution)/shard_map/ppermute | solution.py:38
  106.3 11.6 %collective-permute-start.11 = (f32[64,256]{1,0:T(8,128)}, f32[64,256]{1,0:T(8,128)S(1)}, u32[]{:S(2)}, u32[]{:S(2)}) collective-permute-start(f32[64,256]{1,0:T(8,128)} %shard_map.70.refs_0_), channel_id=1, source_target_pairs={{0,32},{1,33},{2,34},{3,35},{4,36},{5,37},{6,38},{7,39},{8,40},{9,... | collective-permute-start | bytes 196616 | tf_op jit(solution)/shard_map/ppermute | solution.py:38
  111.9 17.4 %collective-permute-start.25 = (f32[64,256]{1,0:T(8,128)S(1)}, f32[64,256]{1,0:T(8,128)S(1)}, u32[]{:S(2)}, u32[]{:S(2)}) collective-permute-start(f32[64,256]{1,0:T(8,128)S(1)} %constant_dynamic-slice_fusion), channel_id=1, source_target_pairs={{0,128},{1,129},{2,130},{3,131},{4,132},{5,133},{6,134},{7,135},{8... | collective-permute-start | bytes 196616 | tf_op jit(solution)/shard_map/ppermute | solution.py:38
  116.6 13.4 %collective-permute-start.26 = (f32[64,256]{1,0:T(8,128)S(1)}, f32[64,256]{1,0:T(8,128)S(1)}, u32[]{:S(2)}, u32[]{:S(2)}) collective-permute-start(f32[64,256]{1,0:T(8,128)S(1)} %constant_dynamic-slice_fusion), channel_id=1, source_target_pairs={{0,144},{1,145},{2,146},{3,147},{4,148},{5,149},{6,150},{7,151},{8... | collective-permute-start | bytes 196616 | tf_op jit(solution)/shard_map/ppermute | solution.py:38
  121.7 12.3 %collective-permute-start.36 = (f32[64,256]{1,0:T(8,128)}, f32[64,256]{1,0:T(8,128)S(1)}, u32[]{:S(2)}, u32[]{:S(2)}) collective-permute-start(f32[64,256]{1,0:T(8,128)} %shard_map.71.refs_0_), channel_id=1, source_target_pairs={{0,2},{1,3},{2,4},{3,5},{4,6},{5,7},{6,8},{7,9},{8,10},{9,11},{10,... | collective-permute-start | bytes 196616 | tf_op jit(solution)/shard_map/ppermute | solution.py:38
  123.1 13.8 %collective-permute-start.37 = (f32[64,256]{1,0:T(8,128)}, f32[64,256]{1,0:T(8,128)S(1)}, u32[]{:S(2)}, u32[]{:S(2)}) collective-permute-start(f32[64,256]{1,0:T(8,128)} %shard_map.71.refs_0_), channel_id=1, source_target_pairs={{0,4},{1,5},{2,6},{3,7},{4,8},{5,9},{6,10},{7,11},{8,12},{9,13},{1... | collective-permute-start | bytes 196616 | tf_op jit(solution)/shard_map/ppermute | solution.py:38
  125.8 11.8 %collective-permute-start.38 = (f32[64,256]{1,0:T(8,128)}, f32[64,256]{1,0:T(8,128)S(1)}, u32[]{:S(2)}, u32[]{:S(2)}) collective-permute-start(f32[64,256]{1,0:T(8,128)} %shard_map.71.refs_0_), channel_id=1, source_target_pairs={{0,6},{1,7},{2,8},{3,9},{4,10},{5,11},{6,12},{7,13},{8,14},{9,15},... | collective-permute-start | bytes 196616 | tf_op jit(solution)/shard_map/ppermute | solution.py:38
  129.3 12.2 %collective-permute-start.39 = (f32[64,256]{1,0:T(8,128)}, f32[64,256]{1,0:T(8,128)S(1)}, u32[]{:S(2)}, u32[]{:S(2)}) collective-permute-start(f32[64,256]{1,0:T(8,128)} %shard_map.71.refs_0_), channel_id=1, source_target_pairs={{0,8},{1,9},{2,10},{3,11},{4,12},{5,13},{6,14},{7,15},{8,0},{9,1},... | collective-permute-start | bytes 196616 | tf_op jit(solution)/shard_map/ppermute | solution.py:38
  129.9 13.3 %collective-permute-start.40 = (f32[64,256]{1,0:T(8,128)}, f32[64,256]{1,0:T(8,128)S(1)}, u32[]{:S(2)}, u32[]{:S(2)}) collective-permute-start(f32[64,256]{1,0:T(8,128)} %shard_map.71.refs_0_), channel_id=1, source_target_pairs={{0,10},{1,11},{2,12},{3,13},{4,14},{5,15},{6,0},{7,1},{8,2},{9,3},... | collective-permute-start | bytes 196616 | tf_op jit(solution)/shard_map/ppermute | solution.py:38
  133.9 10.7 %collective-permute-start.41 = (f32[64,256]{1,0:T(8,128)}, f32[64,256]{1,0:T(8,128)S(1)}, u32[]{:S(2)}, u32[]{:S(2)}) collective-permute-start(f32[64,256]{1,0:T(8,128)} %shard_map.71.refs_0_), channel_id=1, source_target_pairs={{0,12},{1,13},{2,14},{3,15},{4,0},{5,1},{6,2},{7,3},{8,4},{9,5},{1... | collective-permute-start | bytes 196616 | tf_op jit(solution)/shard_map/ppermute | solution.py:38
  137.6 13.4 %collective-permute-start.27 = (f32[64,256]{1,0:T(8,128)S(1)}, f32[64,256]{1,0:T(8,128)S(1)}, u32[]{:S(2)}, u32[]{:S(2)}) collective-permute-start(f32[64,256]{1,0:T(8,128)S(1)} %constant_dynamic-slice_fusion), channel_id=1, source_target_pairs={{0,160},{1,161},{2,162},{3,163},{4,164},{5,165},{6,166},{7,167},{8... | collective-permute-start | bytes 196616 | tf_op jit(solution)/shard_map/ppermute | solution.py:38
  141.5 11.5 %collective-permute-start.28 = (f32[64,256]{1,0:T(8,128)S(1)}, f32[64,256]{1,0:T(8,128)S(1)}, u32[]{:S(2)}, u32[]{:S(2)}) collective-permute-start(f32[64,256]{1,0:T(8,128)S(1)} %constant_dynamic-slice_fusion), channel_id=1, source_target_pairs={{0,176},{1,177},{2,178},{3,179},{4,180},{5,181},{6,182},{7,183},{8... | collective-permute-start | bytes 196616 | tf_op jit(solution)/shard_map/ppermute | solution.py:38
  143.3 11.3 %collective-permute-start.17 = (f32[64,256]{1,0:T(8,128)S(1)}, f32[64,256]{1,0:T(8,128)S(1)}, u32[]{:S(2)}, u32[]{:S(2)}) collective-permute-start(f32[64,256]{1,0:T(8,128)S(1)} %constant_dynamic-slice_fusion), channel_id=1, source_target_pairs={{0,192},{1,193},{2,194},{3,195},{4,196},{5,197},{6,198},{7,199},{8... | collective-permute-start | bytes 196616 | tf_op jit(solution)/shard_map/ppermute | solution.py:38
  144.6 10.7 %collective-permute-start.18 = (f32[64,256]{1,0:T(8,128)S(1)}, f32[64,256]{1,0:T(8,128)S(1)}, u32[]{:S(2)}, u32[]{:S(2)}) collective-permute-start(f32[64,256]{1,0:T(8,128)S(1)} %constant_dynamic-slice_fusion), channel_id=1, source_target_pairs={{0,208},{1,209},{2,210},{3,211},{4,212},{5,213},{6,214},{7,215},{8... | collective-permute-start | bytes 196616 | tf_op jit(solution)/shard_map/ppermute | solution.py:38
  151.0 35.1 %collective-permute-start.43 = (f32[8,64,256]{2,1,0:T(8,128)}, f32[8,64,256]{2,1,0:T(8,128)S(1)}, u32[]{:S(2)}, u32[]{:S(2)}) collective-permute-start(f32[8,64,256]{2,1,0:T(8,128)} %shard_map.76.refs_9_.refs_0_), channel_id=1, source_target_pairs={{0,1},{1,0},{2,3},{3,2},{4,5},{5,4},{6,7},{7,6},{8,9},{9,8},{10,11... | collective-permute-start | bytes 1572872 | tf_op jit(solution)/shard_map/ppermute | solution.py:38
  159.5 15.6 %collective-permute-start.16 = (f32[64,256]{1,0:T(8,128)}, f32[64,256]{1,0:T(8,128)S(1)}, u32[]{:S(2)}, u32[]{:S(2)}) collective-permute-start(f32[64,256]{1,0:T(8,128)} %shard_map.71.refs_0_), channel_id=1, source_target_pairs={{64,240},{65,241},{66,242},{67,243},{68,244},{69,245},{70,246},{71... | collective-permute-start | bytes 196616 | tf_op jit(solution)/shard_map/ppermute | solution.py:38
  162.8 15.5 %collective-permute-start.52 = (f32[64,256]{1,0:T(8,128)}, f32[64,256]{1,0:T(8,128)S(1)}, u32[]{:S(2)}, u32[]{:S(2)}) collective-permute-start(f32[64,256]{1,0:T(8,128)} %shard_map.74.refs_6_.refs_0_), channel_id=1, source_target_pairs={{0,16},{1,17},{2,18},{3,19},{4,20},{5,21},{6,22},{7,23},{8,24},{9,... | collective-permute-start | bytes 196616 | tf_op jit(solution)/shard_map/ppermute | solution.py:38
  165.2 13.9 %collective-permute-start.53 = (f32[64,256]{1,0:T(8,128)}, f32[64,256]{1,0:T(8,128)S(1)}, u32[]{:S(2)}, u32[]{:S(2)}) collective-permute-start(f32[64,256]{1,0:T(8,128)} %shard_map.74.refs_6_.refs_0_), channel_id=1, source_target_pairs={{0,32},{1,33},{2,34},{3,35},{4,36},{5,37},{6,38},{7,39},{8,40},{9,... | collective-permute-start | bytes 196616 | tf_op jit(solution)/shard_map/ppermute | solution.py:38
  168.5 11.3 %collective-permute-start.54 = (f32[64,256]{1,0:T(8,128)}, f32[64,256]{1,0:T(8,128)S(1)}, u32[]{:S(2)}, u32[]{:S(2)}) collective-permute-start(f32[64,256]{1,0:T(8,128)} %shard_map.74.refs_6_.refs_0_), channel_id=1, source_target_pairs={{0,48},{1,49},{2,50},{3,51},{4,52},{5,53},{6,54},{7,55},{8,56},{9,... | collective-permute-start | bytes 196616 | tf_op jit(solution)/shard_map/ppermute | solution.py:38
  191.3 14.4 %collective-permute-start.59 = (f32[64,256]{1,0:T(8,128)S(1)}, f32[64,256]{1,0:T(8,128)S(1)}, u32[]{:S(2)}, u32[]{:S(2)}) collective-permute-start(f32[64,256]{1,0:T(8,128)S(1)} %broadcast_select_fusion.2.refs_0_), channel_id=1, source_target_pairs={{0,2},{1,3},{2,4},{3,5},{4,6},{5,7},{6,8},{7,9},{8,10},{9,11},{10,... | collective-permute-start | bytes 196616 | tf_op jit(solution)/shard_map/ppermute | solution.py:38
  193.1 13.9 %collective-permute-start.60 = (f32[64,256]{1,0:T(8,128)S(1)}, f32[64,256]{1,0:T(8,128)S(1)}, u32[]{:S(2)}, u32[]{:S(2)}) collective-permute-start(f32[64,256]{1,0:T(8,128)S(1)} %broadcast_select_fusion.2.refs_0_), channel_id=1, source_target_pairs={{0,4},{1,5},{2,6},{3,7},{4,8},{5,9},{6,10},{7,11},{8,12},{9,13},{1... | collective-permute-start | bytes 196616 | tf_op jit(solution)/shard_map/ppermute | solution.py:38
  193.6 13.9 %collective-permute-start.61 = (f32[64,256]{1,0:T(8,128)S(1)}, f32[64,256]{1,0:T(8,128)S(1)}, u32[]{:S(2)}, u32[]{:S(2)}) collective-permute-start(f32[64,256]{1,0:T(8,128)S(1)} %broadcast_select_fusion.2.refs_0_), channel_id=1, source_target_pairs={{0,6},{1,7},{2,8},{3,9},{4,10},{5,11},{6,12},{7,13},{8,14},{9,15},... | collective-permute-start | bytes 196616 | tf_op jit(solution)/shard_map/ppermute | solution.py:38
  198.6 11.1 %collective-permute-start.63 = (f32[64,256]{1,0:T(8,128)S(1)}, f32[64,256]{1,0:T(8,128)S(1)}, u32[]{:S(2)}, u32[]{:S(2)}) collective-permute-start(f32[64,256]{1,0:T(8,128)S(1)} %broadcast_select_fusion.2.refs_0_), channel_id=1, source_target_pairs={{0,10},{1,11},{2,12},{3,13},{4,14},{5,15},{6,0},{7,1},{8,2},{9,3},... | collective-permute-start | bytes 196616 | tf_op jit(solution)/shard_map/ppermute | solution.py:38
  207.0 17.0 %collective-permute-start.65 = (f32[64,256]{1,0:T(8,128)S(1)}, f32[64,256]{1,0:T(8,128)S(1)}, u32[]{:S(2)}, u32[]{:S(2)}) collective-permute-start(f32[64,256]{1,0:T(8,128)S(1)} %broadcast_select_fusion.2.refs_0_), channel_id=1, source_target_pairs={{0,14},{1,15},{2,0},{3,1},{4,2},{5,3},{6,4},{7,5},{8,6},{9,7},{10,... | collective-permute-start | bytes 196616 | tf_op jit(solution)/shard_map/ppermute | solution.py:38
  207.6 17.3 %collective-permute-start.44 = (f32[64,256]{1,0:T(8,128)S(1)}, f32[64,256]{1,0:T(8,128)S(1)}, u32[]{:S(2)}, u32[]{:S(2)}) collective-permute-start(f32[64,256]{1,0:T(8,128)S(1)} %broadcast_select_fusion.3.refs_0_), channel_id=1, source_target_pairs={{0,2},{1,3},{2,4},{3,5},{4,6},{5,7},{6,8},{7,9},{8,10},{9,11},{10,... | collective-permute-start | bytes 196616 | tf_op jit(solution)/shard_map/ppermute | solution.py:38
  208.5 19.5 %collective-permute-start.45 = (f32[64,256]{1,0:T(8,128)S(1)}, f32[64,256]{1,0:T(8,128)S(1)}, u32[]{:S(2)}, u32[]{:S(2)}) collective-permute-start(f32[64,256]{1,0:T(8,128)S(1)} %broadcast_select_fusion.3.refs_0_), channel_id=1, source_target_pairs={{0,4},{1,5},{2,6},{3,7},{4,8},{5,9},{6,10},{7,11},{8,12},{9,13},{1... | collective-permute-start | bytes 196616 | tf_op jit(solution)/shard_map/ppermute | solution.py:38
  209.7 21.2 %collective-permute-start.46 = (f32[64,256]{1,0:T(8,128)S(1)}, f32[64,256]{1,0:T(8,128)S(1)}, u32[]{:S(2)}, u32[]{:S(2)}) collective-permute-start(f32[64,256]{1,0:T(8,128)S(1)} %broadcast_select_fusion.3.refs_0_), channel_id=1, source_target_pairs={{0,6},{1,7},{2,8},{3,9},{4,10},{5,11},{6,12},{7,13},{8,14},{9,15},... | collective-permute-start | bytes 196616 | tf_op jit(solution)/shard_map/ppermute | solution.py:38
  211.3 24.2 %collective-permute-start.47 = (f32[64,256]{1,0:T(8,128)S(1)}, f32[64,256]{1,0:T(8,128)S(1)}, u32[]{:S(2)}, u32[]{:S(2)}) collective-permute-start(f32[64,256]{1,0:T(8,128)S(1)} %broadcast_select_fusion.3.refs_0_), channel_id=1, source_target_pairs={{0,8},{1,9},{2,10},{3,11},{4,12},{5,13},{6,14},{7,15},{8,0},{9,1},... | collective-permute-start | bytes 196616 | tf_op jit(solution)/shard_map/ppermute | solution.py:38
  224.0 11.5 %collective-permute-start.48 = (f32[64,256]{1,0:T(8,128)S(1)}, f32[64,256]{1,0:T(8,128)S(1)}, u32[]{:S(2)}, u32[]{:S(2)}) collective-permute-start(f32[64,256]{1,0:T(8,128)S(1)} %broadcast_select_fusion.3.refs_0_), channel_id=1, source_target_pairs={{0,10},{1,11},{2,12},{3,13},{4,14},{5,15},{6,0},{7,1},{8,2},{9,3},... | collective-permute-start | bytes 196616 | tf_op jit(solution)/shard_map/ppermute | solution.py:38
  224.9 10.6 %collective-permute-start.49 = (f32[64,256]{1,0:T(8,128)S(1)}, f32[64,256]{1,0:T(8,128)S(1)}, u32[]{:S(2)}, u32[]{:S(2)}) collective-permute-start(f32[64,256]{1,0:T(8,128)S(1)} %broadcast_select_fusion.3.refs_0_), channel_id=1, source_target_pairs={{0,12},{1,13},{2,14},{3,15},{4,0},{5,1},{6,2},{7,3},{8,4},{9,5},{1... | collective-permute-start | bytes 196616 | tf_op jit(solution)/shard_map/ppermute | solution.py:38
  230.9 43.9 %collective-permute-start.66 = (f32[8,64,256]{2,1,0:T(8,128)}, f32[8,64,256]{2,1,0:T(8,128)S(1)}, u32[]{:S(2)}, u32[]{:S(2)}) collective-permute-start(f32[8,64,256]{2,1,0:T(8,128)} %shard_map.80.refs_0_), channel_id=1, source_target_pairs={{0,1},{1,0},{2,3},{3,2},{4,5},{5,4},{6,7},{7,6},{8,9},{9,8},{10,11... | collective-permute-start | bytes 1572872 | tf_op jit(solution)/shard_map/ppermute | solution.py:38
  239.8 42.9 %collective-permute-start.51 = (f32[8,64,256]{2,1,0:T(8,128)}, f32[8,64,256]{2,1,0:T(8,128)S(1)}, u32[]{:S(2)}, u32[]{:S(2)}) collective-permute-start(f32[8,64,256]{2,1,0:T(8,128)} %shard_map.78.refs_0_), channel_id=1, source_target_pairs={{0,1},{1,0},{2,3},{3,2},{4,5},{5,4},{6,7},{7,6},{8,9},{9,8},{10,11... | collective-permute-start | bytes 1572872 | tf_op jit(solution)/shard_map/ppermute | solution.py:38
  290.7 46.7 %collective-permute-start.67 = (f32[1,1024]{1,0:T(1,128)}, f32[1,1024]{1,0:T(1,128)S(1)}, u32[]{:S(2)}, u32[]{:S(2)}) collective-permute-start(f32[1,1024]{1,0:T(1,128)} %get-tuple-element.13), channel_id=1, source_target_pairs={{0,16},{1,17},{2,18},{3,19},{4,20},{5,21},{6,22},{7,23},{8,24},{9,... | collective-permute-start | bytes 12296 | tf_op jit(solution)/shard_map/ppermute | solution.py:38
  313.7 23.7 %collective-permute-start.68 = (f32[1,1024]{1,0:T(1,128)}, f32[1,1024]{1,0:T(1,128)S(1)}, u32[]{:S(2)}, u32[]{:S(2)}) collective-permute-start(f32[1,1024]{1,0:T(1,128)} %get-tuple-element.13), channel_id=1, source_target_pairs={{0,32},{1,33},{2,34},{3,35},{4,36},{5,37},{6,38},{7,39},{8,40},{9,... | collective-permute-start | bytes 12296 | tf_op jit(solution)/shard_map/ppermute | solution.py:38
  325.5 14.4 %collective-permute-start.69 = (f32[1,1024]{1,0:T(1,128)}, f32[1,1024]{1,0:T(1,128)S(1)}, u32[]{:S(2)}, u32[]{:S(2)}) collective-permute-start(f32[1,1024]{1,0:T(1,128)} %get-tuple-element.13), channel_id=1, source_target_pairs={{0,48},{1,49},{2,50},{3,51},{4,52},{5,53},{6,54},{7,55},{8,56},{9,... | collective-permute-start | bytes 12296 | tf_op jit(solution)/shard_map/ppermute | solution.py:38
  340.6 36.0 %collective-permute-start.70 = (f32[1,1024]{1,0:T(1,128)S(1)}, f32[1,1024]{1,0:T(1,128)S(1)}, u32[]{:S(2)}, u32[]{:S(2)}) collective-permute-start(f32[1,1024]{1,0:T(1,128)S(1)} %add_add_fusion.1), channel_id=1, source_target_pairs={{0,64},{1,65},{2,66},{3,67},{4,68},{5,69},{6,70},{7,71},{8,72},{9,... | collective-permute-start | bytes 12296 | tf_op jit(solution)/shard_map/ppermute | solution.py:38
  352.9 23.7 %collective-permute-start.71 = (f32[1,1024]{1,0:T(1,128)S(1)}, f32[1,1024]{1,0:T(1,128)S(1)}, u32[]{:S(2)}, u32[]{:S(2)}) collective-permute-start(f32[1,1024]{1,0:T(1,128)S(1)} %add_add_fusion.1), channel_id=1, source_target_pairs={{0,128},{1,129},{2,130},{3,131},{4,132},{5,133},{6,134},{7,135},{8... | collective-permute-start | bytes 12296 | tf_op jit(solution)/shard_map/ppermute | solution.py:38
  364.8 14.2 %collective-permute-start.72 = (f32[1,1024]{1,0:T(1,128)S(1)}, f32[1,1024]{1,0:T(1,128)S(1)}, u32[]{:S(2)}, u32[]{:S(2)}) collective-permute-start(f32[1,1024]{1,0:T(1,128)S(1)} %add_add_fusion.1), channel_id=1, source_target_pairs={{0,192},{1,193},{2,194},{3,195},{4,196},{5,197},{6,198},{7,199},{8... | collective-permute-start | bytes 12296 | tf_op jit(solution)/shard_map/ppermute | solution.py:38
  (99 other events, 1021.3 us)
Sparse Core Ops, SparseCore 0:
  11.7 122.7 all-gather.1

commit v2 on v0

v2 whole, which is shorter than its diff:
```python
import functools
import math

import jax
import jax.numpy as jnp
from jax import lax
from jax.experimental import pallas as pl
from jax.experimental.pallas import tpu as pltpu
from jax.sharding import PartitionSpec as P

EPS = 1e-06
BF16 = jnp.bfloat16
F32 = jnp.float32
AXES = ("chain", "group")
SIDE = 4
ZS = 8
VMEM = pl.BlockSpec(memory_space=pltpu.VMEM)
SMEM = pl.BlockSpec(memory_space=pltpu.SMEM)
PARAMS = pltpu.CompilerParams(vmem_limit_bytes=56 * 1024 * 1024)


def moves(target):
    pairs = []
    for y in range(SIDE):
        for x in range(SIDE):
            for z in range(ZS):
                for c in range(2):
                    to = target(y, x, z, c)
                    if to is not None:
                        ty, tx, tz, tc = to
                        source = ((y * SIDE + x) * ZS + z) * 2 + c
                        dest = ((ty * SIDE + tx) * ZS + tz) * 2 + tc
                        pairs.append((source, dest))
    return pairs


def send(value, target):
    return lax.ppermute(value, AXES, moves(target))


def swap_core(value):
    return send(value, lambda y, x, z, c: (y, x, z, 1 - c))


def x_ring(value):
    return [value] + [send(value, lambda y, x, z, c: (y, (x + k) % SIDE, z, c)) for k in (1, 2, 3)]


def y_ring(value):
    return [value] + [send(value, lambda y, x, z, c: ((y + k) % SIDE, x, z, c)) for k in (1, 2, 3)]


def hop(value, dy, dx=0):
    return send(value, lambda y, x, z, c: (y + dy, (x + dx) % SIDE, z, c) if y + dy < SIDE else None)


def split(a):
    hi = a.astype(BF16)
    return hi, (a - hi.astype(F32)).astype(BF16)


def mul(a, b, dims):
    return lax.dot_general(a, b, (dims, ((), ())), preferred_element_type=F32)


NT = ((1,), (1,))
NN = ((1,), (0,))


def mul3(a, b, dims):
    (ah, al), (bh, bl) = a, b
    return mul(ah, bh, dims) + (mul(ah, bl, dims) + mul(al, bh, dims))


def nt(a, b):
    return mul3(split(a), split(b), NT)


def spot(k, x, bs):
    return pl.ds(pl.multiple_of(lax.rem(x - k + SIDE, SIDE) * bs, bs), bs)


def diagonal_kernel(place, d_ref, f_ref, near, far, out_ref, d, f):
    bs = d_ref.shape[0]
    x, c = place[0], place[1]
    own = (d_ref[...], f_ref[:, :bs], f_ref[:, bs : 2 * bs], f_ref[:, 2 * bs : 3 * bs])
    d[x] = own[0]
    for j in range(3):
        f[x, j] = own[1 + j]
    for k in (1, 2, 3):
        at = lax.rem(x - k + SIDE, SIDE)

        @pl.when(c == 0)
        def _():
            d[at], f[at, 0] = near[k - 1, :bs], near[k - 1, bs:]
            f[at, 1], f[at, 2] = far[k - 1, :bs], far[k - 1, bs:]

        @pl.when(c == 1)
        def _():
            d[at], f[at, 0] = far[k - 1, :bs], far[k - 1, bs:]
            f[at, 1], f[at, 2] = near[k - 1, :bs], near[k - 1, bs:]

    out_ref[...] = jnp.zeros_like(out_ref)
    columns = []
    for i in range(SIDE):
        above = []
        for k in range(i):
            part = nt(columns[k], f[i, k])
            for j in range(k + 1):
                piece = part[j * bs : (j + 1) * bs]
                if j < len(above):
                    above[j] = above[j] + piece
                else:
                    above.append(piece)
        column = d[i].T
        if above:
            column = jnp.concatenate([-nt(jnp.concatenate(above, 0), d[i]), column], 0)
        columns.append(column)
        out_ref[: (i + 1) * bs, i * bs : (i + 1) * bs] = column


def diagonal(place, d, f, near, far):
    bs = d.shape[0]
    return pl.pallas_call(
        diagonal_kernel,
        in_specs=[SMEM] + [VMEM] * 4,
        out_specs=VMEM,
        out_shape=jax.ShapeDtypeStruct((SIDE * bs, SIDE * bs), F32),
        scratch_shapes=[pltpu.VMEM((SIDE, bs, bs), F32), pltpu.VMEM((SIDE, 3, bs, bs), F32)],
        compiler_params=PARAMS,
    )(place, d, f, near, far)


def first_factor_kernel(place, s_ref, f_ref, out_ref):
    out_ref[...] = nt(s_ref[...], f_ref[...])


def first_factor(place, s, factor):
    m, size = s.shape
    bs = factor.shape[0]
    return pl.pallas_call(
        first_factor_kernel,
        grid_spec=pltpu.PrefetchScalarGridSpec(
            num_scalar_prefetch=1,
            grid=(1,),
            in_specs=[
                pl.BlockSpec((m, size), lambda i, p: (0, 0)),
                pl.BlockSpec((bs, size), lambda i, p: (0, jnp.maximum(p[3] - 1, 0))),
            ],
            out_specs=pl.BlockSpec((m, bs), lambda i, p: (0, 0)),
        ),
        out_shape=jax.ShapeDtypeStruct((m, bs), F32),
        compiler_params=PARAMS,
    )(place, s, factor)


def first_inverse_kernel(place, t0, t1, t2, t3, st, out_ref, own_ref, t):
    x = place[0]
    bs = t0.shape[1]
    for k, ref in enumerate((t0, t1, t2, t3)):
        t[:, spot(k, x, bs)] = ref[...]
    out_ref[...] = -mul3(split(t[...]), split(st[...]), NN)
    own_ref[...] = out_ref[:, spot(0, x, bs)]


def first_inverse(place, ts, st):
    m, bs = ts[0].shape
    size = SIDE * bs
    return pl.pallas_call(
        first_inverse_kernel,
        in_specs=[SMEM] + [VMEM] * (SIDE + 1),
        out_specs=[VMEM, VMEM],
        out_shape=[jax.ShapeDtypeStruct((m, size), F32), jax.ShapeDtypeStruct((m, bs), F32)],
        scratch_shapes=[pltpu.VMEM((m, size), F32)],
        compiler_params=PARAMS,
    )(place, *ts, st)


def second_factor_kernel(place, s2, s3, m1, m2, t1, f_ref, out_ref):
    m, size = s2.shape
    y = place[3]
    low = y == 2
    zero = nt(jnp.where(low, s2[...], s3[...]), f_ref[:, :size])
    both = jnp.concatenate([jnp.where(low, m1[...], m2[...]), s2[...]], 0)
    both = nt(both, f_ref[:, size:])
    out_ref[:m] = jnp.where(y >= 2, zero + both[:m], 0.0)
    out_ref[m:] = jnp.where(low, t1[...], jnp.where(y == 3, both[m:], 0.0))


def second_factor(place, s2, s3, m1, m2, t1, factor):
    m, bs = t1.shape
    args = (s2, s3, m1, m2, t1)
    return pl.pallas_call(
        second_factor_kernel,
        grid=(1,),
        in_specs=[SMEM]
        + [pl.BlockSpec(a.shape, lambda i: (0, 0)) for a in args]
        + [pl.BlockSpec((bs, 2 * SIDE * bs), lambda i: (0, 0))],
        out_specs=pl.BlockSpec((2 * m, bs), lambda i: (0, 0)),
        out_shape=jax.ShapeDtypeStruct((2 * m, bs), F32),
        compiler_params=PARAMS,
    )(place, *args, factor)


def interleave(full, mine, other, c):
    m = full.shape[0] // (2 * ZS)
    for z in range(ZS):
        full[pl.ds(pl.multiple_of((2 * z + c) * m, m), m), :] = mine[z]
        full[pl.ds(pl.multiple_of((2 * z + 1 - c) * m, m), m), :] = other[z]


def second_inverse_kernel(place, *refs):
    ts, qs, (st, ma, mb, out_ref, t, q, full) = refs[:SIDE], refs[SIDE : 2 * SIDE], refs[2 * SIDE :]
    x, c, y = place[0], place[1], place[3]
    m, bs = ts[0].shape
    for k in range(SIDE):
        t[:, spot(k, x, bs)] = ts[k][...]
        q[:, spot(k, x, bs)] = qs[k][...]
    interleave(full, ma, mb, c)
    total = mul3(split(t[...]), split(st[...]), NN)
    below = mul3(split(q[...]), split(full[...]), NN)
    total = total + jnp.where(y == 3, below, 0.0)
    half = m // 2
    out_ref[:half] = jnp.where(y >= 2, -total[:half], 0.0)
    out_ref[half:] = jnp.where(y == 3, -total[half:], 0.0)


def second_inverse(place, ts, qs, st, ma, mb):
    m, bs = ts[0].shape
    size = SIDE * bs
    fixed = lambda a: pl.BlockSpec(a.shape, lambda i, p: (0,) * a.ndim)
    return pl.pallas_call(
        second_inverse_kernel,
        grid_spec=pltpu.PrefetchScalarGridSpec(
            num_scalar_prefetch=1,
            grid=(1,),
            in_specs=[fixed(a) for a in (*ts, *qs)]
            + [pl.BlockSpec((size, bs), lambda i, p: (0, p[0])), fixed(ma), fixed(mb)],
            out_specs=pl.BlockSpec((m, bs), lambda i, p: (0, 0)),
            scratch_shapes=[pltpu.VMEM((m, size), F32)] * 2 + [pltpu.VMEM((size, bs), F32)],
        ),
        out_shape=jax.ShapeDtypeStruct((m, bs), F32),
        compiler_params=PARAMS,
    )(place, *ts, *qs, st, ma, mb)


def panel_kernel(beta, train_ref, cand_ref, scale_ref, hi_ref, lo_ref):
    rows = train_ref[...]
    wide = rows.astype(F32)
    square = jnp.sum(wide * wide, axis=1, keepdims=True)
    row = jnp.broadcast_to(beta * lax.rsqrt(square + EPS), (rows.shape[0], 128)).T[:1]
    hi, lo = split(jnp.exp(mul(cand_ref[...], rows, NT) * row * scale_ref[...]))
    hi_ref[0] = hi
    lo_ref[0] = lo


def make_panel(train, cand, cand_scale, size):
    total, e = train.shape
    n = cand.shape[0]
    rows = size // 2
    spec = pl.BlockSpec((1, n, rows), lambda i: (i // 2, 0, i % 2))
    shape = jax.ShapeDtypeStruct((total // size, n, size), BF16)
    return pl.pallas_call(
        functools.partial(panel_kernel, 0.5 * math.sqrt(e)),
        grid=(total // rows,),
        in_specs=[
            pl.BlockSpec((rows, e), lambda i: (i, 0)),
            pl.BlockSpec((n, e), lambda i: (0, 0)),
            pl.BlockSpec((n, 1), lambda i: (0, 0)),
        ],
        out_specs=[spec, spec],
        out_shape=[shape, shape],
        cost_estimate=pl.CostEstimate(flops=4 * total * n * e, bytes_accessed=6 * total * n, transcendentals=total * n),
        compiler_params=PARAMS,
    )(train, cand, cand_scale)


def arrange_kernel(place, *refs):
    z = place[2]
    out = refs[-1]
    for k in range(ZS):
        out[lax.rem(z - k + ZS, ZS)] = refs[k][...]


def z_gather(place, own):
    parts = [own]
    for k in range(1, ZS):
        parts.append(send(own, lambda y, x, z, c: (y, x, (z + k) % ZS, c)))
    mine = pl.pallas_call(
        arrange_kernel,
        in_specs=[SMEM] + [VMEM] * ZS,
        out_specs=VMEM,
        out_shape=jax.ShapeDtypeStruct((ZS,) + own.shape, own.dtype),
        compiler_params=PARAMS,
    )(place, *parts)
    return mine, swap_core(mine)


def apply_kernel(last, sup, place, *refs):
    if last:
        m2, win, h0, l0, h1, l1, targets, out, mean, full, mh, ml = refs
    else:
        st, mine, other, h0, l0, h1, l1, out, full, mh, ml = refs
    size = full.shape[0]

    @pl.when(pl.program_id(0) == 0)
    def _():
        if last:
            m = size // (2 * ZS)
            for g in range(2 * ZS):
                full[g * m : (g + 1) * m] = m2[g, :m]
            mh[:size], ml[:size] = split(full[...])
            for g in range(2 * ZS):
                full[g * m : (g + 1) * m] = m2[g, m:]
        else:
            mh[:size], ml[:size] = split(st[...])
            interleave(full, mine, other, place[1])
        mh[size:], ml[size:] = split(full[...])

    w = mul3((h0[0], l0[0]), (mh[:size], ml[:size]), NN)
    w = w + mul3((h1[0], l1[0]), (mh[size:], ml[size:]), NN)
    if last:
        w = (w + win[...]).T
        out[...] = w
        mean[...] = jnp.sum(w * targets[...], axis=0, keepdims=True)
    else:
        out[...] = w


def apply(sup, place, arrays, panel, bs, targets=None):
    _, n, size = panel[0].shape
    last = targets is not None
    tile = n // 2
    fixed = lambda shape: pl.BlockSpec(shape, lambda i, s, p: (0,) * len(shape))
    args = [*arrays, *panel, *panel]
    specs = [fixed(a.shape) for a in arrays]
    across = pl.BlockSpec((tile, bs), lambda i, s, p: (i, 0))
    if last:
        specs[1] = across
    else:
        specs[0] = pl.BlockSpec((size, bs), lambda i, s, p: (0, p[0]))
    specs += [pl.BlockSpec((1, tile, size), lambda i, s, p: (s[0], i, 0))] * 2
    specs += [pl.BlockSpec((1, tile, size), lambda i, s, p: (s[1], i, 0))] * 2
    shapes, outs = [jax.ShapeDtypeStruct((n, bs), F32)], [across]
    if last:
        args.append(targets)
        specs.append(fixed(targets.shape))
        shapes = [jax.ShapeDtypeStruct((bs, n), F32), jax.ShapeDtypeStruct((1, n), F32)]
        outs = [pl.BlockSpec((bs, tile), lambda i, s, p: (0, i)), pl.BlockSpec((1, tile), lambda i, s, p: (0, i))]
    return pl.pallas_call(
        functools.partial(apply_kernel, last),
        grid_spec=pltpu.PrefetchScalarGridSpec(
            num_scalar_prefetch=2,
            grid=(n // tile,),
            in_specs=specs,
            out_specs=outs,
            scratch_shapes=[pltpu.VMEM((size, bs), F32)] + [pltpu.VMEM((2 * size, bs), BF16)] * 2,
        ),
        out_shape=shapes,
        cost_estimate=pl.CostEstimate(flops=24 * n * bs * size, bytes_accessed=8 * n * size, transcendentals=0),
        compiler_params=PARAMS,
    )(sup, place, *args)


def shards(train_emb, cand_emb, factor, diag_inverse, targets):
    bs = diag_inverse.shape[1]
    n = cand_emb.shape[0]
    size = SIDE * bs
    p = lax.axis_index("chain")
    group = lax.axis_index("group")
    y, x, z, c = p // SIDE, p % SIDE, group // 2, group % 2
    place = jnp.stack([x, c, z, y]).astype(jnp.int32)

    train = lax.all_gather(train_emb, AXES, axis=0, tiled=True)

    square = lax.dynamic_slice(factor, (0, y * size), (bs, size))
    pair0 = jnp.concatenate([diag_inverse, square[:, :bs]], 0)
    pair1 = jnp.concatenate([square[:, bs : 2 * bs], square[:, 2 * bs : 3 * bs]], 0)
    pair = jnp.where(c == 0, pair0, pair1)
    near = jnp.stack(
        [send(pair, lambda y, x, z, c: (y, (x + k) % SIDE, z, c) if c == 0 or x >= 2 else None) for k in (1, 2, 3)]
    )
    st = diagonal(place, diag_inverse, square, near, swap_core(near))

    m = size // (2 * ZS)
    sl = lax.dynamic_slice(st, (group * m, 0), (m, size))
    t1 = first_factor(place, hop(sl, 1), factor)
    m1, m1_own = first_inverse(place, x_ring(t1), st)
    t2 = second_factor(place, hop(sl, 2), hop(sl, 3), hop(m1, 1), hop(m1, 2), t1, factor)
    m1_full = z_gather(place, m1_own)
    m2 = second_inverse(place, x_ring(t2), [hop(t2, 1, k) for k in range(SIDE)], st, *m1_full)
    m2_full = lax.all_gather(m2, "group", axis=0)

    cand_f = cand_emb.astype(F32)
    cand_scale = lax.rsqrt(jnp.sum(cand_f * cand_f, axis=1, keepdims=True) + EPS)
    panel = make_panel(train, cand_emb, cand_scale, size)
    sup = jnp.stack([y, jnp.maximum(y - 1, 0)]).astype(jnp.int32)
    (w,) = apply(sup, place, (st, *m1_full), panel, bs)
    w, mean = apply(jnp.arange(2, dtype=jnp.int32), place, (m2_full, w), panel, bs, targets.reshape(bs, 1))
    for ring in (x_ring, y_ring):
        a, b, d, e = ring(mean)
        mean = (a + b) + (d + e)
    return w, mean.reshape(n)


def solution(mesh):
    in_specs = (
        P(("chain", "group"), None),
        P("group", None),
        P("chain", None),
        P("chain", None),
        P("chain"),
    )
    out_specs = (P("chain", "group"), P("group"))
    return jax.shard_map(shards, mesh=mesh, in_specs=in_specs, out_specs=out_specs, check_vma=False)
```

time: 1740 us -> 231 us (0.13)
  waiting for transfers between devices: 1630 us -> 65.8 us
  starting transfers between devices: 0.65 us -> 71.3 us
  Pallas kernels: 0 us -> 60.9 us
  blocking collectives: 55.9 us -> 0 us
  other arithmetic: 25.6 us -> 4.11 us
    psum x16 -> x0, waiting for transfers between devices: 1630 us -> none  [from_root(): return lax.psum(jnp.where(mine, x, jnp.zeros_like(x)), axis)]
    ppermute x0 -> x33, starting transfers between devices: none -> 71.2 us  [send(): return lax.ppermute(value, AXES, moves(target))]
    pallas_call x0 -> x9, Pallas kernels: none -> 60.9 us  [the longest x2 18.1 us: apply(): pl.pallas_call(functools.partial(apply_kernel, last), grid_spec=pltpu.Pre...]
    ppermute x0 -> x33, waiting for transfers between devices: none -> 51.9 us  [send(): return lax.ppermute(value, AXES, moves(target))]
    psum x1 -> x0, blocking collectives: 32.8 us -> none  [shards(): post_mean = lax.psum(local_mean, 'chain')]
    all_gather x1 -> x0, blocking collectives: 23.1 us -> none  [shards(): piece = lax.all_gather(train_emb, 'group', axis=0, tiled=True)]
    select_n x32 -> x1, other arithmetic: 23.2 us -> 1.02 us  [shards(): pair = jnp.where(c == 0, pair0, pair1)]
  transfers between devices with their start and end apart: 16 -> 35, of which waited for: 16 -> 16; matrix products, arithmetic and copies ran while one was open for 0% -> 4% of each run, Pallas kernels for 0% -> 23%
where the time goes in v2:
time: 231 us; the launch traced here: 229 us
  starting transfers between devices  71.3 us (31%)
  waiting for transfers between devices  65.8 us (28%)
  Pallas kernels  60.9 us (26%)
  between operations  14.5 us (6%)
  local copies, waits for them, and re-layouts  12.2 us (5%)
  other arithmetic  4.11 us (2%)
    ppermute x33, starting transfers between devices, send(): return lax.ppermute(value, AXES, moves(target))  71.2 us
    ppermute x33, waiting for transfers between devices, send(): return lax.ppermute(value, AXES, moves(target))  51.9 us
    pallas_call x2, Pallas kernels, apply(): pl.pallas_call(functools.partial(apply_kernel, last), grid_spec=pltpu.Pre...  18.1 us
    pallas_call x1, Pallas kernels, make_panel(): pl.pallas_call(functools.partial(panel_kernel, 0.5 * math.sqrt(e)), grid=...  17.5 us
    all_gather x1, waiting for transfers between devices, shards(): m2_full = lax.all_gather(m2, 'group', axis=0)  13.2 us
    pallas_call x1, Pallas kernels, diagonal(): pl.pallas_call(diagonal_kernel, in_specs=[SMEM] + [VMEM] * 4, out_specs=V...  7.82 us
    unnamed x54, local copies, waits for them, and re-layouts  5.32 us
  transfers between devices with their start and end apart: 35, of which 16 were waited for; matrix products, arithmetic and copies ran while one was open for 4% of the time, Pallas kernels for 23%

profile of v2, /device:TPU:1, one launch (start us, length us, event | category | flops | bytes accessed | tf_op | source)
XLA Modules:
  0.0 228.8 jit_solution(16503302825920393849)
XLA Ops:
  8.0 1.2 constant_dynamic-slice_fusion.1
  10.2 1.3 collective-permute-start
  11.5 1.3 collective-permute-start.1
  13.5 11.3 %collective-permute-done = f32[512,256]{1,0:T(8,128)S(1)} collective-permute-done((f32[512,256]{1,0:T(8,128)S(1)}, f32[512,256]{1,0:T(8,128)S(1)}, u32[]{:S(2)}, u32[]{:S(2)}) %collective-permute-start) | collective-permute-done | bytes 524320 | tf_op jit(solution)/shard_map/ppermute | solution.py:38
  24.7 14.6 %collective-permute-done.1 = f32[512,256]{1,0:T(8,128)S(1)} collective-permute-done((f32[512,256]{1,0:T(8,128)S(1)}, f32[512,256]{1,0:T(8,128)S(1)}, u32[]{:S(2)}, u32[]{:S(2)}) %collective-permute-start.1) | collective-permute-done | bytes 524320 | tf_op jit(solution)/shard_map/ppermute | solution.py:38
  39.5 1.6 collective-permute-start.3
  41.8 2.3 %constant_dynamic-slice_fusion.4.f_ref = f32[256,1024]{1,0:T(8,128)} fusion(f32[256,4096]{1,0:T(8,128)} %f_ref.3, s32[]{:T(128)S(6)} %select_n.36), kind=kLoop, calls=%fused_computation.10 | loop fusion | bytes 2097156 | tf_op jit(solution)/shard_map/dynamic_slice | solution.py:376
  44.2 1.1 copy-done.3
  45.3 7.8 %shard_map.68.st.refs_8_.refs_0_ = f32[1024,1024]{1,0:T(8,128)} custom-call(s32[4]{0:T(128)} %pad_add_fusion.place, f32[256,256]{1,0:T(8,128)} %d_ref.1, f32[256,1024]{1,0:T(8,128)} %constant_dynamic-slice_fusion.4.f_ref, f32[3,512,256]{2,1,0:T(8,128)} %copy-done, f32[3,512,256]{2,1,0:T(8,128)} %copy-done.3), custom_call_target="tpu_custom_call" | custom-call | tf_op jit(solution)/shard_map/pallas_call | solution.py:124
  54.1 3.2 %collective-permute-start.6 = (f32[64,1024]{1,0:T(8,128)S(1)}, f32[64,1024]{1,0:T(8,128)S(1)}, u32[]{:S(2)}, u32[]{:S(2)}) collective-permute-start(f32[64,1024]{1,0:T(8,128)S(1)} %constant_dynamic-slice_fusion.3), channel_id=1, source_target_pairs={{0,64},{1,65},{2,66},{3,67},{4,68},{5,69},{6,70},{7,71},{8,72},{9,... | collective-permute-start | bytes 786440 | tf_op jit(solution)/shard_map/ppermute | solution.py:38
  57.3 5.3 %collective-permute-done.6.s_ref = f32[64,1024]{1,0:T(8,128)S(1)} collective-permute-done((f32[64,1024]{1,0:T(8,128)S(1)}, f32[64,1024]{1,0:T(8,128)S(1)}, u32[]{:S(2)}, u32[]{:S(2)}) %collective-permute-start.6) | collective-permute-done | bytes 262176 | tf_op jit(solution)/shard_map/ppermute | solution.py:38
  63.3 3.2 %shard_map.69.t0.t1 = f32[64,256]{1,0:T(8,128)} custom-call(s32[4]{0:T(128)} %pad_add_fusion.place, f32[64,1024]{1,0:T(8,128)} %copy-done.8, f32[256,4096]{1,0:T(8,128)} %f_ref.3), custom_call_target="tpu_custom_call" | custom-call | tf_op jit(solution)/shard_map/pallas_call | solution.py:141
  66.5 1.2 collective-permute-start.7
  68.4 2.1 collective-permute-start.9
  71.0 1.6 collective-permute-done.8.t2
  73.9 4.4 %shard_map.70 = (f32[64,1024]{1,0:T(8,128)}, f32[64,256]{1,0:T(8,128)}) custom-call(s32[4]{0:T(128)} %pad_add_fusion.place, f32[64,256]{1,0:T(8,128)} %shard_map.69.t0.t1, f32[64,256]{1,0:T(8,128)} %copy-done.16, f32[64,256]{1,0:T(8,128)} %copy-done.17, f32[64,256]{1,0:T(8,128)} %copy-done.18, f32[1024,1024]{1,0:T(8,128)} %shard_map.68.st.refs_8_.refs_0_), custom_call_target="tpu_custom_call" | custom-call | tf_op jit(solution)/shard_map/pallas_call | solution.py:169
  78.3 2.1 collective-permute-start.19
  80.4 3.0 %collective-permute-start.20 = (f32[64,256]{1,0:T(8,128)}, f32[64,256]{1,0:T(8,128)S(1)}, u32[]{:S(2)}, u32[]{:S(2)}) collective-permute-start(f32[64,256]{1,0:T(8,128)} %get-tuple-element.9.refs_0_), channel_id=1, source_target_pairs={{0,4},{1,5},{2,6},{3,7},{4,8},{5,9},{6,10},{7,11},{8,12},{9,13},{1... | collective-permute-start | bytes 196616 | tf_op jit(solution)/shard_map/ppermute | solution.py:38
  83.4 3.6 %collective-permute-start.21 = (f32[64,256]{1,0:T(8,128)}, f32[64,256]{1,0:T(8,128)S(1)}, u32[]{:S(2)}, u32[]{:S(2)}) collective-permute-start(f32[64,256]{1,0:T(8,128)} %get-tuple-element.9.refs_0_), channel_id=1, source_target_pairs={{0,6},{1,7},{2,8},{3,9},{4,10},{5,11},{6,12},{7,13},{8,14},{9,15},... | collective-permute-start | bytes 196616 | tf_op jit(solution)/shard_map/ppermute | solution.py:38
  87.4 4.5 %collective-permute-start.23 = (f32[64,256]{1,0:T(8,128)}, f32[64,256]{1,0:T(8,128)S(1)}, u32[]{:S(2)}, u32[]{:S(2)}) collective-permute-start(f32[64,256]{1,0:T(8,128)} %get-tuple-element.9.refs_0_), channel_id=1, source_target_pairs={{0,10},{1,11},{2,12},{3,13},{4,14},{5,15},{6,0},{7,1},{8,2},{9,3},... | collective-permute-start | bytes 196616 | tf_op jit(solution)/shard_map/ppermute | solution.py:38
  91.9 2.5 %collective-permute-start.24 = (f32[64,256]{1,0:T(8,128)}, f32[64,256]{1,0:T(8,128)S(1)}, u32[]{:S(2)}, u32[]{:S(2)}) collective-permute-start(f32[64,256]{1,0:T(8,128)} %get-tuple-element.9.refs_0_), channel_id=1, source_target_pairs={{0,12},{1,13},{2,14},{3,15},{4,0},{5,1},{6,2},{7,3},{8,4},{9,5},{1... | collective-permute-start | bytes 196616 | tf_op jit(solution)/shard_map/ppermute | solution.py:38
  95.5 5.1 %collective-permute-start.4 = (f32[64,1024]{1,0:T(8,128)S(1)}, f32[64,1024]{1,0:T(8,128)S(1)}, u32[]{:S(2)}, u32[]{:S(2)}) collective-permute-start(f32[64,1024]{1,0:T(8,128)S(1)} %constant_dynamic-slice_fusion.3), channel_id=1, source_target_pairs={{0,128},{1,129},{2,130},{3,131},{4,132},{5,133},{6,134},{7,135},{8... | collective-permute-start | bytes 786440 | tf_op jit(solution)/shard_map/ppermute | solution.py:38
  100.6 1.3 collective-permute-start.5
  101.9 1.7 collective-permute-start.10
  103.6 2.5 %collective-permute-start.11 = (f32[64,1024]{1,0:T(8,128)}, f32[64,1024]{1,0:T(8,128)S(1)}, u32[]{:S(2)}, u32[]{:S(2)}) collective-permute-start(f32[64,1024]{1,0:T(8,128)} %get-tuple-element.8), channel_id=1, source_target_pairs={{0,128},{1,129},{2,130},{3,131},{4,132},{5,133},{6,134},{7,135},{8... | collective-permute-start | bytes 786440 | tf_op jit(solution)/shard_map/ppermute | solution.py:38
  106.8 2.0 shard_map.72.refs_9_.refs_1_
  108.8 5.2 %collective-permute-start.26 = (f32[8,64,256]{2,1,0:T(8,128)}, f32[8,64,256]{2,1,0:T(8,128)S(1)}, u32[]{:S(2)}, u32[]{:S(2)}) collective-permute-start(f32[8,64,256]{2,1,0:T(8,128)} %shard_map.72.refs_9_.refs_1_), channel_id=1, source_target_pairs={{0,1},{1,0},{2,3},{3,2},{4,5},{5,4},{6,7},{7,6},{8,9},{9,8},{10,11... | collective-permute-start | bytes 1572872 | tf_op jit(solution)/shard_map/ppermute | solution.py:38
  114.1 7.4 %collective-permute-done.5.s3 = f32[64,1024]{1,0:T(8,128)S(1)} collective-permute-done((f32[64,1024]{1,0:T(8,128)S(1)}, f32[64,1024]{1,0:T(8,128)S(1)}, u32[]{:S(2)}, u32[]{:S(2)}) %collective-permute-start.5) | collective-permute-done | bytes 262176 | tf_op jit(solution)/shard_map/ppermute | solution.py:38
  121.5 4.4 %collective-permute-done.11.m2 = f32[64,1024]{1,0:T(8,128)S(1)} collective-permute-done((f32[64,1024]{1,0:T(8,128)}, f32[64,1024]{1,0:T(8,128)S(1)}, u32[]{:S(2)}, u32[]{:S(2)}) %collective-permute-start.11) | collective-permute-done | bytes 262176 | tf_op jit(solution)/shard_map/ppermute | solution.py:38
  126.6 3.7 %shard_map.71.refs_0_ = f32[128,256]{1,0:T(8,128)} custom-call(s32[4]{0:T(128)} %pad_add_fusion.place, f32[64,1024]{1,0:T(8,128)} %copy-done.4, f32[64,1024]{1,0:T(8,128)} %copy-done.5, f32[64,1024]{1,0:T(8,128)} %copy-done.6, f32[64,1024]{1,0:T(8,128)} %copy-done.7, f32[64,256]{1,0:T(8,128)} %shard_map.69.t0.t1, f32[256,4096]{1,0:T(8,128)} %f_ref.3), custom_call_target="tpu_custom_call" | custom-call | tf_op jit(solution)/shard_map/pallas_call | solution.py:193
  131.1 2.1 collective-permute-start.13
  133.6 1.3 collective-permute-start.15
  135.6 6.1 %collective-permute-start.16 = (f32[128,256]{1,0:T(8,128)}, f32[128,256]{1,0:T(8,128)S(1)}, u32[]{:S(2)}, u32[]{:S(2)}) collective-permute-start(f32[128,256]{1,0:T(8,128)} %shard_map.71.refs_0_), channel_id=1, source_target_pairs={{0,80},{1,81},{2,82},{3,83},{4,84},{5,85},{6,86},{7,87},{8,88},{9,... | collective-permute-start | bytes 393224 | tf_op jit(solution)/shard_map/ppermute | solution.py:38
  141.6 2.5 %collective-permute-start.17 = (f32[128,256]{1,0:T(8,128)}, f32[128,256]{1,0:T(8,128)S(1)}, u32[]{:S(2)}, u32[]{:S(2)}) collective-permute-start(f32[128,256]{1,0:T(8,128)} %shard_map.71.refs_0_), channel_id=1, source_target_pairs={{0,96},{1,97},{2,98},{3,99},{4,100},{5,101},{6,102},{7,103},{8,104... | collective-permute-start | bytes 393224 | tf_op jit(solution)/shard_map/ppermute | solution.py:38
  144.2 3.4 %collective-permute-start.18 = (f32[128,256]{1,0:T(8,128)}, f32[128,256]{1,0:T(8,128)S(1)}, u32[]{:S(2)}, u32[]{:S(2)}) collective-permute-start(f32[128,256]{1,0:T(8,128)} %shard_map.71.refs_0_), channel_id=1, source_target_pairs={{0,112},{1,113},{2,114},{3,115},{4,116},{5,117},{6,118},{7,119},{8... | collective-permute-start | bytes 393224 | tf_op jit(solution)/shard_map/ppermute | solution.py:38
  147.7 2.2 collective-permute-done.18.refs_7_
  151.3 4.1 %shard_map.73 = f32[128,256]{1,0:T(8,128)} custom-call(s32[4]{0:T(128)} %pad_add_fusion.place, f32[128,256]{1,0:T(8,128)} %shard_map.71.refs_0_, f32[128,256]{1,0:T(8,128)} %copy-done.9, f32[128,256]{1,0:T(8,128)} %copy-done.10, f32[128,256]{1,0:T(8,128)} %copy-done.11, f32[128,256]{1,0:T(8,128)} %copy-done.12, f32[128,256]{1,0:T(8,128)} %copy-done.13, ...), custom_call_target="tpu_custom_call" | custom-call | tf_op jit(solution)/shard_map/pallas_call | solution.py:232
  158.3 17.5 %shard_map.74 = (bf16[4,1024,1024]{2,1,0:T(8,128)(2,1)}, bf16[4,1024,1024]{2,1,0:T(8,128)(2,1)}) custom-call(bf16[4096,1024]{1,0:T(8,128)(2,1)} %all-gather.4.cloned.1.call-done.train_ref, bf16[1024,1024]{1,0:T(8,128)(2,1)} %cand_ref.1, f32[1024,1]{1,0:T(8,128)} %copy.7.scale_ref), custom_call_target="tpu_custom_call" | custom-call | flops 17179869184 | bytes 25165824 | tf_op jit(solution)/shard_map/pallas_call | solution.py:263
  175.9 8.9 %shard_map.75.refs_1_ = f32[1024,256]{1,0:T(8,128)} custom-call(s32[2]{0:T(128)} %pad_add_fusion.1.sup, s32[4]{0:T(128)} %pad_add_fusion.place, f32[1024,1024]{1,0:T(8,128)} %shard_map.68.st.refs_8_.refs_0_, f32[8,64,256]{2,1,0:T(8,128)} %shard_map.72.refs_9_.refs_1_, f32[8,64,256]{2,1,0:T(8,128)} %copy-done.1, ...), custom_call_target="tpu_custom_call" | custom-call | flops 6442450944 | bytes 8388608 | tf_op jit(solution)/shard_map/pallas_call | solution.py:350
  184.8 13.2 %all-gather.6.cloned.1.call-done = f32[2048,256]{1,0:T(8,128)} async-done(((f32[128,256]{1,0:T(8,128)}), f32[2048,256]{1,0:T(8,128)}) %all-gather.6.cloned.1.call-update) | async-done | bytes 2097168 | tf_op jit(solution)/shard_map/all_gather | solution.py:392
  198.6 9.3 %shard_map.76 = (f32[256,1024]{1,0:T(8,128)}, f32[1,1024]{1,0:T(1,128)}) custom-call(s32[2]{0:T(128)} %iota.3.sup, s32[4]{0:T(128)} %pad_add_fusion.place, f32[16,128,256]{2,1,0:T(8,128)} %bitcast.12, f32[1024,256]{1,0:T(8,128)} %shard_map.75.refs_1_, bf16[4,1024,1024]{2,1,0:T(8,128)(2,1)} %get-tuple-element.10.refs_3_.refs_5_.refs_2_.refs_4_, ...), custom_call_target="tpu_custom_call" | custom-call | flops 6442450944 | bytes 8388608 | tf_op jit(solution)/shard_map/pallas_call | solution.py:350
  207.8 1.3 collective-permute-start.27
  209.1 2.4 %collective-permute-start.28 = (f32[1,1024]{1,0:T(1,128)}, f32[1,1024]{1,0:T(1,128)S(1)}, u32[]{:S(2)}, u32[]{:S(2)}) collective-permute-start(f32[1,1024]{1,0:T(1,128)} %get-tuple-element.13), channel_id=1, source_target_pairs={{0,32},{1,33},{2,34},{3,35},{4,36},{5,37},{6,38},{7,39},{8,40},{9,... | collective-permute-start | bytes 12296 | tf_op jit(solution)/shard_map/ppermute | solution.py:38
  211.5 1.1 collective-permute-start.29
  213.3 1.2 collective-permute-done.29
  215.2 1.2 collective-permute-start.30
  216.4 2.4 %collective-permute-start.31 = (f32[1,1024]{1,0:T(1,128)S(1)}, f32[1,1024]{1,0:T(1,128)S(1)}, u32[]{:S(2)}, u32[]{:S(2)}) collective-permute-start(f32[1,1024]{1,0:T(1,128)S(1)} %add_add_fusion.1), channel_id=1, source_target_pairs={{0,128},{1,129},{2,130},{3,131},{4,132},{5,133},{6,134},{7,135},{8... | collective-permute-start | bytes 12296 | tf_op jit(solution)/shard_map/ppermute | solution.py:38
  218.8 1.2 collective-permute-start.32
  (101 shorter events, 20.4 us)
Async XLA Ops:
  7.2 151.2 %all-gather.4.cloned.1.call-start = ((), (), s32[]{:S(2)}) async-start(), calls=%async_computation | async-start | bytes 8421376 | tf_op jit(solution)/shard_map/all_gather | solution.py:374
  7.9 190.1 %all-gather.6.cloned.1.call-start = ((), (), s32[]{:S(2)}) async-start(), calls=%async_computation.1 | async-start | bytes 2228224 | tf_op jit(solution)/shard_map/all_gather | solution.py:392
  10.2 14.6 %collective-permute-start = (f32[512,256]{1,0:T(8,128)S(1)}, f32[512,256]{1,0:T(8,128)S(1)}, u32[]{:S(2)}, u32[]{:S(2)}) collective-permute-start(f32[512,256]{1,0:T(8,128)S(1)} %maximum_select_fusion), channel_id=1, source_target_pairs={{0,16},{2,18},{4,20},{6,22},{8,24},{10,26},{12,28},{14,30},{16,32}... | collective-permute-start | bytes 1572872 | tf_op jit(solution)/shard_map/ppermute | solution.py:38
  11.5 27.9 %collective-permute-start.1 = (f32[512,256]{1,0:T(8,128)S(1)}, f32[512,256]{1,0:T(8,128)S(1)}, u32[]{:S(2)}, u32[]{:S(2)}) collective-permute-start(f32[512,256]{1,0:T(8,128)S(1)} %maximum_select_fusion), channel_id=1, source_target_pairs={{0,32},{2,34},{4,36},{6,38},{8,40},{10,42},{12,44},{14,46},{16,48}... | collective-permute-start | bytes 1572872 | tf_op jit(solution)/shard_map/ppermute | solution.py:38
  12.8 26.6 %collective-permute-start.2 = (f32[512,256]{1,0:T(8,128)S(1)}, f32[512,256]{1,0:T(8,128)S(1)}, u32[]{:S(2)}, u32[]{:S(2)}) collective-permute-start(f32[512,256]{1,0:T(8,128)S(1)} %maximum_select_fusion), channel_id=1, source_target_pairs={{0,48},{2,50},{4,52},{6,54},{8,56},{10,58},{12,60},{14,62},{16,0},... | collective-permute-start | bytes 1572872 | tf_op jit(solution)/shard_map/ppermute | solution.py:38
  39.5 4.7 %copy-start = (f32[3,512,256]{2,1,0:T(8,128)}, f32[3,512,256]{2,1,0:T(8,128)S(1)}, u32[]{:S(2)}) copy-start(f32[3,512,256]{2,1,0:T(8,128)S(1)} %pad_maximum_fusion.near) | copy-start | bytes 4718596
  39.5 4.7 %collective-permute-start.3 = (f32[3,512,256]{2,1,0:T(8,128)S(1)}, f32[3,512,256]{2,1,0:T(8,128)S(1)}, u32[]{:S(2)}, u32[]{:S(2)}) collective-permute-start(f32[3,512,256]{2,1,0:T(8,128)S(1)} %pad_maximum_fusion.near), channel_id=1, source_target_pairs={{0,1},{1,0},{2,3},{3,2},{4,5},{5,4},{6,7},{7,6},{8,9},{9,8},{10,11... | collective-permute-start | bytes 4718600 | tf_op jit(solution)/shard_map/ppermute | solution.py:38
  54.1 8.5 %collective-permute-start.6 = (f32[64,1024]{1,0:T(8,128)S(1)}, f32[64,1024]{1,0:T(8,128)S(1)}, u32[]{:S(2)}, u32[]{:S(2)}) collective-permute-start(f32[64,1024]{1,0:T(8,128)S(1)} %constant_dynamic-slice_fusion.3), channel_id=1, source_target_pairs={{0,64},{1,65},{2,66},{3,67},{4,68},{5,69},{6,70},{7,71},{8,72},{9,... | collective-permute-start | bytes 786440 | tf_op jit(solution)/shard_map/ppermute | solution.py:38
  66.5 4.5 %collective-permute-start.7 = (f32[64,256]{1,0:T(8,128)}, f32[64,256]{1,0:T(8,128)S(1)}, u32[]{:S(2)}, u32[]{:S(2)}) collective-permute-start(f32[64,256]{1,0:T(8,128)} %shard_map.69.t0.t1), channel_id=1, source_target_pairs={{0,16},{1,17},{2,18},{3,19},{4,20},{5,21},{6,22},{7,23},{8,24},{9,... | collective-permute-start | bytes 196616 | tf_op jit(solution)/shard_map/ppermute | solution.py:38
  67.7 4.9 %collective-permute-start.8 = (f32[64,256]{1,0:T(8,128)}, f32[64,256]{1,0:T(8,128)S(1)}, u32[]{:S(2)}, u32[]{:S(2)}) collective-permute-start(f32[64,256]{1,0:T(8,128)} %shard_map.69.t0.t1), channel_id=1, source_target_pairs={{0,32},{1,33},{2,34},{3,35},{4,36},{5,37},{6,38},{7,39},{8,40},{9,... | collective-permute-start | bytes 196616 | tf_op jit(solution)/shard_map/ppermute | solution.py:38
  68.4 4.8 %collective-permute-start.9 = (f32[64,256]{1,0:T(8,128)}, f32[64,256]{1,0:T(8,128)S(1)}, u32[]{:S(2)}, u32[]{:S(2)}) collective-permute-start(f32[64,256]{1,0:T(8,128)} %shard_map.69.t0.t1), channel_id=1, source_target_pairs={{0,48},{1,49},{2,50},{3,51},{4,52},{5,53},{6,54},{7,55},{8,56},{9,... | collective-permute-start | bytes 196616 | tf_op jit(solution)/shard_map/ppermute | solution.py:38
  78.3 13.6 %collective-permute-start.19 = (f32[64,256]{1,0:T(8,128)}, f32[64,256]{1,0:T(8,128)S(1)}, u32[]{:S(2)}, u32[]{:S(2)}) collective-permute-start(f32[64,256]{1,0:T(8,128)} %get-tuple-element.9.refs_0_), channel_id=1, source_target_pairs={{0,2},{1,3},{2,4},{3,5},{4,6},{5,7},{6,8},{7,9},{8,10},{9,11},{10,... | collective-permute-start | bytes 196616 | tf_op jit(solution)/shard_map/ppermute | solution.py:38
  80.4 14.0 %collective-permute-start.20 = (f32[64,256]{1,0:T(8,128)}, f32[64,256]{1,0:T(8,128)S(1)}, u32[]{:S(2)}, u32[]{:S(2)}) collective-permute-start(f32[64,256]{1,0:T(8,128)} %get-tuple-element.9.refs_0_), channel_id=1, source_target_pairs={{0,4},{1,5},{2,6},{3,7},{4,8},{5,9},{6,10},{7,11},{8,12},{9,13},{1... | collective-permute-start | bytes 196616 | tf_op jit(solution)/shard_map/ppermute | solution.py:38
  83.4 12.1 %collective-permute-start.21 = (f32[64,256]{1,0:T(8,128)}, f32[64,256]{1,0:T(8,128)S(1)}, u32[]{:S(2)}, u32[]{:S(2)}) collective-permute-start(f32[64,256]{1,0:T(8,128)} %get-tuple-element.9.refs_0_), channel_id=1, source_target_pairs={{0,6},{1,7},{2,8},{3,9},{4,10},{5,11},{6,12},{7,13},{8,14},{9,15},... | collective-permute-start | bytes 196616 | tf_op jit(solution)/shard_map/ppermute | solution.py:38
  87.0 13.5 %collective-permute-start.22 = (f32[64,256]{1,0:T(8,128)}, f32[64,256]{1,0:T(8,128)S(1)}, u32[]{:S(2)}, u32[]{:S(2)}) collective-permute-start(f32[64,256]{1,0:T(8,128)} %get-tuple-element.9.refs_0_), channel_id=1, source_target_pairs={{0,8},{1,9},{2,10},{3,11},{4,12},{5,13},{6,14},{7,15},{8,0},{9,1},... | collective-permute-start | bytes 196616 | tf_op jit(solution)/shard_map/ppermute | solution.py:38
  87.4 14.5 %collective-permute-start.23 = (f32[64,256]{1,0:T(8,128)}, f32[64,256]{1,0:T(8,128)S(1)}, u32[]{:S(2)}, u32[]{:S(2)}) collective-permute-start(f32[64,256]{1,0:T(8,128)} %get-tuple-element.9.refs_0_), channel_id=1, source_target_pairs={{0,10},{1,11},{2,12},{3,13},{4,14},{5,15},{6,0},{7,1},{8,2},{9,3},... | collective-permute-start | bytes 196616 | tf_op jit(solution)/shard_map/ppermute | solution.py:38
  91.9 14.2 %copy-start.19 = (f32[64,256]{1,0:T(8,128)}, f32[64,256]{1,0:T(8,128)S(1)}, u32[]{:S(2)}) copy-start(f32[64,256]{1,0:T(8,128)S(1)} %collective-permute-done.19.refs_1_) | copy-start | bytes 196612
  91.9 11.7 %collective-permute-start.24 = (f32[64,256]{1,0:T(8,128)}, f32[64,256]{1,0:T(8,128)S(1)}, u32[]{:S(2)}, u32[]{:S(2)}) collective-permute-start(f32[64,256]{1,0:T(8,128)} %get-tuple-element.9.refs_0_), channel_id=1, source_target_pairs={{0,12},{1,13},{2,14},{3,15},{4,0},{5,1},{6,2},{7,3},{8,4},{9,5},{1... | collective-permute-start | bytes 196616 | tf_op jit(solution)/shard_map/ppermute | solution.py:38
  94.4 11.7 %copy-start.20 = (f32[64,256]{1,0:T(8,128)}, f32[64,256]{1,0:T(8,128)S(1)}, u32[]{:S(2)}) copy-start(f32[64,256]{1,0:T(8,128)S(1)} %collective-permute-done.20.refs_2_) | copy-start | bytes 196612
  94.4 11.7 %collective-permute-start.25 = (f32[64,256]{1,0:T(8,128)}, f32[64,256]{1,0:T(8,128)S(1)}, u32[]{:S(2)}, u32[]{:S(2)}) collective-permute-start(f32[64,256]{1,0:T(8,128)} %get-tuple-element.9.refs_0_), channel_id=1, source_target_pairs={{0,14},{1,15},{2,0},{3,1},{4,2},{5,3},{6,4},{7,5},{8,6},{9,7},{10,... | collective-permute-start | bytes 196616 | tf_op jit(solution)/shard_map/ppermute | solution.py:38
  95.5 10.7 %copy-start.21 = (f32[64,256]{1,0:T(8,128)}, f32[64,256]{1,0:T(8,128)S(1)}, u32[]{:S(2)}) copy-start(f32[64,256]{1,0:T(8,128)S(1)} %collective-permute-done.21.refs_3_) | copy-start | bytes 196612
  95.5 18.6 %collective-permute-start.4 = (f32[64,1024]{1,0:T(8,128)S(1)}, f32[64,1024]{1,0:T(8,128)S(1)}, u32[]{:S(2)}, u32[]{:S(2)}) collective-permute-start(f32[64,1024]{1,0:T(8,128)S(1)} %constant_dynamic-slice_fusion.3), channel_id=1, source_target_pairs={{0,128},{1,129},{2,130},{3,131},{4,132},{5,133},{6,134},{7,135},{8... | collective-permute-start | bytes 786440 | tf_op jit(solution)/shard_map/ppermute | solution.py:38
  100.6 5.6 %copy-start.22 = (f32[64,256]{1,0:T(8,128)}, f32[64,256]{1,0:T(8,128)S(1)}, u32[]{:S(2)}) copy-start(f32[64,256]{1,0:T(8,128)S(1)} %collective-permute-done.22.refs_4_) | copy-start | bytes 196612
  100.6 20.9 %collective-permute-start.5 = (f32[64,1024]{1,0:T(8,128)S(1)}, f32[64,1024]{1,0:T(8,128)S(1)}, u32[]{:S(2)}, u32[]{:S(2)}) collective-permute-start(f32[64,1024]{1,0:T(8,128)S(1)} %constant_dynamic-slice_fusion.3), channel_id=1, source_target_pairs={{0,192},{1,193},{2,194},{3,195},{4,196},{5,197},{6,198},{7,199},{8... | collective-permute-start | bytes 786440 | tf_op jit(solution)/shard_map/ppermute | solution.py:38
  101.9 19.5 %collective-permute-start.10 = (f32[64,1024]{1,0:T(8,128)}, f32[64,1024]{1,0:T(8,128)S(1)}, u32[]{:S(2)}, u32[]{:S(2)}) collective-permute-start(f32[64,1024]{1,0:T(8,128)} %get-tuple-element.8), channel_id=1, source_target_pairs={{0,64},{1,65},{2,66},{3,67},{4,68},{5,69},{6,70},{7,71},{8,72},{9,... | collective-permute-start | bytes 786440 | tf_op jit(solution)/shard_map/ppermute | solution.py:38
  103.6 22.3 %collective-permute-start.11 = (f32[64,1024]{1,0:T(8,128)}, f32[64,1024]{1,0:T(8,128)S(1)}, u32[]{:S(2)}, u32[]{:S(2)}) collective-permute-start(f32[64,1024]{1,0:T(8,128)} %get-tuple-element.8), channel_id=1, source_target_pairs={{0,128},{1,129},{2,130},{3,131},{4,132},{5,133},{6,134},{7,135},{8... | collective-permute-start | bytes 786440 | tf_op jit(solution)/shard_map/ppermute | solution.py:38
  108.8 41.0 %collective-permute-start.26 = (f32[8,64,256]{2,1,0:T(8,128)}, f32[8,64,256]{2,1,0:T(8,128)S(1)}, u32[]{:S(2)}, u32[]{:S(2)}) collective-permute-start(f32[8,64,256]{2,1,0:T(8,128)} %shard_map.72.refs_9_.refs_1_), channel_id=1, source_target_pairs={{0,1},{1,0},{2,3},{3,2},{4,5},{5,4},{6,7},{7,6},{8,9},{9,8},{10,11... | collective-permute-start | bytes 1572872 | tf_op jit(solution)/shard_map/ppermute | solution.py:38
  114.1 11.8 %copy-start.4 = (f32[64,1024]{1,0:T(8,128)}, f32[64,1024]{1,0:T(8,128)S(1)}, u32[]{:S(2)}) copy-start(f32[64,1024]{1,0:T(8,128)S(1)} %collective-permute-done.4.s2) | copy-start | bytes 786436
  121.4 4.5 %copy-start.5 = (f32[64,1024]{1,0:T(8,128)}, f32[64,1024]{1,0:T(8,128)S(1)}, u32[]{:S(2)}) copy-start(f32[64,1024]{1,0:T(8,128)S(1)} %collective-permute-done.5.s3) | copy-start | bytes 786436
  121.4 4.5 %copy-start.6 = (f32[64,1024]{1,0:T(8,128)}, f32[64,1024]{1,0:T(8,128)S(1)}, u32[]{:S(2)}) copy-start(f32[64,1024]{1,0:T(8,128)S(1)} %collective-permute-done.10.m1) | copy-start | bytes 786436
  130.3 25.1 %copy-start.2 = (bf16[1024,1024]{1,0:T(8,128)(2,1)S(1)}, bf16[1024,1024]{1,0:T(8,128)(2,1)}, u32[]{:S(2)}) copy-start(bf16[1024,1024]{1,0:T(8,128)(2,1)} %cand_ref.1) | copy-start | bytes 6291460
  130.3 26.6 %copy-start.26 = (f32[256]{0:T(256)S(1)}, f32[256]{0:T(256)}, u32[]{:S(2)}) copy-start(f32[256]{0:T(256)} %param.9) | copy-start | bytes 3076
  130.3 5.2 %collective-permute-start.12 = (f32[128,256]{1,0:T(8,128)}, f32[128,256]{1,0:T(8,128)S(1)}, u32[]{:S(2)}, u32[]{:S(2)}) collective-permute-start(f32[128,256]{1,0:T(8,128)} %shard_map.71.refs_0_), channel_id=1, source_target_pairs={{0,16},{1,17},{2,18},{3,19},{4,20},{5,21},{6,22},{7,23},{8,24},{9,... | collective-permute-start | bytes 393224 | tf_op jit(solution)/shard_map/ppermute | solution.py:38
  131.1 10.5 %collective-permute-start.13 = (f32[128,256]{1,0:T(8,128)}, f32[128,256]{1,0:T(8,128)S(1)}, u32[]{:S(2)}, u32[]{:S(2)}) collective-permute-start(f32[128,256]{1,0:T(8,128)} %shard_map.71.refs_0_), channel_id=1, source_target_pairs={{0,32},{1,33},{2,34},{3,35},{4,36},{5,37},{6,38},{7,39},{8,40},{9,... | collective-permute-start | bytes 393224 | tf_op jit(solution)/shard_map/ppermute | solution.py:38
  133.2 11.0 %collective-permute-start.14 = (f32[128,256]{1,0:T(8,128)}, f32[128,256]{1,0:T(8,128)S(1)}, u32[]{:S(2)}, u32[]{:S(2)}) collective-permute-start(f32[128,256]{1,0:T(8,128)} %shard_map.71.refs_0_), channel_id=1, source_target_pairs={{0,48},{1,49},{2,50},{3,51},{4,52},{5,53},{6,54},{7,55},{8,56},{9,... | collective-permute-start | bytes 393224 | tf_op jit(solution)/shard_map/ppermute | solution.py:38
  133.6 14.0 %collective-permute-start.15 = (f32[128,256]{1,0:T(8,128)}, f32[128,256]{1,0:T(8,128)S(1)}, u32[]{:S(2)}, u32[]{:S(2)}) collective-permute-start(f32[128,256]{1,0:T(8,128)} %shard_map.71.refs_0_), channel_id=1, source_target_pairs={{0,64},{1,65},{2,66},{3,67},{4,68},{5,69},{6,70},{7,71},{8,72},{9,... | collective-permute-start | bytes 393224 | tf_op jit(solution)/shard_map/ppermute | solution.py:38
  135.5 14.3 %copy-start.9 = (f32[128,256]{1,0:T(8,128)}, f32[128,256]{1,0:T(8,128)S(1)}, u32[]{:S(2)}) copy-start(f32[128,256]{1,0:T(8,128)S(1)} %collective-permute-done.12.refs_1_) | copy-start | bytes 393220
  135.6 12.1 %collective-permute-start.16 = (f32[128,256]{1,0:T(8,128)}, f32[128,256]{1,0:T(8,128)S(1)}, u32[]{:S(2)}, u32[]{:S(2)}) collective-permute-start(f32[128,256]{1,0:T(8,128)} %shard_map.71.refs_0_), channel_id=1, source_target_pairs={{0,80},{1,81},{2,82},{3,83},{4,84},{5,85},{6,86},{7,87},{8,88},{9,... | collective-permute-start | bytes 393224 | tf_op jit(solution)/shard_map/ppermute | solution.py:38
  141.6 8.2 %copy-start.10 = (f32[128,256]{1,0:T(8,128)}, f32[128,256]{1,0:T(8,128)S(1)}, u32[]{:S(2)}) copy-start(f32[128,256]{1,0:T(8,128)S(1)} %collective-permute-done.13.refs_2_) | copy-start | bytes 393220
  141.6 6.0 %collective-permute-start.17 = (f32[128,256]{1,0:T(8,128)}, f32[128,256]{1,0:T(8,128)S(1)}, u32[]{:S(2)}, u32[]{:S(2)}) collective-permute-start(f32[128,256]{1,0:T(8,128)} %shard_map.71.refs_0_), channel_id=1, source_target_pairs={{0,96},{1,97},{2,98},{3,99},{4,100},{5,101},{6,102},{7,103},{8,104... | collective-permute-start | bytes 393224 | tf_op jit(solution)/shard_map/ppermute | solution.py:38
  144.2 5.7 %copy-start.11 = (f32[128,256]{1,0:T(8,128)}, f32[128,256]{1,0:T(8,128)S(1)}, u32[]{:S(2)}) copy-start(f32[128,256]{1,0:T(8,128)S(1)} %collective-permute-done.14.refs_3_) | copy-start | bytes 393220
  144.2 5.7 %collective-permute-start.18 = (f32[128,256]{1,0:T(8,128)}, f32[128,256]{1,0:T(8,128)S(1)}, u32[]{:S(2)}, u32[]{:S(2)}) collective-permute-start(f32[128,256]{1,0:T(8,128)} %shard_map.71.refs_0_), channel_id=1, source_target_pairs={{0,112},{1,113},{2,114},{3,115},{4,116},{5,117},{6,118},{7,119},{8... | collective-permute-start | bytes 393224 | tf_op jit(solution)/shard_map/ppermute | solution.py:38
  207.8 4.8 %collective-permute-start.27 = (f32[1,1024]{1,0:T(1,128)}, f32[1,1024]{1,0:T(1,128)S(1)}, u32[]{:S(2)}, u32[]{:S(2)}) collective-permute-start(f32[1,1024]{1,0:T(1,128)} %get-tuple-element.13), channel_id=1, source_target_pairs={{0,16},{1,17},{2,18},{3,19},{4,20},{5,21},{6,22},{7,23},{8,24},{9,... | collective-permute-start | bytes 12296 | tf_op jit(solution)/shard_map/ppermute | solution.py:38
  209.1 4.2 %collective-permute-start.28 = (f32[1,1024]{1,0:T(1,128)}, f32[1,1024]{1,0:T(1,128)S(1)}, u32[]{:S(2)}, u32[]{:S(2)}) collective-permute-start(f32[1,1024]{1,0:T(1,128)} %get-tuple-element.13), channel_id=1, source_target_pairs={{0,32},{1,33},{2,34},{3,35},{4,36},{5,37},{6,38},{7,39},{8,40},{9,... | collective-permute-start | bytes 12296 | tf_op jit(solution)/shard_map/ppermute | solution.py:38
  211.5 3.0 %collective-permute-start.29 = (f32[1,1024]{1,0:T(1,128)}, f32[1,1024]{1,0:T(1,128)S(1)}, u32[]{:S(2)}, u32[]{:S(2)}) collective-permute-start(f32[1,1024]{1,0:T(1,128)} %get-tuple-element.13), channel_id=1, source_target_pairs={{0,48},{1,49},{2,50},{3,51},{4,52},{5,53},{6,54},{7,55},{8,56},{9,... | collective-permute-start | bytes 12296 | tf_op jit(solution)/shard_map/ppermute | solution.py:38
  215.2 4.8 %collective-permute-start.30 = (f32[1,1024]{1,0:T(1,128)S(1)}, f32[1,1024]{1,0:T(1,128)S(1)}, u32[]{:S(2)}, u32[]{:S(2)}) collective-permute-start(f32[1,1024]{1,0:T(1,128)S(1)} %add_add_fusion.1), channel_id=1, source_target_pairs={{0,64},{1,65},{2,66},{3,67},{4,68},{5,69},{6,70},{7,71},{8,72},{9,... | collective-permute-start | bytes 12296 | tf_op jit(solution)/shard_map/ppermute | solution.py:38
  216.4 4.0 %collective-permute-start.31 = (f32[1,1024]{1,0:T(1,128)S(1)}, f32[1,1024]{1,0:T(1,128)S(1)}, u32[]{:S(2)}, u32[]{:S(2)}) collective-permute-start(f32[1,1024]{1,0:T(1,128)S(1)} %add_add_fusion.1), channel_id=1, source_target_pairs={{0,128},{1,129},{2,130},{3,131},{4,132},{5,133},{6,134},{7,135},{8... | collective-permute-start | bytes 12296 | tf_op jit(solution)/shard_map/ppermute | solution.py:38
  218.8 2.5 %collective-permute-start.32 = (f32[1,1024]{1,0:T(1,128)S(1)}, f32[1,1024]{1,0:T(1,128)S(1)}, u32[]{:S(2)}, u32[]{:S(2)}) collective-permute-start(f32[1,1024]{1,0:T(1,128)S(1)} %add_add_fusion.1), channel_id=1, source_target_pairs={{0,192},{1,193},{2,194},{3,195},{4,196},{5,197},{6,198},{7,199},{8... | collective-permute-start | bytes 12296 | tf_op jit(solution)/shard_map/ppermute | solution.py:38
  (14 other events, 21.5 us)
Sparse Core Ops, SparseCore 0:
  11.7 126.9 all-gather.3
  155.5 42.4 all-gather.5

commit v3 on v2

--- a/solution.py
+++ b/solution.py
@@ -6,14 +6,16 @@
 from jax import lax
 from jax.experimental import pallas as pl
 from jax.experimental.pallas import tpu as pltpu
+from jax.sharding import Mesh
 from jax.sharding import PartitionSpec as P
 
 EPS = 1e-06
 BF16 = jnp.bfloat16
 F32 = jnp.float32
-AXES = ("chain", "group")
+AXES = ("chain", "z", "c")
 SIDE = 4
 ZS = 8
+CHAIN = SIDE * SIDE
 VMEM = pl.BlockSpec(memory_space=pltpu.VMEM)
 SMEM = pl.BlockSpec(memory_space=pltpu.SMEM)
 PARAMS = pltpu.CompilerParams(vmem_limit_bytes=56 * 1024 * 1024)
@@ -44,10 +46,6 @@
 
 def x_ring(value):
     return [value] + [send(value, lambda y, x, z, c: (y, (x + k) % SIDE, z, c)) for k in (1, 2, 3)]
-
-
-def y_ring(value):
-    return [value] + [send(value, lambda y, x, z, c: ((y + k) % SIDE, x, z, c)) for k in (1, 2, 3)]
 
 
 def hop(value, dy, dx=0):
@@ -159,7 +157,10 @@
     bs = t0.shape[1]
     for k, ref in enumerate((t0, t1, t2, t3)):
         t[:, spot(k, x, bs)] = ref[...]
-    out_ref[...] = -mul3(split(t[...]), split(st[...]), NN)
+    th, tl = split(t[...])
+    for i in range(SIDE):
+        rows, columns = (i + 1) * bs, slice(i * bs, (i + 1) * bs)
+        out_ref[:, columns] = -mul3((th[:, :rows], tl[:, :rows]), split(st[:rows, columns]), NN)
     own_ref[...] = out_ref[:, spot(0, x, bs)]
 
 
@@ -202,30 +203,22 @@
     )(place, *args, factor)
 
 
-def interleave(full, mine, other, c):
-    m = full.shape[0] // (2 * ZS)
-    for z in range(ZS):
-        full[pl.ds(pl.multiple_of((2 * z + c) * m, m), m), :] = mine[z]
-        full[pl.ds(pl.multiple_of((2 * z + 1 - c) * m, m), m), :] = other[z]
-
-
 def second_inverse_kernel(place, *refs):
-    ts, qs, (st, ma, mb, out_ref, t, q, full) = refs[:SIDE], refs[SIDE : 2 * SIDE], refs[2 * SIDE :]
-    x, c, y = place[0], place[1], place[3]
+    ts, qs, (st, below_ref, out_ref, t, q) = refs[:SIDE], refs[SIDE : 2 * SIDE], refs[2 * SIDE :]
+    x, y = place[0], place[3]
     m, bs = ts[0].shape
     for k in range(SIDE):
         t[:, spot(k, x, bs)] = ts[k][...]
         q[:, spot(k, x, bs)] = qs[k][...]
-    interleave(full, ma, mb, c)
     total = mul3(split(t[...]), split(st[...]), NN)
-    below = mul3(split(q[...]), split(full[...]), NN)
+    below = mul3(split(q[...]), split(below_ref[...]), NN)
     total = total + jnp.where(y == 3, below, 0.0)
     half = m // 2
     out_ref[:half] = jnp.where(y >= 2, -total[:half], 0.0)
     out_ref[half:] = jnp.where(y == 3, -total[half:], 0.0)
 
 
-def second_inverse(place, ts, qs, st, ma, mb):
+def second_inverse(place, ts, qs, st, below):
     m, bs = ts[0].shape
     size = SIDE * bs
     fixed = lambda a: pl.BlockSpec(a.shape, lambda i, p: (0,) * a.ndim)
@@ -235,13 +228,13 @@
             num_scalar_prefetch=1,
             grid=(1,),
             in_specs=[fixed(a) for a in (*ts, *qs)]
-            + [pl.BlockSpec((size, bs), lambda i, p: (0, p[0])), fixed(ma), fixed(mb)],
+            + [pl.BlockSpec((size, bs), lambda i, p: (0, p[0])), fixed(below)],
             out_specs=pl.BlockSpec((m, bs), lambda i, p: (0, 0)),
-            scratch_shapes=[pltpu.VMEM((m, size), F32)] * 2 + [pltpu.VMEM((size, bs), F32)],
+            scratch_shapes=[pltpu.VMEM((m, size), F32)] * 2,
         ),
         out_shape=jax.ShapeDtypeStruct((m, bs), F32),
         compiler_params=PARAMS,
-    )(place, *ts, *qs, st, ma, mb)
+    )(place, *ts, *qs, st, below)
 
 
 def panel_kernel(beta, train_ref, cand_ref, scale_ref, hi_ref, lo_ref):
@@ -275,32 +268,11 @@
     )(train, cand, cand_scale)
 
 
-def arrange_kernel(place, *refs):
-    z = place[2]
-    out = refs[-1]
-    for k in range(ZS):
-        out[lax.rem(z - k + ZS, ZS)] = refs[k][...]
-
-
-def z_gather(place, own):
-    parts = [own]
-    for k in range(1, ZS):
-        parts.append(send(own, lambda y, x, z, c: (y, x, (z + k) % ZS, c)))
-    mine = pl.pallas_call(
-        arrange_kernel,
-        in_specs=[SMEM] + [VMEM] * ZS,
-        out_specs=VMEM,
-        out_shape=jax.ShapeDtypeStruct((ZS,) + own.shape, own.dtype),
-        compiler_params=PARAMS,
-    )(place, *parts)
-    return mine, swap_core(mine)
-
-
 def apply_kernel(last, sup, place, *refs):
     if last:
         m2, win, h0, l0, h1, l1, targets, out, mean, full, mh, ml = refs
     else:
-        st, mine, other, h0, l0, h1, l1, out, full, mh, ml = refs
+        st, m1, h0, l0, h1, l1, out, full, mh, ml = refs
     size = full.shape[0]
 
     @pl.when(pl.program_id(0) == 0)
@@ -314,7 +286,7 @@
                 full[g * m : (g + 1) * m] = m2[g, m:]
         else:
             mh[:size], ml[:size] = split(st[...])
-            interleave(full, mine, other, place[1])
+            full[...] = m1[...]
         mh[size:], ml[size:] = split(full[...])
 
     w = mul3((h0[0], l0[0]), (mh[:size], ml[:size]), NN)
@@ -362,13 +334,22 @@
     )(sup, place, *args)
 
 
+def z_gather(z, c, own):
+    m, bs = own.shape
+    parts = [own] + [send(own, lambda y, x, z, c: (y, x, (z - k) % ZS, c)) for k in range(1, ZS)]
+    mine = jnp.stack(parts)
+    other = swap_core(mine)
+    even = c == 0
+    both = jnp.stack([jnp.where(even, mine, other), jnp.where(even, other, mine)], 1)
+    return jnp.roll(both, z, axis=0).reshape(2 * ZS * m, bs)
+
+
 def shards(train_emb, cand_emb, factor, diag_inverse, targets):
     bs = diag_inverse.shape[1]
     n = cand_emb.shape[0]
     size = SIDE * bs
-    p = lax.axis_index("chain")
-    group = lax.axis_index("group")
-    y, x, z, c = p // SIDE, p % SIDE, group // 2, group % 2
+    p, z, c = (lax.axis_index(axis) for axis in AXES)
+    y, x, group = p // SIDE, p % SIDE, 2 * z + c
     place = jnp.stack([x, c, z, y]).astype(jnp.int32)
 
     train = lax.all_gather(train_emb, AXES, axis=0, tiled=True)
@@ -385,31 +366,33 @@
     m = size // (2 * ZS)
     sl = lax.dynamic_slice(st, (group * m, 0), (m, size))
     t1 = first_factor(place, hop(sl, 1), factor)
+    t1, s2, s3 = lax.optimization_barrier((t1, hop(sl, 2), hop(sl, 3)))
     m1, m1_own = first_inverse(place, x_ring(t1), st)
-    t2 = second_factor(place, hop(sl, 2), hop(sl, 3), hop(m1, 1), hop(m1, 2), t1, factor)
-    m1_full = z_gather(place, m1_own)
-    m2 = second_inverse(place, x_ring(t2), [hop(t2, 1, k) for k in range(SIDE)], st, *m1_full)
-    m2_full = lax.all_gather(m2, "group", axis=0)
-
+    t2 = second_factor(place, s2, s3, hop(m1, 1), hop(m1, 2), t1, factor)
+    m1_full = z_gather(z, c, m1_own)
+    m2 = second_inverse(place, x_ring(t2), [hop(t2, 1, k) for k in range(SIDE)], st, m1_full)
+    m2_full = lax.all_gather(m2, ("z", "c"), axis=0)
+
+    train, _ = lax.optimization_barrier((train, m2))
     cand_f = cand_emb.astype(F32)
     cand_scale = lax.rsqrt(jnp.sum(cand_f * cand_f, axis=1, keepdims=True) + EPS)
     panel = make_panel(train, cand_emb, cand_scale, size)
     sup = jnp.stack([y, jnp.maximum(y - 1, 0)]).astype(jnp.int32)
-    (w,) = apply(sup, place, (st, *m1_full), panel, bs)
+    (w,) = apply(sup, place, (st, m1_full), panel, bs)
     w, mean = apply(jnp.arange(2, dtype=jnp.int32), place, (m2_full, w), panel, bs, targets.reshape(bs, 1))
-    for ring in (x_ring, y_ring):
-        a, b, d, e = ring(mean)
-        mean = (a + b) + (d + e)
-    return w, mean.reshape(n)
+    parts = lax.all_to_all(jnp.broadcast_to(mean, (CHAIN, n)), "chain", 0, 0, tiled=True)
+    return w, jnp.sum(parts, axis=0)
 
 
 def solution(mesh):
+    fine = Mesh(mesh.devices.reshape(CHAIN, ZS, 2), AXES)
+    group = ("z", "c")
     in_specs = (
-        P(("chain", "group"), None),
-        P("group", None),
+        P(AXES, None),
+        P(group, None),
         P("chain", None),
         P("chain", None),
         P("chain"),
     )
-    out_specs = (P("chain", "group"), P("group"))
-    return jax.shard_map(shards, mesh=mesh, in_specs=in_specs, out_specs=out_specs, check_vma=False)
+    out_specs = (P("chain", group), P(group))
+    return jax.shard_map(shards, mesh=fine, in_specs=in_specs, out_specs=out_specs, check_vma=False)

time: 231 us -> 233 us (level)
  blocking collectives: 0 us -> 12.8 us
  starting transfers between devices: 71.3 us -> 62.5 us
  Pallas kernels: 60.9 us -> 58.5 us
    all_to_all x0 -> x1, blocking collectives: none -> 12.8 us  [shards(): lax.all_to_all(jnp.broadcast_to(mean, (CHAIN, n)), 'chain', 0, 0, tiled=T...]
    ppermute x33 -> x27, starting transfers between devices: 71.2 us -> 62.4 us  [send(): return lax.ppermute(value, AXES, moves(target))]
    ppermute x33 -> x27, waiting for transfers between devices: 51.9 us -> 55.1 us  [send(): return lax.ppermute(value, AXES, moves(target))]
    all_gather x1, waiting for transfers between devices: 13.2 us -> 10.7 us  [shards(): m2_full = lax.all_gather(m2, ('z', 'c'), axis=0)]
    unnamed x54 -> x47, local copies, waits for them, and re-layouts: 5.32 us -> 4.75 us
  transfers between devices with their start and end apart: 35 -> 29, of which waited for: 16 -> 15; matrix products, arithmetic and copies ran while one was open for 4% -> 5% of each run, Pallas kernels for 23% -> 21%
where the time goes in v3:
time: 233 us; the launch traced here: 232 us
  waiting for transfers between devices  66.5 us (29%)
  starting transfers between devices  62.5 us (27%)
  Pallas kernels  58.5 us (25%)
  between operations  14.4 us (6%)
  local copies, waits for them, and re-layouts  13.4 us (6%)
  blocking collectives  12.8 us (5%)
  other arithmetic  3.74 us (2%)
    ppermute x27, starting transfers between devices, send(): return lax.ppermute(value, AXES, moves(target))  62.4 us
    ppermute x27, waiting for transfers between devices, send(): return lax.ppermute(value, AXES, moves(target))  55.1 us
    pallas_call x2, Pallas kernels, apply(): pl.pallas_call(functools.partial(apply_kernel, last), grid_spec=pltpu.Pre...  18.1 us
    pallas_call x1, Pallas kernels, make_panel(): pl.pallas_call(functools.partial(panel_kernel, 0.5 * math.sqrt(e)), grid=...  17.5 us
    all_to_all x1, blocking collectives, shards(): lax.all_to_all(jnp.broadcast_to(mean, (CHAIN, n)), 'chain', 0, 0, tiled=T...  12.8 us
    all_gather x1, waiting for transfers between devices, shards(): m2_full = lax.all_gather(m2, ('z', 'c'), axis=0)  10.7 us
    pallas_call x1, Pallas kernels, diagonal(): pl.pallas_call(diagonal_kernel, in_specs=[SMEM] + [VMEM] * 4, out_specs=V...  7.79 us
    unnamed x47, local copies, waits for them, and re-layouts  4.75 us
  transfers between devices with their start and end apart: 29, of which 15 were waited for; matrix products, arithmetic and copies ran while one was open for 5% of the time, Pallas kernels for 21%

profile of v3, /device:TPU:1, one launch (start us, length us, event | category | flops | bytes accessed | tf_op | source)
XLA Modules:
  0.0 231.9 jit_solution(10974776559902099255)
XLA Ops:
  8.0 1.2 constant_dynamic-slice_fusion.1
  10.2 1.3 collective-permute-start
  11.5 1.3 collective-permute-start.1
  13.5 11.3 %collective-permute-done = f32[512,256]{1,0:T(8,128)S(1)} collective-permute-done((f32[512,256]{1,0:T(8,128)S(1)}, f32[512,256]{1,0:T(8,128)S(1)}, u32[]{:S(2)}, u32[]{:S(2)}) %collective-permute-start) | collective-permute-done | bytes 524320 | tf_op jit(solution)/shard_map/ppermute | solution.py:40
  24.7 14.6 %collective-permute-done.1 = f32[512,256]{1,0:T(8,128)S(1)} collective-permute-done((f32[512,256]{1,0:T(8,128)S(1)}, f32[512,256]{1,0:T(8,128)S(1)}, u32[]{:S(2)}, u32[]{:S(2)}) %collective-permute-start.1) | collective-permute-done | bytes 524320 | tf_op jit(solution)/shard_map/ppermute | solution.py:40
  39.5 1.6 collective-permute-start.3
  41.7 2.3 constant_dynamic-slice_fusion.4.f_ref
  44.2 1.1 copy-done.2
  45.3 7.8 %shard_map.68.st.refs_8_.refs_0_ = f32[1024,1024]{1,0:T(8,128)} custom-call(s32[4]{0:T(128)} %pad_add_fusion.place, f32[256,256]{1,0:T(8,128)} %d_ref.1, f32[256,1024]{1,0:T(8,128)} %constant_dynamic-slice_fusion.4.f_ref, f32[3,512,256]{2,1,0:T(8,128)} %copy-done, f32[3,512,256]{2,1,0:T(8,128)} %copy-done.2), custom_call_target="tpu_custom_call" | custom-call | tf_op jit(solution)/shard_map/pallas_call | solution.py:122
  54.1 3.2 %collective-permute-start.4 = (f32[64,1024]{1,0:T(8,128)S(1)}, f32[64,1024]{1,0:T(8,128)S(1)}, u32[]{:S(2)}, u32[]{:S(2)}) collective-permute-start(f32[64,1024]{1,0:T(8,128)S(1)} %constant_dynamic-slice_fusion.3), channel_id=1, source_target_pairs={{0,64},{1,65},{2,66},{3,67},{4,68},{5,69},{6,70},{7,71},{8,72},{9,... | collective-permute-start | bytes 786440 | tf_op jit(solution)/shard_map/ppermute | solution.py:40
  57.3 4.5 %collective-permute-start.5 = (f32[64,1024]{1,0:T(8,128)S(1)}, f32[64,1024]{1,0:T(8,128)S(1)}, u32[]{:S(2)}, u32[]{:S(2)}) collective-permute-start(f32[64,1024]{1,0:T(8,128)S(1)} %constant_dynamic-slice_fusion.3), channel_id=1, source_target_pairs={{0,128},{1,129},{2,130},{3,131},{4,132},{5,133},{6,134},{7,135},{8... | collective-permute-start | bytes 786440 | tf_op jit(solution)/shard_map/ppermute | solution.py:40
  61.8 1.3 collective-permute-start.6
  63.9 3.3 %shard_map.69.t0.t1 = f32[64,256]{1,0:T(8,128)} custom-call(s32[4]{0:T(128)} %pad_add_fusion.place, f32[64,1024]{1,0:T(8,128)} %copy-done.8, f32[256,4096]{1,0:T(8,128)} %f_ref.3), custom_call_target="tpu_custom_call" | custom-call | tf_op jit(solution)/shard_map/pallas_call | solution.py:139
  67.1 1.6 collective-permute-done.5.s2
  68.7 4.2 %collective-permute-done.6.s3 = f32[64,1024]{1,0:T(8,128)S(1)} collective-permute-done((f32[64,1024]{1,0:T(8,128)S(1)}, f32[64,1024]{1,0:T(8,128)S(1)}, u32[]{:S(2)}, u32[]{:S(2)}) %collective-permute-start.6) | collective-permute-done | bytes 262176 | tf_op jit(solution)/shard_map/ppermute | solution.py:40
  72.9 1.2 collective-permute-start.7
  74.8 2.1 collective-permute-start.9
  77.8 1.3 collective-permute-done.8.t2
  79.1 1.0 collective-permute-done.9.t3
  80.7 4.0 %shard_map.70 = (f32[64,1024]{1,0:T(8,128)}, f32[64,256]{1,0:T(8,128)}) custom-call(s32[4]{0:T(128)} %pad_add_fusion.place, f32[64,256]{1,0:T(8,128)} %shard_map.69.t0.t1, f32[64,256]{1,0:T(8,128)} %copy-done.16, f32[64,256]{1,0:T(8,128)} %copy-done.17, f32[64,256]{1,0:T(8,128)} %copy-done.18, f32[1024,1024]{1,0:T(8,128)} %shard_map.68.st.refs_8_.refs_0_), custom_call_target="tpu_custom_call" | custom-call | tf_op jit(solution)/shard_map/pallas_call | solution.py:170
  84.7 5.7 %collective-permute-start.19 = (f32[64,256]{1,0:T(8,128)}, f32[64,256]{1,0:T(8,128)S(1)}, u32[]{:S(2)}, u32[]{:S(2)}) collective-permute-start(f32[64,256]{1,0:T(8,128)} %get-tuple-element.16), channel_id=1, source_target_pairs={{0,14},{1,15},{2,0},{3,1},{4,2},{5,3},{6,4},{7,5},{8,6},{9,7},{10,... | collective-permute-start | bytes 196616 | tf_op jit(solution)/shard_map/ppermute | solution.py:40
  91.2 1.3 collective-permute-start.20
  93.0 4.4 %collective-permute-start.22 = (f32[64,256]{1,0:T(8,128)}, f32[64,256]{1,0:T(8,128)S(1)}, u32[]{:S(2)}, u32[]{:S(2)}) collective-permute-start(f32[64,256]{1,0:T(8,128)} %get-tuple-element.16), channel_id=1, source_target_pairs={{0,8},{1,9},{2,10},{3,11},{4,12},{5,13},{6,14},{7,15},{8,0},{9,1},... | collective-permute-start | bytes 196616 | tf_op jit(solution)/shard_map/ppermute | solution.py:40
  97.4 2.2 collective-permute-start.24
  99.6 1.5 collective-permute-start.25
  101.2 4.0 %collective-permute-done.23 = f32[64,256]{1,0:T(8,128)S(1)} collective-permute-done((f32[64,256]{1,0:T(8,128)}, f32[64,256]{1,0:T(8,128)S(1)}, u32[]{:S(2)}, u32[]{:S(2)}) %collective-permute-start.23) | collective-permute-done | bytes 65568 | tf_op jit(solution)/shard_map/ppermute | solution.py:40
  105.2 4.9 %collective-permute-done.24 = f32[64,256]{1,0:T(8,128)S(1)} collective-permute-done((f32[64,256]{1,0:T(8,128)}, f32[64,256]{1,0:T(8,128)S(1)}, u32[]{:S(2)}, u32[]{:S(2)}) %collective-permute-start.24) | collective-permute-done | bytes 65568 | tf_op jit(solution)/shard_map/ppermute | solution.py:40
  110.2 1.8 collective-permute-done.25
  112.0 3.3 %collective-permute-start.26 = (f32[8,64,256]{2,1,0:T(8,128)S(1)}, f32[8,64,256]{2,1,0:T(8,128)S(1)}, u32[]{:S(2)}, u32[]{:S(2)}) collective-permute-start(f32[8,64,256]{2,1,0:T(8,128)S(1)} %bitcast_dynamic-update-slice_fusion), channel_id=1, source_target_pairs={{0,1},{1,0},{2,3},{3,2},{4,5},{5,4},{6,7},{7,6},{8,9},{9,8},{10,11... | collective-permute-start | bytes 1572872 | tf_op jit(solution)/shard_map/ppermute | solution.py:40
  115.3 1.3 collective-permute-start.10
  116.6 7.4 %collective-permute-start.11 = (f32[64,1024]{1,0:T(8,128)}, f32[64,1024]{1,0:T(8,128)S(1)}, u32[]{:S(2)}, u32[]{:S(2)}) collective-permute-start(f32[64,1024]{1,0:T(8,128)} %get-tuple-element.15), channel_id=1, source_target_pairs={{0,128},{1,129},{2,130},{3,131},{4,132},{5,133},{6,134},{7,135},{8... | collective-permute-start | bytes 786440 | tf_op jit(solution)/shard_map/ppermute | solution.py:40
  124.1 2.0 collective-permute-done.10.m1
  126.1 5.6 %collective-permute-done.11.m2 = f32[64,1024]{1,0:T(8,128)S(1)} collective-permute-done((f32[64,1024]{1,0:T(8,128)}, f32[64,1024]{1,0:T(8,128)S(1)}, u32[]{:S(2)}, u32[]{:S(2)}) %collective-permute-start.11) | collective-permute-done | bytes 262176 | tf_op jit(solution)/shard_map/ppermute | solution.py:40
  132.4 3.7 %shard_map.71.refs_0_ = f32[128,256]{1,0:T(8,128)} custom-call(s32[4]{0:T(128)} %pad_add_fusion.place, f32[64,1024]{1,0:T(8,128)} %copy-done.4, f32[64,1024]{1,0:T(8,128)} %copy-done.5, f32[64,1024]{1,0:T(8,128)} %copy-done.6, f32[64,1024]{1,0:T(8,128)} %copy-done.7, f32[64,256]{1,0:T(8,128)} %shard_map.69.t0.t1, f32[256,4096]{1,0:T(8,128)} %f_ref.3), custom_call_target="tpu_custom_call" | custom-call | tf_op jit(solution)/shard_map/pallas_call | solution.py:194
  136.4 2.4 %collective-permute-start.13 = (f32[128,256]{1,0:T(8,128)}, f32[128,256]{1,0:T(8,128)S(1)}, u32[]{:S(2)}, u32[]{:S(2)}) collective-permute-start(f32[128,256]{1,0:T(8,128)} %shard_map.71.refs_0_), channel_id=1, source_target_pairs={{0,32},{1,33},{2,34},{3,35},{4,36},{5,37},{6,38},{7,39},{8,40},{9,... | collective-permute-start | bytes 393224 | tf_op jit(solution)/shard_map/ppermute | solution.py:40
  138.9 1.3 collective-permute-start.15
  140.2 6.9 %collective-permute-start.16 = (f32[128,256]{1,0:T(8,128)}, f32[128,256]{1,0:T(8,128)S(1)}, u32[]{:S(2)}, u32[]{:S(2)}) collective-permute-start(f32[128,256]{1,0:T(8,128)} %shard_map.71.refs_0_), channel_id=1, source_target_pairs={{0,80},{1,81},{2,82},{3,83},{4,84},{5,85},{6,86},{7,87},{8,88},{9,... | collective-permute-start | bytes 393224 | tf_op jit(solution)/shard_map/ppermute | solution.py:40
  147.3 2.8 %collective-permute-start.17 = (f32[128,256]{1,0:T(8,128)S(1)}, f32[128,256]{1,0:T(8,128)S(1)}, u32[]{:S(2)}, u32[]{:S(2)}) collective-permute-start(f32[128,256]{1,0:T(8,128)S(1)} %copy-done.3), channel_id=1, source_target_pairs={{0,96},{1,97},{2,98},{3,99},{4,100},{5,101},{6,102},{7,103},{8,104... | collective-permute-start | bytes 393224 | tf_op jit(solution)/shard_map/ppermute | solution.py:40
  150.1 3.2 %collective-permute-start.18 = (f32[128,256]{1,0:T(8,128)S(1)}, f32[128,256]{1,0:T(8,128)S(1)}, u32[]{:S(2)}, u32[]{:S(2)}) collective-permute-start(f32[128,256]{1,0:T(8,128)S(1)} %copy-done.3), channel_id=1, source_target_pairs={{0,112},{1,113},{2,114},{3,115},{4,116},{5,117},{6,118},{7,119},{8... | collective-permute-start | bytes 393224 | tf_op jit(solution)/shard_map/ppermute | solution.py:40
  153.5 1.1 copy.14
  154.6 1.6 collective-permute-done.18.refs_7_
  156.8 4.2 %shard_map.72 = f32[128,256]{1,0:T(8,128)} custom-call(s32[4]{0:T(128)} %pad_add_fusion.place, f32[128,256]{1,0:T(8,128)} %shard_map.71.refs_0_, f32[128,256]{1,0:T(8,128)} %copy-done.9, f32[128,256]{1,0:T(8,128)} %copy-done.10, f32[128,256]{1,0:T(8,128)} %copy-done.11, f32[128,256]{1,0:T(8,128)} %copy-done.12, f32[128,256]{1,0:T(8,128)} %copy-done.13, ...), custom_call_target="tpu_custom_call" | custom-call | tf_op jit(solution)/shard_map/pallas_call | solution.py:225
  161.6 1.0 copy.15.scale_ref
  164.0 17.5 %shard_map.73 = (bf16[4,1024,1024]{2,1,0:T(8,128)(2,1)}, bf16[4,1024,1024]{2,1,0:T(8,128)(2,1)}) custom-call(bf16[4096,1024]{1,0:T(8,128)(2,1)} %all-gather.4.cloned.1.call-done.train_ref, bf16[1024,1024]{1,0:T(8,128)(2,1)} %cand_ref.1, f32[1024,1]{1,0:T(8,128)} %copy.15.scale_ref), custom_call_target="tpu_custom_call" | custom-call | flops 17179869184 | bytes 25165824 | tf_op jit(solution)/shard_map/pallas_call | solution.py:256
  181.5 8.8 %shard_map.74.refs_1_ = f32[1024,256]{1,0:T(8,128)} custom-call(s32[2]{0:T(128)} %pad_add_fusion.1.sup, s32[4]{0:T(128)} %pad_add_fusion.place, f32[1024,1024]{1,0:T(8,128)} %shard_map.68.st.refs_8_.refs_0_, f32[1024,256]{1,0:T(8,128)} %bitcast.34, bf16[4,1024,1024]{2,1,0:T(8,128)(2,1)} %get-tuple-element.18.refs_2_.refs_4_, ...), custom_call_target="tpu_custom_call" | custom-call | flops 6442450944 | bytes 8388608 | tf_op jit(solution)/shard_map/pallas_call | solution.py:322
  190.3 10.7 %all-gather.6.cloned.1.call-done = f32[2048,256]{1,0:T(8,128)} async-done(((f32[128,256]{1,0:T(8,128)}), f32[2048,256]{1,0:T(8,128)}) %all-gather.6.cloned.1.call-update) | async-done | bytes 2097168 | tf_op jit(solution)/shard_map/all_gather | solution.py:374
  201.5 9.3 %shard_map.75 = (f32[256,1024]{1,0:T(8,128)}, f32[1,1024]{1,0:T(1,128)}) custom-call(s32[2]{0:T(128)} %iota.3.sup, s32[4]{0:T(128)} %pad_add_fusion.place, f32[16,128,256]{2,1,0:T(8,128)} %bitcast.35, f32[1024,256]{1,0:T(8,128)} %shard_map.74.refs_1_, bf16[4,1024,1024]{2,1,0:T(8,128)(2,1)} %get-tuple-element.18.refs_2_.refs_4_, ...), custom_call_target="tpu_custom_call" | custom-call | flops 6442450944 | bytes 8388608 | tf_op jit(solution)/shard_map/pallas_call | solution.py:322
  211.5 12.8 %all_to_all.6 = f32[16,1,1024]{2,1,0:T(1,128)S(1)} all-to-all(f32[16,1,1024]{2,1,0:T(1,128)S(1)} %broadcast_in_dim.2), channel_id=1, replica_groups=mesh['chain'=16,'z'=8,'c'=2] {'chain'}, dimensions={0} | all-to-all | bytes 131072 | tf_op jit(solution)/shard_map/all_to_all | solution.py:383
  (86 shorter events, 14.5 us)
Async XLA Ops:
  7.2 156.8 %all-gather.4.cloned.1.call-start = ((), (), s32[]{:S(2)}) async-start(), calls=%async_computation.1 | async-start | bytes 8421376 | tf_op jit(solution)/shard_map/all_gather | solution.py:355
  7.9 193.1 %all-gather.6.cloned.1.call-start = ((), (), s32[]{:S(2)}) async-start(), calls=%async_computation.2 | async-start | bytes 2228224 | tf_op jit(solution)/shard_map/all_gather | solution.py:374
  10.2 14.6 %collective-permute-start = (f32[512,256]{1,0:T(8,128)S(1)}, f32[512,256]{1,0:T(8,128)S(1)}, u32[]{:S(2)}, u32[]{:S(2)}) collective-permute-start(f32[512,256]{1,0:T(8,128)S(1)} %maximum_select_fusion), channel_id=1, source_target_pairs={{0,16},{2,18},{4,20},{6,22},{8,24},{10,26},{12,28},{14,30},{16,32}... | collective-permute-start | bytes 1572872 | tf_op jit(solution)/shard_map/ppermute | solution.py:40
  11.5 27.9 %collective-permute-start.1 = (f32[512,256]{1,0:T(8,128)S(1)}, f32[512,256]{1,0:T(8,128)S(1)}, u32[]{:S(2)}, u32[]{:S(2)}) collective-permute-start(f32[512,256]{1,0:T(8,128)S(1)} %maximum_select_fusion), channel_id=1, source_target_pairs={{0,32},{2,34},{4,36},{6,38},{8,40},{10,42},{12,44},{14,46},{16,48}... | collective-permute-start | bytes 1572872 | tf_op jit(solution)/shard_map/ppermute | solution.py:40
  12.8 26.6 %collective-permute-start.2 = (f32[512,256]{1,0:T(8,128)S(1)}, f32[512,256]{1,0:T(8,128)S(1)}, u32[]{:S(2)}, u32[]{:S(2)}) collective-permute-start(f32[512,256]{1,0:T(8,128)S(1)} %maximum_select_fusion), channel_id=1, source_target_pairs={{0,48},{2,50},{4,52},{6,54},{8,56},{10,58},{12,60},{14,62},{16,0},... | collective-permute-start | bytes 1572872 | tf_op jit(solution)/shard_map/ppermute | solution.py:40
  39.5 4.7 %copy-start = (f32[3,512,256]{2,1,0:T(8,128)}, f32[3,512,256]{2,1,0:T(8,128)S(1)}, u32[]{:S(2)}) copy-start(f32[3,512,256]{2,1,0:T(8,128)S(1)} %pad_maximum_fusion.near) | copy-start | bytes 4718596
  39.5 4.7 %collective-permute-start.3 = (f32[3,512,256]{2,1,0:T(8,128)S(1)}, f32[3,512,256]{2,1,0:T(8,128)S(1)}, u32[]{:S(2)}, u32[]{:S(2)}) collective-permute-start(f32[3,512,256]{2,1,0:T(8,128)S(1)} %pad_maximum_fusion.near), channel_id=1, source_target_pairs={{0,1},{1,0},{2,3},{3,2},{4,5},{5,4},{6,7},{7,6},{8,9},{9,8},{10,11... | collective-permute-start | bytes 4718600 | tf_op jit(solution)/shard_map/ppermute | solution.py:40
  44.2 1.1 copy-start.2
  54.1 9.1 %collective-permute-start.4 = (f32[64,1024]{1,0:T(8,128)S(1)}, f32[64,1024]{1,0:T(8,128)S(1)}, u32[]{:S(2)}, u32[]{:S(2)}) collective-permute-start(f32[64,1024]{1,0:T(8,128)S(1)} %constant_dynamic-slice_fusion.3), channel_id=1, source_target_pairs={{0,64},{1,65},{2,66},{3,67},{4,68},{5,69},{6,70},{7,71},{8,72},{9,... | collective-permute-start | bytes 786440 | tf_op jit(solution)/shard_map/ppermute | solution.py:40
  57.3 11.4 %collective-permute-start.5 = (f32[64,1024]{1,0:T(8,128)S(1)}, f32[64,1024]{1,0:T(8,128)S(1)}, u32[]{:S(2)}, u32[]{:S(2)}) collective-permute-start(f32[64,1024]{1,0:T(8,128)S(1)} %constant_dynamic-slice_fusion.3), channel_id=1, source_target_pairs={{0,128},{1,129},{2,130},{3,131},{4,132},{5,133},{6,134},{7,135},{8... | collective-permute-start | bytes 786440 | tf_op jit(solution)/shard_map/ppermute | solution.py:40
  61.8 11.1 %collective-permute-start.6 = (f32[64,1024]{1,0:T(8,128)S(1)}, f32[64,1024]{1,0:T(8,128)S(1)}, u32[]{:S(2)}, u32[]{:S(2)}) collective-permute-start(f32[64,1024]{1,0:T(8,128)S(1)} %constant_dynamic-slice_fusion.3), channel_id=1, source_target_pairs={{0,192},{1,193},{2,194},{3,195},{4,196},{5,197},{6,198},{7,199},{8... | collective-permute-start | bytes 786440 | tf_op jit(solution)/shard_map/ppermute | solution.py:40
  63.2 0.7 copy-start.8
  68.7 16.0 %copy-start.4 = (f32[64,1024]{1,0:T(8,128)}, f32[64,1024]{1,0:T(8,128)S(1)}, u32[]{:S(2)}) copy-start(f32[64,1024]{1,0:T(8,128)S(1)} %collective-permute-done.5.s2) | copy-start | bytes 786436
  72.9 11.8 %copy-start.5 = (f32[64,1024]{1,0:T(8,128)}, f32[64,1024]{1,0:T(8,128)S(1)}, u32[]{:S(2)}) copy-start(f32[64,1024]{1,0:T(8,128)S(1)} %collective-permute-done.6.s3) | copy-start | bytes 786436
  72.9 4.9 %collective-permute-start.7 = (f32[64,256]{1,0:T(8,128)}, f32[64,256]{1,0:T(8,128)S(1)}, u32[]{:S(2)}, u32[]{:S(2)}) collective-permute-start(f32[64,256]{1,0:T(8,128)} %shard_map.69.t0.t1), channel_id=1, source_target_pairs={{0,16},{1,17},{2,18},{3,19},{4,20},{5,21},{6,22},{7,23},{8,24},{9,... | collective-permute-start | bytes 196616 | tf_op jit(solution)/shard_map/ppermute | solution.py:40
  74.1 4.9 %collective-permute-start.8 = (f32[64,256]{1,0:T(8,128)}, f32[64,256]{1,0:T(8,128)S(1)}, u32[]{:S(2)}, u32[]{:S(2)}) collective-permute-start(f32[64,256]{1,0:T(8,128)} %shard_map.69.t0.t1), channel_id=1, source_target_pairs={{0,32},{1,33},{2,34},{3,35},{4,36},{5,37},{6,38},{7,39},{8,40},{9,... | collective-permute-start | bytes 196616 | tf_op jit(solution)/shard_map/ppermute | solution.py:40
  74.8 5.3 %collective-permute-start.9 = (f32[64,256]{1,0:T(8,128)}, f32[64,256]{1,0:T(8,128)S(1)}, u32[]{:S(2)}, u32[]{:S(2)}) collective-permute-start(f32[64,256]{1,0:T(8,128)} %shard_map.69.t0.t1), channel_id=1, source_target_pairs={{0,48},{1,49},{2,50},{3,51},{4,52},{5,53},{6,54},{7,55},{8,56},{9,... | collective-permute-start | bytes 196616 | tf_op jit(solution)/shard_map/ppermute | solution.py:40
  77.8 2.3 copy-start.16
  79.1 1.0 copy-start.17
  84.7 12.7 %collective-permute-start.19 = (f32[64,256]{1,0:T(8,128)}, f32[64,256]{1,0:T(8,128)S(1)}, u32[]{:S(2)}, u32[]{:S(2)}) collective-permute-start(f32[64,256]{1,0:T(8,128)} %get-tuple-element.16), channel_id=1, source_target_pairs={{0,14},{1,15},{2,0},{3,1},{4,2},{5,3},{6,4},{7,5},{8,6},{9,7},{10,... | collective-permute-start | bytes 196616 | tf_op jit(solution)/shard_map/ppermute | solution.py:40
  91.2 8.4 %collective-permute-start.20 = (f32[64,256]{1,0:T(8,128)}, f32[64,256]{1,0:T(8,128)S(1)}, u32[]{:S(2)}, u32[]{:S(2)}) collective-permute-start(f32[64,256]{1,0:T(8,128)} %get-tuple-element.16), channel_id=1, source_target_pairs={{0,12},{1,13},{2,14},{3,15},{4,0},{5,1},{6,2},{7,3},{8,4},{9,5},{1... | collective-permute-start | bytes 196616 | tf_op jit(solution)/shard_map/ppermute | solution.py:40
  92.5 8.6 %collective-permute-start.21 = (f32[64,256]{1,0:T(8,128)}, f32[64,256]{1,0:T(8,128)S(1)}, u32[]{:S(2)}, u32[]{:S(2)}) collective-permute-start(f32[64,256]{1,0:T(8,128)} %get-tuple-element.16), channel_id=1, source_target_pairs={{0,10},{1,11},{2,12},{3,13},{4,14},{5,15},{6,0},{7,1},{8,2},{9,3},... | collective-permute-start | bytes 196616 | tf_op jit(solution)/shard_map/ppermute | solution.py:40
  93.0 8.1 %collective-permute-start.22 = (f32[64,256]{1,0:T(8,128)}, f32[64,256]{1,0:T(8,128)S(1)}, u32[]{:S(2)}, u32[]{:S(2)}) collective-permute-start(f32[64,256]{1,0:T(8,128)} %get-tuple-element.16), channel_id=1, source_target_pairs={{0,8},{1,9},{2,10},{3,11},{4,12},{5,13},{6,14},{7,15},{8,0},{9,1},... | collective-permute-start | bytes 196616 | tf_op jit(solution)/shard_map/ppermute | solution.py:40
  97.4 7.8 %collective-permute-start.23 = (f32[64,256]{1,0:T(8,128)}, f32[64,256]{1,0:T(8,128)S(1)}, u32[]{:S(2)}, u32[]{:S(2)}) collective-permute-start(f32[64,256]{1,0:T(8,128)} %get-tuple-element.16), channel_id=1, source_target_pairs={{0,6},{1,7},{2,8},{3,9},{4,10},{5,11},{6,12},{7,13},{8,14},{9,15},... | collective-permute-start | bytes 196616 | tf_op jit(solution)/shard_map/ppermute | solution.py:40
  97.4 12.7 %collective-permute-start.24 = (f32[64,256]{1,0:T(8,128)}, f32[64,256]{1,0:T(8,128)S(1)}, u32[]{:S(2)}, u32[]{:S(2)}) collective-permute-start(f32[64,256]{1,0:T(8,128)} %get-tuple-element.16), channel_id=1, source_target_pairs={{0,4},{1,5},{2,6},{3,7},{4,8},{5,9},{6,10},{7,11},{8,12},{9,13},{1... | collective-permute-start | bytes 196616 | tf_op jit(solution)/shard_map/ppermute | solution.py:40
  99.6 12.4 %collective-permute-start.25 = (f32[64,256]{1,0:T(8,128)}, f32[64,256]{1,0:T(8,128)S(1)}, u32[]{:S(2)}, u32[]{:S(2)}) collective-permute-start(f32[64,256]{1,0:T(8,128)} %get-tuple-element.16), channel_id=1, source_target_pairs={{0,2},{1,3},{2,4},{3,5},{4,6},{5,7},{6,8},{7,9},{8,10},{9,11},{10,... | collective-permute-start | bytes 196616 | tf_op jit(solution)/shard_map/ppermute | solution.py:40
  112.0 28.2 %collective-permute-start.26 = (f32[8,64,256]{2,1,0:T(8,128)S(1)}, f32[8,64,256]{2,1,0:T(8,128)S(1)}, u32[]{:S(2)}, u32[]{:S(2)}) collective-permute-start(f32[8,64,256]{2,1,0:T(8,128)S(1)} %bitcast_dynamic-update-slice_fusion), channel_id=1, source_target_pairs={{0,1},{1,0},{2,3},{3,2},{4,5},{5,4},{6,7},{7,6},{8,9},{9,8},{10,11... | collective-permute-start | bytes 1572872 | tf_op jit(solution)/shard_map/ppermute | solution.py:40
  115.3 10.8 %collective-permute-start.10 = (f32[64,1024]{1,0:T(8,128)}, f32[64,1024]{1,0:T(8,128)S(1)}, u32[]{:S(2)}, u32[]{:S(2)}) collective-permute-start(f32[64,1024]{1,0:T(8,128)} %get-tuple-element.15), channel_id=1, source_target_pairs={{0,64},{1,65},{2,66},{3,67},{4,68},{5,69},{6,70},{7,71},{8,72},{9,... | collective-permute-start | bytes 786440 | tf_op jit(solution)/shard_map/ppermute | solution.py:40
  116.6 15.1 %collective-permute-start.11 = (f32[64,1024]{1,0:T(8,128)}, f32[64,1024]{1,0:T(8,128)S(1)}, u32[]{:S(2)}, u32[]{:S(2)}) collective-permute-start(f32[64,1024]{1,0:T(8,128)} %get-tuple-element.15), channel_id=1, source_target_pairs={{0,128},{1,129},{2,130},{3,131},{4,132},{5,133},{6,134},{7,135},{8... | collective-permute-start | bytes 786440 | tf_op jit(solution)/shard_map/ppermute | solution.py:40
  126.1 5.6 %copy-start.6 = (f32[64,1024]{1,0:T(8,128)}, f32[64,1024]{1,0:T(8,128)S(1)}, u32[]{:S(2)}) copy-start(f32[64,1024]{1,0:T(8,128)S(1)} %collective-permute-done.10.m1) | copy-start | bytes 786436
  131.7 0.7 copy-start.7
  136.1 11.1 %copy-start.3 = (f32[128,256]{1,0:T(8,128)S(1)}, f32[128,256]{1,0:T(8,128)}, u32[]{:S(2)}) copy-start(f32[128,256]{1,0:T(8,128)} %shard_map.71.refs_0_) | copy-start | bytes 393220
  136.1 11.1 %collective-permute-start.12 = (f32[128,256]{1,0:T(8,128)}, f32[128,256]{1,0:T(8,128)S(1)}, u32[]{:S(2)}, u32[]{:S(2)}) collective-permute-start(f32[128,256]{1,0:T(8,128)} %shard_map.71.refs_0_), channel_id=1, source_target_pairs={{0,16},{1,17},{2,18},{3,19},{4,20},{5,21},{6,22},{7,23},{8,24},{9,... | collective-permute-start | bytes 393224 | tf_op jit(solution)/shard_map/ppermute | solution.py:40
  136.4 13.6 %collective-permute-start.13 = (f32[128,256]{1,0:T(8,128)}, f32[128,256]{1,0:T(8,128)S(1)}, u32[]{:S(2)}, u32[]{:S(2)}) collective-permute-start(f32[128,256]{1,0:T(8,128)} %shard_map.71.refs_0_), channel_id=1, source_target_pairs={{0,32},{1,33},{2,34},{3,35},{4,36},{5,37},{6,38},{7,39},{8,40},{9,... | collective-permute-start | bytes 393224 | tf_op jit(solution)/shard_map/ppermute | solution.py:40
  138.8 15.7 %collective-permute-start.14 = (f32[128,256]{1,0:T(8,128)}, f32[128,256]{1,0:T(8,128)S(1)}, u32[]{:S(2)}, u32[]{:S(2)}) collective-permute-start(f32[128,256]{1,0:T(8,128)} %shard_map.71.refs_0_), channel_id=1, source_target_pairs={{0,48},{1,49},{2,50},{3,51},{4,52},{5,53},{6,54},{7,55},{8,56},{9,... | collective-permute-start | bytes 393224 | tf_op jit(solution)/shard_map/ppermute | solution.py:40
  138.9 15.7 %collective-permute-start.15 = (f32[128,256]{1,0:T(8,128)}, f32[128,256]{1,0:T(8,128)S(1)}, u32[]{:S(2)}, u32[]{:S(2)}) collective-permute-start(f32[128,256]{1,0:T(8,128)} %shard_map.71.refs_0_), channel_id=1, source_target_pairs={{0,64},{1,65},{2,66},{3,67},{4,68},{5,69},{6,70},{7,71},{8,72},{9,... | collective-permute-start | bytes 393224 | tf_op jit(solution)/shard_map/ppermute | solution.py:40
  140.2 14.4 %collective-permute-start.16 = (f32[128,256]{1,0:T(8,128)}, f32[128,256]{1,0:T(8,128)S(1)}, u32[]{:S(2)}, u32[]{:S(2)}) collective-permute-start(f32[128,256]{1,0:T(8,128)} %shard_map.71.refs_0_), channel_id=1, source_target_pairs={{0,80},{1,81},{2,82},{3,83},{4,84},{5,85},{6,86},{7,87},{8,88},{9,... | collective-permute-start | bytes 393224 | tf_op jit(solution)/shard_map/ppermute | solution.py:40
  147.3 7.3 %copy-start.9 = (f32[128,256]{1,0:T(8,128)}, f32[128,256]{1,0:T(8,128)S(1)}, u32[]{:S(2)}) copy-start(f32[128,256]{1,0:T(8,128)S(1)} %collective-permute-done.12.refs_1_) | copy-start | bytes 393220
  147.3 7.3 %collective-permute-start.17 = (f32[128,256]{1,0:T(8,128)S(1)}, f32[128,256]{1,0:T(8,128)S(1)}, u32[]{:S(2)}, u32[]{:S(2)}) collective-permute-start(f32[128,256]{1,0:T(8,128)S(1)} %copy-done.3), channel_id=1, source_target_pairs={{0,96},{1,97},{2,98},{3,99},{4,100},{5,101},{6,102},{7,103},{8,104... | collective-permute-start | bytes 393224 | tf_op jit(solution)/shard_map/ppermute | solution.py:40
  150.1 4.5 %copy-start.10 = (f32[128,256]{1,0:T(8,128)}, f32[128,256]{1,0:T(8,128)S(1)}, u32[]{:S(2)}) copy-start(f32[128,256]{1,0:T(8,128)S(1)} %collective-permute-done.13.refs_2_) | copy-start | bytes 393220
  150.1 6.1 %collective-permute-start.18 = (f32[128,256]{1,0:T(8,128)S(1)}, f32[128,256]{1,0:T(8,128)S(1)}, u32[]{:S(2)}, u32[]{:S(2)}) collective-permute-start(f32[128,256]{1,0:T(8,128)S(1)} %copy-done.3), channel_id=1, source_target_pairs={{0,112},{1,113},{2,114},{3,115},{4,116},{5,117},{6,118},{7,119},{8... | collective-permute-start | bytes 393224 | tf_op jit(solution)/shard_map/ppermute | solution.py:40
  154.6 1.6 copy-start.11
  154.6 1.6 copy-start.12
  154.6 1.6 copy-start.13
  154.6 1.6 copy-start.14
  156.2 0.7 copy-start.15
  156.8 4.2 %copy-start.1 = (bf16[1024,1024]{1,0:T(8,128)(2,1)S(1)}, bf16[1024,1024]{1,0:T(8,128)(2,1)}, u32[]{:S(2)}) copy-start(bf16[1024,1024]{1,0:T(8,128)(2,1)} %cand_ref.1) | copy-start | bytes 6291460
  161.0 1.6 copy-start.19
  (1 other events, 0.6 us)
Sparse Core Ops, SparseCore 0:
  11.7 123.7 all-gather.3
  161.2 39.7 all-gather.5

commit v4 on v3

--- a/solution.py
+++ b/solution.py
@@ -203,22 +203,32 @@
     )(place, *args, factor)
 
 
+def interleave(full, mine, other, place):
+    m = mine.shape[1]
+    c, z = place[1], place[2]
+    for k in range(ZS):
+        at = 2 * jnp.bitwise_xor(z, k)
+        full[pl.ds(pl.multiple_of((at + c) * m, m), m), :] = mine[k]
+        full[pl.ds(pl.multiple_of((at + 1 - c) * m, m), m), :] = other[k]
+
+
 def second_inverse_kernel(place, *refs):
-    ts, qs, (st, below_ref, out_ref, t, q) = refs[:SIDE], refs[SIDE : 2 * SIDE], refs[2 * SIDE :]
+    ts, qs, (st, mine, other, out_ref, t, q, full) = refs[:SIDE], refs[SIDE : 2 * SIDE], refs[2 * SIDE :]
     x, y = place[0], place[3]
     m, bs = ts[0].shape
     for k in range(SIDE):
         t[:, spot(k, x, bs)] = ts[k][...]
         q[:, spot(k, x, bs)] = qs[k][...]
+    interleave(full, mine, other, place)
     total = mul3(split(t[...]), split(st[...]), NN)
-    below = mul3(split(q[...]), split(below_ref[...]), NN)
+    below = mul3(split(q[...]), split(full[...]), NN)
     total = total + jnp.where(y == 3, below, 0.0)
     half = m // 2
     out_ref[:half] = jnp.where(y >= 2, -total[:half], 0.0)
     out_ref[half:] = jnp.where(y == 3, -total[half:], 0.0)
 
 
-def second_inverse(place, ts, qs, st, below):
+def second_inverse(place, ts, qs, st, mine, other):
     m, bs = ts[0].shape
     size = SIDE * bs
     fixed = lambda a: pl.BlockSpec(a.shape, lambda i, p: (0,) * a.ndim)
@@ -228,13 +238,13 @@
             num_scalar_prefetch=1,
             grid=(1,),
             in_specs=[fixed(a) for a in (*ts, *qs)]
-            + [pl.BlockSpec((size, bs), lambda i, p: (0, p[0])), fixed(below)],
+            + [pl.BlockSpec((size, bs), lambda i, p: (0, p[0])), fixed(mine), fixed(other)],
             out_specs=pl.BlockSpec((m, bs), lambda i, p: (0, 0)),
-            scratch_shapes=[pltpu.VMEM((m, size), F32)] * 2,
+            scratch_shapes=[pltpu.VMEM((m, size), F32)] * 2 + [pltpu.VMEM((size, bs), F32)],
         ),
         out_shape=jax.ShapeDtypeStruct((m, bs), F32),
         compiler_params=PARAMS,
-    )(place, *ts, *qs, st, below)
+    )(place, *ts, *qs, st, mine, other)
 
 
 def panel_kernel(beta, train_ref, cand_ref, scale_ref, hi_ref, lo_ref):
@@ -272,7 +282,7 @@
     if last:
         m2, win, h0, l0, h1, l1, targets, out, mean, full, mh, ml = refs
     else:
-        st, m1, h0, l0, h1, l1, out, full, mh, ml = refs
+        st, mine, other, h0, l0, h1, l1, out, full, mh, ml = refs
     size = full.shape[0]
 
     @pl.when(pl.program_id(0) == 0)
@@ -286,7 +296,7 @@
                 full[g * m : (g + 1) * m] = m2[g, m:]
         else:
             mh[:size], ml[:size] = split(st[...])
-            full[...] = m1[...]
+            interleave(full, mine, other, place)
         mh[size:], ml[size:] = split(full[...])
 
     w = mul3((h0[0], l0[0]), (mh[:size], ml[:size]), NN)
@@ -334,14 +344,8 @@
     )(sup, place, *args)
 
 
-def z_gather(z, c, own):
-    m, bs = own.shape
-    parts = [own] + [send(own, lambda y, x, z, c: (y, x, (z - k) % ZS, c)) for k in range(1, ZS)]
-    mine = jnp.stack(parts)
-    other = swap_core(mine)
-    even = c == 0
-    both = jnp.stack([jnp.where(even, mine, other), jnp.where(even, other, mine)], 1)
-    return jnp.roll(both, z, axis=0).reshape(2 * ZS * m, bs)
+def join_z(mine, bit):
+    return jnp.concatenate([mine, send(mine, lambda y, x, z, c: (y, x, z ^ bit, c))], 0)
 
 
 def shards(train_emb, cand_emb, factor, diag_inverse, targets):
@@ -368,9 +372,12 @@
     t1 = first_factor(place, hop(sl, 1), factor)
     t1, s2, s3 = lax.optimization_barrier((t1, hop(sl, 2), hop(sl, 3)))
     m1, m1_own = first_inverse(place, x_ring(t1), st)
-    t2 = second_factor(place, s2, s3, hop(m1, 1), hop(m1, 2), t1, factor)
-    m1_full = z_gather(z, c, m1_own)
-    m2 = second_inverse(place, x_ring(t2), [hop(t2, 1, k) for k in range(SIDE)], st, m1_full)
+    slices, up1, up2 = lax.optimization_barrier((join_z(m1_own[None], 1), hop(m1, 1), hop(m1, 2)))
+    t2 = second_factor(place, s2, s3, up1, up2, t1, factor)
+    slices, t2, *ts = lax.optimization_barrier((join_z(slices, 2), *x_ring(t2)))
+    slices, *qs = lax.optimization_barrier((join_z(slices, 4), *[hop(t2, 1, k) for k in range(SIDE)]))
+    m1_full = (slices, swap_core(slices))
+    m2 = second_inverse(place, [t2, *ts], qs, st, *m1_full)
     m2_full = lax.all_gather(m2, ("z", "c"), axis=0)
 
     train, _ = lax.optimization_barrier((train, m2))
@@ -378,7 +385,7 @@
     cand_scale = lax.rsqrt(jnp.sum(cand_f * cand_f, axis=1, keepdims=True) + EPS)
     panel = make_panel(train, cand_emb, cand_scale, size)
     sup = jnp.stack([y, jnp.maximum(y - 1, 0)]).astype(jnp.int32)
-    (w,) = apply(sup, place, (st, m1_full), panel, bs)
+    (w,) = apply(sup, place, (st, *m1_full), panel, bs)
     w, mean = apply(jnp.arange(2, dtype=jnp.int32), place, (m2_full, w), panel, bs, targets.reshape(bs, 1))
     parts = lax.all_to_all(jnp.broadcast_to(mean, (CHAIN, n)), "chain", 0, 0, tiled=True)
     return w, jnp.sum(parts, axis=0)

time: 233 us -> 219 us (0.940)
  waiting for transfers between devices: 66.5 us -> 55.7 us
  local copies, waits for them, and re-layouts: 13.4 us -> 10.9 us
    ppermute x27 -> x23, waiting for transfers between devices: 55.1 us -> 48.5 us  [send(): return lax.ppermute(value, AXES, moves(target))]
    all_gather x1, waiting for transfers between devices: 10.7 us -> 6.6 us  [shards(): m2_full = lax.all_gather(m2, ('z', 'c'), axis=0)]
    ppermute x27 -> x23, starting transfers between devices: 62.4 us -> 60.8 us  [send(): return lax.ppermute(value, AXES, moves(target))]
    unnamed x47 -> x42, local copies, waits for them, and re-layouts: 4.75 us -> 3.34 us
  transfers between devices with their start and end apart: 29 -> 25, of which waited for: 15 -> 16; matrix products, arithmetic and copies ran while one was open for 5% -> 5% of each run, Pallas kernels for 21% -> 23%
where the time goes in v4:
time: 219 us; the launch traced here: 218 us
  starting transfers between devices  60.8 us (28%)
  Pallas kernels  59.1 us (27%)
  waiting for transfers between devices  55.7 us (25%)
  between operations  14.4 us (7%)
  blocking collectives  12.8 us (6%)
  local copies, waits for them, and re-layouts  10.9 us (5%)
  other arithmetic  4.43 us (2%)
    ppermute x23, starting transfers between devices, send(): return lax.ppermute(value, AXES, moves(target))  60.8 us
    ppermute x23, waiting for transfers between devices, send(): return lax.ppermute(value, AXES, moves(target))  48.5 us
    pallas_call x2, Pallas kernels, apply(): pl.pallas_call(functools.partial(apply_kernel, last), grid_spec=pltpu.Pre...  18.3 us
    pallas_call x1, Pallas kernels, make_panel(): pl.pallas_call(functools.partial(panel_kernel, 0.5 * math.sqrt(e)), grid=...  17.5 us
    all_to_all x1, blocking collectives, shards(): lax.all_to_all(jnp.broadcast_to(mean, (CHAIN, n)), 'chain', 0, 0, tiled=T...  12.8 us
    pallas_call x1, Pallas kernels, diagonal(): pl.pallas_call(diagonal_kernel, in_specs=[SMEM] + [VMEM] * 4, out_specs=V...  7.8 us
    all_gather x1, waiting for transfers between devices, shards(): m2_full = lax.all_gather(m2, ('z', 'c'), axis=0)  6.6 us
  transfers between devices with their start and end apart: 25, of which 16 were waited for; matrix products, arithmetic and copies ran while one was open for 5% of the time, Pallas kernels for 23%

profile of v4, /device:TPU:1, one launch (start us, length us, event | category | flops | bytes accessed | tf_op | source)
XLA Modules:
  0.0 218.2 jit_solution(6975299095257980112)
XLA Ops:
  8.0 1.2 constant_dynamic-slice_fusion.1
  9.1 1.0 maximum_select_fusion
  10.2 1.3 collective-permute-start
  11.5 1.3 collective-permute-start.1
  13.5 11.3 %collective-permute-done = f32[512,256]{1,0:T(8,128)S(1)} collective-permute-done((f32[512,256]{1,0:T(8,128)S(1)}, f32[512,256]{1,0:T(8,128)S(1)}, u32[]{:S(2)}, u32[]{:S(2)}) %collective-permute-start) | collective-permute-done | bytes 524320 | tf_op jit(solution)/shard_map/ppermute | solution.py:40
  24.7 14.6 %collective-permute-done.1 = f32[512,256]{1,0:T(8,128)S(1)} collective-permute-done((f32[512,256]{1,0:T(8,128)S(1)}, f32[512,256]{1,0:T(8,128)S(1)}, u32[]{:S(2)}, u32[]{:S(2)}) %collective-permute-start.1) | collective-permute-done | bytes 524320 | tf_op jit(solution)/shard_map/ppermute | solution.py:40
  39.5 1.6 collective-permute-start.3
  41.7 2.3 %constant_dynamic-slice_fusion.4.f_ref = f32[256,1024]{1,0:T(8,128)} fusion(f32[256,4096]{1,0:T(8,128)} %f_ref.3, s32[]{:T(128)S(6)} %select_n.27), kind=kLoop, calls=%fused_computation.11 | loop fusion | bytes 2097156 | tf_op jit(solution)/shard_map/dynamic_slice | solution.py:361
  44.2 1.1 copy-done.4
  45.3 7.8 %shard_map.68.st.refs_8_.refs_0_ = f32[1024,1024]{1,0:T(8,128)} custom-call(s32[4]{0:T(128)} %pad_add_fusion.place, f32[256,256]{1,0:T(8,128)} %d_ref.1, f32[256,1024]{1,0:T(8,128)} %constant_dynamic-slice_fusion.4.f_ref, f32[3,512,256]{2,1,0:T(8,128)} %copy-done, f32[3,512,256]{2,1,0:T(8,128)} %copy-done.4), custom_call_target="tpu_custom_call" | custom-call | tf_op jit(solution)/shard_map/pallas_call | solution.py:122
  53.1 1.0 constant_dynamic-slice_fusion.3
  54.1 3.2 %collective-permute-start.4 = (f32[64,1024]{1,0:T(8,128)S(1)}, f32[64,1024]{1,0:T(8,128)S(1)}, u32[]{:S(2)}, u32[]{:S(2)}) collective-permute-start(f32[64,1024]{1,0:T(8,128)S(1)} %constant_dynamic-slice_fusion.3), channel_id=1, source_target_pairs={{0,64},{1,65},{2,66},{3,67},{4,68},{5,69},{6,70},{7,71},{8,72},{9,... | collective-permute-start | bytes 786440 | tf_op jit(solution)/shard_map/ppermute | solution.py:40
  57.3 4.5 %collective-permute-start.5 = (f32[64,1024]{1,0:T(8,128)S(1)}, f32[64,1024]{1,0:T(8,128)S(1)}, u32[]{:S(2)}, u32[]{:S(2)}) collective-permute-start(f32[64,1024]{1,0:T(8,128)S(1)} %constant_dynamic-slice_fusion.3), channel_id=1, source_target_pairs={{0,128},{1,129},{2,130},{3,131},{4,132},{5,133},{6,134},{7,135},{8... | collective-permute-start | bytes 786440 | tf_op jit(solution)/shard_map/ppermute | solution.py:40
  61.9 1.3 collective-permute-start.6
  63.9 3.3 %shard_map.69.t0.t1 = f32[64,256]{1,0:T(8,128)} custom-call(s32[4]{0:T(128)} %pad_add_fusion.place, f32[64,1024]{1,0:T(8,128)} %copy-done.9, f32[256,4096]{1,0:T(8,128)} %f_ref.3), custom_call_target="tpu_custom_call" | custom-call | tf_op jit(solution)/shard_map/pallas_call | solution.py:139
  67.1 1.6 collective-permute-done.5.s2
  68.7 4.2 %collective-permute-done.6.s3 = f32[64,1024]{1,0:T(8,128)S(1)} collective-permute-done((f32[64,1024]{1,0:T(8,128)S(1)}, f32[64,1024]{1,0:T(8,128)S(1)}, u32[]{:S(2)}, u32[]{:S(2)}) %collective-permute-start.6) | collective-permute-done | bytes 262176 | tf_op jit(solution)/shard_map/ppermute | solution.py:40
  72.9 1.2 collective-permute-start.7
  74.8 2.1 collective-permute-start.9
  77.8 1.3 collective-permute-done.8.t2
  79.1 1.0 collective-permute-done.9.t3
  80.7 4.0 %shard_map.70 = (f32[64,1024]{1,0:T(8,128)}, f32[64,256]{1,0:T(8,128)}) custom-call(s32[4]{0:T(128)} %pad_add_fusion.place, f32[64,256]{1,0:T(8,128)} %shard_map.69.t0.t1, f32[64,256]{1,0:T(8,128)} %copy-done.17, f32[64,256]{1,0:T(8,128)} %copy-done.18, f32[64,256]{1,0:T(8,128)} %copy-done.19, f32[1024,1024]{1,0:T(8,128)} %shard_map.68.st.refs_8_.refs_0_), custom_call_target="tpu_custom_call" | custom-call | tf_op jit(solution)/shard_map/pallas_call | solution.py:170
  84.7 1.3 collective-permute-start.11
  86.0 6.9 %collective-permute-start.12 = (f32[64,1024]{1,0:T(8,128)}, f32[64,1024]{1,0:T(8,128)S(1)}, u32[]{:S(2)}, u32[]{:S(2)}) collective-permute-start(f32[64,1024]{1,0:T(8,128)} %get-tuple-element.27), channel_id=1, source_target_pairs={{0,128},{1,129},{2,130},{3,131},{4,132},{5,133},{6,134},{7,135},{8... | collective-permute-start | bytes 786440 | tf_op jit(solution)/shard_map/ppermute | solution.py:40
  93.0 1.9 collective-permute-start.10
  94.8 1.9 collective-permute-done.10
  97.6 3.1 %collective-permute-start.13 = (f32[2,64,256]{2,1,0:T(8,128)S(1)}, f32[2,64,256]{2,1,0:T(8,128)S(1)}, u32[]{:S(2)}, u32[]{:S(2)}) collective-permute-start(f32[2,64,256]{2,1,0:T(8,128)S(1)} %pad_maximum_fusion.3), channel_id=1, source_target_pairs={{0,4},{1,5},{2,6},{3,7},{4,0},{5,1},{6,2},{7,3},{8,12},{9,13},{10,... | collective-permute-start | bytes 393224 | tf_op jit(solution)/shard_map/ppermute | solution.py:40
  100.7 4.1 %shard_map.71.refs_0_ = f32[128,256]{1,0:T(8,128)} custom-call(s32[4]{0:T(128)} %pad_add_fusion.place, f32[64,1024]{1,0:T(8,128)} %copy-done.5, f32[64,1024]{1,0:T(8,128)} %copy-done.6, f32[64,1024]{1,0:T(8,128)} %copy-done.7, f32[64,1024]{1,0:T(8,128)} %copy-done.8, f32[64,256]{1,0:T(8,128)} %shard_map.69.t0.t1, f32[256,4096]{1,0:T(8,128)} %f_ref.3), custom_call_target="tpu_custom_call" | custom-call | tf_op jit(solution)/shard_map/pallas_call | solution.py:194
  104.8 2.2 collective-permute-start.14
  107.9 1.6 collective-permute-start.16
  109.5 2.6 %collective-permute-done.14.refs_1_ = f32[128,256]{1,0:T(8,128)S(1)} collective-permute-done((f32[128,256]{1,0:T(8,128)}, f32[128,256]{1,0:T(8,128)S(1)}, u32[]{:S(2)}, u32[]{:S(2)}) %collective-permute-start.14) | collective-permute-done | bytes 131104 | tf_op jit(solution)/shard_map/ppermute | solution.py:40
  112.1 4.2 %collective-permute-done.15.refs_2_ = f32[128,256]{1,0:T(8,128)S(1)} collective-permute-done((f32[128,256]{1,0:T(8,128)}, f32[128,256]{1,0:T(8,128)S(1)}, u32[]{:S(2)}, u32[]{:S(2)}) %collective-permute-start.15) | collective-permute-done | bytes 131104 | tf_op jit(solution)/shard_map/ppermute | solution.py:40
  116.3 1.1 collective-permute-done.16.refs_3_
  117.4 6.8 %collective-permute-start.17 = (f32[4,64,256]{2,1,0:T(8,128)S(1)}, f32[4,64,256]{2,1,0:T(8,128)S(1)}, u32[]{:S(2)}, u32[]{:S(2)}) collective-permute-start(f32[4,64,256]{2,1,0:T(8,128)S(1)} %pad_maximum_fusion.2), channel_id=1, source_target_pairs={{0,8},{1,9},{2,10},{3,11},{4,12},{5,13},{6,14},{7,15},{8,0},{9,1},... | collective-permute-start | bytes 786440 | tf_op jit(solution)/shard_map/ppermute | solution.py:40
  124.2 1.3 collective-permute-start.18
  125.5 3.6 %collective-permute-start.19 = (f32[128,256]{1,0:T(8,128)}, f32[128,256]{1,0:T(8,128)S(1)}, u32[]{:S(2)}, u32[]{:S(2)}) collective-permute-start(f32[128,256]{1,0:T(8,128)} %shard_map.71.refs_0_), channel_id=1, source_target_pairs={{0,80},{1,81},{2,82},{3,83},{4,84},{5,85},{6,86},{7,87},{8,88},{9,... | collective-permute-start | bytes 393224 | tf_op jit(solution)/shard_map/ppermute | solution.py:40
  129.1 4.7 %collective-permute-start.20 = (f32[128,256]{1,0:T(8,128)}, f32[128,256]{1,0:T(8,128)S(1)}, u32[]{:S(2)}, u32[]{:S(2)}) collective-permute-start(f32[128,256]{1,0:T(8,128)} %shard_map.71.refs_0_), channel_id=1, source_target_pairs={{0,96},{1,97},{2,98},{3,99},{4,100},{5,101},{6,102},{7,103},{8,104... | collective-permute-start | bytes 393224 | tf_op jit(solution)/shard_map/ppermute | solution.py:40
  133.8 3.3 %collective-permute-start.21 = (f32[128,256]{1,0:T(8,128)}, f32[128,256]{1,0:T(8,128)S(1)}, u32[]{:S(2)}, u32[]{:S(2)}) collective-permute-start(f32[128,256]{1,0:T(8,128)} %shard_map.71.refs_0_), channel_id=1, source_target_pairs={{0,112},{1,113},{2,114},{3,115},{4,116},{5,117},{6,118},{7,119},{8... | collective-permute-start | bytes 393224 | tf_op jit(solution)/shard_map/ppermute | solution.py:40
  138.0 1.3 collective-permute-done.21.refs_7_
  139.4 5.3 %collective-permute-start.22 = (f32[8,64,256]{2,1,0:T(8,128)S(1)}, f32[8,64,256]{2,1,0:T(8,128)S(1)}, u32[]{:S(2)}, u32[]{:S(2)}) collective-permute-start(f32[8,64,256]{2,1,0:T(8,128)S(1)} %pad_maximum_fusion.1.refs_9_.refs_1_), channel_id=1, source_target_pairs={{0,1},{1,0},{2,3},{3,2},{4,5},{5,4},{6,7},{7,6},{8,9},{9,8},{10,11... | collective-permute-start | bytes 1572872 | tf_op jit(solution)/shard_map/ppermute | solution.py:40
  144.7 1.5 collective-permute-done.22.refs_10_.refs_2_
  147.1 4.1 %shard_map.72 = f32[128,256]{1,0:T(8,128)} custom-call(s32[4]{0:T(128)} %pad_add_fusion.place, f32[128,256]{1,0:T(8,128)} %shard_map.71.refs_0_, f32[128,256]{1,0:T(8,128)} %copy-done.10, f32[128,256]{1,0:T(8,128)} %copy-done.11, f32[128,256]{1,0:T(8,128)} %copy-done.12, f32[128,256]{1,0:T(8,128)} %copy-done.13, f32[128,256]{1,0:T(8,128)} %copy-done.14, ...), custom_call_target="tpu_custom_call" | custom-call | tf_op jit(solution)/shard_map/pallas_call | solution.py:235
  151.7 1.1 copy.11.scale_ref
  154.2 17.5 %shard_map.73 = (bf16[4,1024,1024]{2,1,0:T(8,128)(2,1)}, bf16[4,1024,1024]{2,1,0:T(8,128)(2,1)}) custom-call(bf16[4096,1024]{1,0:T(8,128)(2,1)} %all-gather.4.cloned.1.call-done.train_ref, bf16[1024,1024]{1,0:T(8,128)(2,1)} %cand_ref.1, f32[1024,1]{1,0:T(8,128)} %copy.11.scale_ref), custom_call_target="tpu_custom_call" | custom-call | flops 17179869184 | bytes 25165824 | tf_op jit(solution)/shard_map/pallas_call | solution.py:266
  171.8 9.0 %shard_map.74.refs_1_ = f32[1024,256]{1,0:T(8,128)} custom-call(s32[2]{0:T(128)} %pad_add_fusion.1.sup, s32[4]{0:T(128)} %pad_add_fusion.place, f32[1024,1024]{1,0:T(8,128)} %shard_map.68.st.refs_8_.refs_0_, f32[8,64,256]{2,1,0:T(8,128)} %copy-done.1, f32[8,64,256]{2,1,0:T(8,128)} %copy-done.2, ...), custom_call_target="tpu_custom_call" | custom-call | flops 6442450944 | bytes 8388608 | tf_op jit(solution)/shard_map/pallas_call | solution.py:332
  180.8 6.6 %all-gather.6.cloned.1.call-done = f32[2048,256]{1,0:T(8,128)} async-done(((f32[128,256]{1,0:T(8,128)}), f32[2048,256]{1,0:T(8,128)}) %all-gather.6.cloned.1.call-update) | async-done | bytes 2097168 | tf_op jit(solution)/shard_map/all_gather | solution.py:381
  187.9 9.3 %shard_map.75 = (f32[256,1024]{1,0:T(8,128)}, f32[1,1024]{1,0:T(1,128)}) custom-call(s32[2]{0:T(128)} %iota.3.sup, s32[4]{0:T(128)} %pad_add_fusion.place, f32[16,128,256]{2,1,0:T(8,128)} %bitcast.13, f32[1024,256]{1,0:T(8,128)} %shard_map.74.refs_1_, bf16[4,1024,1024]{2,1,0:T(8,128)(2,1)} %get-tuple-element.44.refs_3_.refs_5_.refs_2_.refs_4_, ...), custom_call_target="tpu_custom_call" | custom-call | flops 6442450944 | bytes 8388608 | tf_op jit(solution)/shard_map/pallas_call | solution.py:332
  197.9 12.8 %all_to_all.6 = f32[16,1,1024]{2,1,0:T(1,128)S(1)} all-to-all(f32[16,1,1024]{2,1,0:T(1,128)S(1)} %broadcast_in_dim.10), channel_id=1, replica_groups=mesh['chain'=16,'z'=8,'c'=2] {'chain'}, dimensions={0} | all-to-all | bytes 131072 | tf_op jit(solution)/shard_map/all_to_all | solution.py:390
  (72 shorter events, 12.5 us)
Async XLA Ops:
  7.2 147.1 %all-gather.4.cloned.1.call-start = ((), (), s32[]{:S(2)}) async-start(), calls=%async_computation.1 | async-start | bytes 8421376 | tf_op jit(solution)/shard_map/all_gather | solution.py:359
  7.9 179.5 %all-gather.6.cloned.1.call-start = ((), (), s32[]{:S(2)}) async-start(), calls=%async_computation.2 | async-start | bytes 2228224 | tf_op jit(solution)/shard_map/all_gather | solution.py:381
  10.2 14.6 %collective-permute-start = (f32[512,256]{1,0:T(8,128)S(1)}, f32[512,256]{1,0:T(8,128)S(1)}, u32[]{:S(2)}, u32[]{:S(2)}) collective-permute-start(f32[512,256]{1,0:T(8,128)S(1)} %maximum_select_fusion), channel_id=1, source_target_pairs={{0,16},{2,18},{4,20},{6,22},{8,24},{10,26},{12,28},{14,30},{16,32}... | collective-permute-start | bytes 1572872 | tf_op jit(solution)/shard_map/ppermute | solution.py:40
  11.5 27.9 %collective-permute-start.1 = (f32[512,256]{1,0:T(8,128)S(1)}, f32[512,256]{1,0:T(8,128)S(1)}, u32[]{:S(2)}, u32[]{:S(2)}) collective-permute-start(f32[512,256]{1,0:T(8,128)S(1)} %maximum_select_fusion), channel_id=1, source_target_pairs={{0,32},{2,34},{4,36},{6,38},{8,40},{10,42},{12,44},{14,46},{16,48}... | collective-permute-start | bytes 1572872 | tf_op jit(solution)/shard_map/ppermute | solution.py:40
  12.8 26.6 %collective-permute-start.2 = (f32[512,256]{1,0:T(8,128)S(1)}, f32[512,256]{1,0:T(8,128)S(1)}, u32[]{:S(2)}, u32[]{:S(2)}) collective-permute-start(f32[512,256]{1,0:T(8,128)S(1)} %maximum_select_fusion), channel_id=1, source_target_pairs={{0,48},{2,50},{4,52},{6,54},{8,56},{10,58},{12,60},{14,62},{16,0},... | collective-permute-start | bytes 1572872 | tf_op jit(solution)/shard_map/ppermute | solution.py:40
  39.5 4.7 %copy-start = (f32[3,512,256]{2,1,0:T(8,128)}, f32[3,512,256]{2,1,0:T(8,128)S(1)}, u32[]{:S(2)}) copy-start(f32[3,512,256]{2,1,0:T(8,128)S(1)} %pad_maximum_fusion.near) | copy-start | bytes 4718596
  39.5 4.7 %collective-permute-start.3 = (f32[3,512,256]{2,1,0:T(8,128)S(1)}, f32[3,512,256]{2,1,0:T(8,128)S(1)}, u32[]{:S(2)}, u32[]{:S(2)}) collective-permute-start(f32[3,512,256]{2,1,0:T(8,128)S(1)} %pad_maximum_fusion.near), channel_id=1, source_target_pairs={{0,1},{1,0},{2,3},{3,2},{4,5},{5,4},{6,7},{7,6},{8,9},{9,8},{10,11... | collective-permute-start | bytes 4718600 | tf_op jit(solution)/shard_map/ppermute | solution.py:40
  44.2 1.1 copy-start.4
  54.1 9.1 %collective-permute-start.4 = (f32[64,1024]{1,0:T(8,128)S(1)}, f32[64,1024]{1,0:T(8,128)S(1)}, u32[]{:S(2)}, u32[]{:S(2)}) collective-permute-start(f32[64,1024]{1,0:T(8,128)S(1)} %constant_dynamic-slice_fusion.3), channel_id=1, source_target_pairs={{0,64},{1,65},{2,66},{3,67},{4,68},{5,69},{6,70},{7,71},{8,72},{9,... | collective-permute-start | bytes 786440 | tf_op jit(solution)/shard_map/ppermute | solution.py:40
  57.3 11.4 %collective-permute-start.5 = (f32[64,1024]{1,0:T(8,128)S(1)}, f32[64,1024]{1,0:T(8,128)S(1)}, u32[]{:S(2)}, u32[]{:S(2)}) collective-permute-start(f32[64,1024]{1,0:T(8,128)S(1)} %constant_dynamic-slice_fusion.3), channel_id=1, source_target_pairs={{0,128},{1,129},{2,130},{3,131},{4,132},{5,133},{6,134},{7,135},{8... | collective-permute-start | bytes 786440 | tf_op jit(solution)/shard_map/ppermute | solution.py:40
  61.9 11.1 %collective-permute-start.6 = (f32[64,1024]{1,0:T(8,128)S(1)}, f32[64,1024]{1,0:T(8,128)S(1)}, u32[]{:S(2)}, u32[]{:S(2)}) collective-permute-start(f32[64,1024]{1,0:T(8,128)S(1)} %constant_dynamic-slice_fusion.3), channel_id=1, source_target_pairs={{0,192},{1,193},{2,194},{3,195},{4,196},{5,197},{6,198},{7,199},{8... | collective-permute-start | bytes 786440 | tf_op jit(solution)/shard_map/ppermute | solution.py:40
  63.2 0.7 copy-start.9
  68.7 32.0 %copy-start.5 = (f32[64,1024]{1,0:T(8,128)}, f32[64,1024]{1,0:T(8,128)S(1)}, u32[]{:S(2)}) copy-start(f32[64,1024]{1,0:T(8,128)S(1)} %collective-permute-done.5.s2) | copy-start | bytes 786436
  72.9 27.8 %copy-start.6 = (f32[64,1024]{1,0:T(8,128)}, f32[64,1024]{1,0:T(8,128)S(1)}, u32[]{:S(2)}) copy-start(f32[64,1024]{1,0:T(8,128)S(1)} %collective-permute-done.6.s3) | copy-start | bytes 786436
  72.9 4.9 %collective-permute-start.7 = (f32[64,256]{1,0:T(8,128)}, f32[64,256]{1,0:T(8,128)S(1)}, u32[]{:S(2)}, u32[]{:S(2)}) collective-permute-start(f32[64,256]{1,0:T(8,128)} %shard_map.69.t0.t1), channel_id=1, source_target_pairs={{0,16},{1,17},{2,18},{3,19},{4,20},{5,21},{6,22},{7,23},{8,24},{9,... | collective-permute-start | bytes 196616 | tf_op jit(solution)/shard_map/ppermute | solution.py:40
  74.1 4.9 %collective-permute-start.8 = (f32[64,256]{1,0:T(8,128)}, f32[64,256]{1,0:T(8,128)S(1)}, u32[]{:S(2)}, u32[]{:S(2)}) collective-permute-start(f32[64,256]{1,0:T(8,128)} %shard_map.69.t0.t1), channel_id=1, source_target_pairs={{0,32},{1,33},{2,34},{3,35},{4,36},{5,37},{6,38},{7,39},{8,40},{9,... | collective-permute-start | bytes 196616 | tf_op jit(solution)/shard_map/ppermute | solution.py:40
  74.8 5.3 %collective-permute-start.9 = (f32[64,256]{1,0:T(8,128)}, f32[64,256]{1,0:T(8,128)S(1)}, u32[]{:S(2)}, u32[]{:S(2)}) collective-permute-start(f32[64,256]{1,0:T(8,128)} %shard_map.69.t0.t1), channel_id=1, source_target_pairs={{0,48},{1,49},{2,50},{3,51},{4,52},{5,53},{6,54},{7,55},{8,56},{9,... | collective-permute-start | bytes 196616 | tf_op jit(solution)/shard_map/ppermute | solution.py:40
  77.8 2.3 %copy-start.17 = (f32[64,256]{1,0:T(8,128)}, f32[64,256]{1,0:T(8,128)S(1)}, u32[]{:S(2)}) copy-start(f32[64,256]{1,0:T(8,128)S(1)} %collective-permute-done.7.t1) | copy-start | bytes 196612
  79.1 1.0 copy-start.18
  80.1 0.6 copy-start.19
  84.7 12.9 %collective-permute-start.11 = (f32[64,1024]{1,0:T(8,128)}, f32[64,1024]{1,0:T(8,128)S(1)}, u32[]{:S(2)}, u32[]{:S(2)}) collective-permute-start(f32[64,1024]{1,0:T(8,128)} %get-tuple-element.27), channel_id=1, source_target_pairs={{0,64},{1,65},{2,66},{3,67},{4,68},{5,69},{6,70},{7,71},{8,72},{9,... | collective-permute-start | bytes 786440 | tf_op jit(solution)/shard_map/ppermute | solution.py:40
  86.0 11.6 %collective-permute-start.12 = (f32[64,1024]{1,0:T(8,128)}, f32[64,1024]{1,0:T(8,128)S(1)}, u32[]{:S(2)}, u32[]{:S(2)}) collective-permute-start(f32[64,1024]{1,0:T(8,128)} %get-tuple-element.27), channel_id=1, source_target_pairs={{0,128},{1,129},{2,130},{3,131},{4,132},{5,133},{6,134},{7,135},{8... | collective-permute-start | bytes 786440 | tf_op jit(solution)/shard_map/ppermute | solution.py:40
  93.0 3.8 %collective-permute-start.10 = (f32[1,64,256]{2,1,0:T(8,128)}, f32[1,64,256]{2,1,0:T(8,128)S(1)}, u32[]{:S(2)}, u32[]{:S(2)}) collective-permute-start(f32[1,64,256]{2,1,0:T(8,128)} %bitcast.17), channel_id=1, source_target_pairs={{0,2},{1,3},{2,0},{3,1},{4,6},{5,7},{6,4},{7,5},{8,10},{9,11},{10,... | collective-permute-start | bytes 196616 | tf_op jit(solution)/shard_map/ppermute | solution.py:40
  97.6 3.1 %copy-start.7 = (f32[64,1024]{1,0:T(8,128)}, f32[64,1024]{1,0:T(8,128)S(1)}, u32[]{:S(2)}) copy-start(f32[64,1024]{1,0:T(8,128)S(1)} %collective-permute-done.11.m1) | copy-start | bytes 786436
  97.6 3.1 %copy-start.8 = (f32[64,1024]{1,0:T(8,128)}, f32[64,1024]{1,0:T(8,128)S(1)}, u32[]{:S(2)}) copy-start(f32[64,1024]{1,0:T(8,128)S(1)} %collective-permute-done.12.m2) | copy-start | bytes 786436
  97.6 11.9 %collective-permute-start.13 = (f32[2,64,256]{2,1,0:T(8,128)S(1)}, f32[2,64,256]{2,1,0:T(8,128)S(1)}, u32[]{:S(2)}, u32[]{:S(2)}) collective-permute-start(f32[2,64,256]{2,1,0:T(8,128)S(1)} %pad_maximum_fusion.3), channel_id=1, source_target_pairs={{0,4},{1,5},{2,6},{3,7},{4,0},{5,1},{6,2},{7,3},{8,12},{9,13},{10,... | collective-permute-start | bytes 393224 | tf_op jit(solution)/shard_map/ppermute | solution.py:40
  104.8 46.4 %copy-start.3 = (bf16[1024,1024]{1,0:T(8,128)(2,1)S(1)}, bf16[1024,1024]{1,0:T(8,128)(2,1)}, u32[]{:S(2)}) copy-start(bf16[1024,1024]{1,0:T(8,128)(2,1)} %cand_ref.1) | copy-start | bytes 6291460
  104.8 7.3 %collective-permute-start.14 = (f32[128,256]{1,0:T(8,128)}, f32[128,256]{1,0:T(8,128)S(1)}, u32[]{:S(2)}, u32[]{:S(2)}) collective-permute-start(f32[128,256]{1,0:T(8,128)} %shard_map.71.refs_0_), channel_id=1, source_target_pairs={{0,16},{1,17},{2,18},{3,19},{4,20},{5,21},{6,22},{7,23},{8,24},{9,... | collective-permute-start | bytes 393224 | tf_op jit(solution)/shard_map/ppermute | solution.py:40
  107.0 9.3 %collective-permute-start.15 = (f32[128,256]{1,0:T(8,128)}, f32[128,256]{1,0:T(8,128)S(1)}, u32[]{:S(2)}, u32[]{:S(2)}) collective-permute-start(f32[128,256]{1,0:T(8,128)} %shard_map.71.refs_0_), channel_id=1, source_target_pairs={{0,32},{1,33},{2,34},{3,35},{4,36},{5,37},{6,38},{7,39},{8,40},{9,... | collective-permute-start | bytes 393224 | tf_op jit(solution)/shard_map/ppermute | solution.py:40
  107.9 9.5 %collective-permute-start.16 = (f32[128,256]{1,0:T(8,128)}, f32[128,256]{1,0:T(8,128)S(1)}, u32[]{:S(2)}, u32[]{:S(2)}) collective-permute-start(f32[128,256]{1,0:T(8,128)} %shard_map.71.refs_0_), channel_id=1, source_target_pairs={{0,48},{1,49},{2,50},{3,51},{4,52},{5,53},{6,54},{7,55},{8,56},{9,... | collective-permute-start | bytes 393224 | tf_op jit(solution)/shard_map/ppermute | solution.py:40
  112.1 34.1 %copy-start.10 = (f32[128,256]{1,0:T(8,128)}, f32[128,256]{1,0:T(8,128)S(1)}, u32[]{:S(2)}) copy-start(f32[128,256]{1,0:T(8,128)S(1)} %collective-permute-done.14.refs_1_) | copy-start | bytes 393220
  116.3 29.9 %copy-start.11 = (f32[128,256]{1,0:T(8,128)}, f32[128,256]{1,0:T(8,128)S(1)}, u32[]{:S(2)}) copy-start(f32[128,256]{1,0:T(8,128)S(1)} %collective-permute-done.15.refs_2_) | copy-start | bytes 393220
  117.4 28.8 %copy-start.12 = (f32[128,256]{1,0:T(8,128)}, f32[128,256]{1,0:T(8,128)S(1)}, u32[]{:S(2)}) copy-start(f32[128,256]{1,0:T(8,128)S(1)} %collective-permute-done.16.refs_3_) | copy-start | bytes 393220
  117.4 20.5 %collective-permute-start.17 = (f32[4,64,256]{2,1,0:T(8,128)S(1)}, f32[4,64,256]{2,1,0:T(8,128)S(1)}, u32[]{:S(2)}, u32[]{:S(2)}) collective-permute-start(f32[4,64,256]{2,1,0:T(8,128)S(1)} %pad_maximum_fusion.2), channel_id=1, source_target_pairs={{0,8},{1,9},{2,10},{3,11},{4,12},{5,13},{6,14},{7,15},{8,0},{9,1},... | collective-permute-start | bytes 786440 | tf_op jit(solution)/shard_map/ppermute | solution.py:40
  124.2 13.8 %collective-permute-start.18 = (f32[128,256]{1,0:T(8,128)}, f32[128,256]{1,0:T(8,128)S(1)}, u32[]{:S(2)}, u32[]{:S(2)}) collective-permute-start(f32[128,256]{1,0:T(8,128)} %shard_map.71.refs_0_), channel_id=1, source_target_pairs={{0,64},{1,65},{2,66},{3,67},{4,68},{5,69},{6,70},{7,71},{8,72},{9,... | collective-permute-start | bytes 393224 | tf_op jit(solution)/shard_map/ppermute | solution.py:40
  125.5 12.5 %collective-permute-start.19 = (f32[128,256]{1,0:T(8,128)}, f32[128,256]{1,0:T(8,128)S(1)}, u32[]{:S(2)}, u32[]{:S(2)}) collective-permute-start(f32[128,256]{1,0:T(8,128)} %shard_map.71.refs_0_), channel_id=1, source_target_pairs={{0,80},{1,81},{2,82},{3,83},{4,84},{5,85},{6,86},{7,87},{8,88},{9,... | collective-permute-start | bytes 393224 | tf_op jit(solution)/shard_map/ppermute | solution.py:40
  129.1 9.0 %collective-permute-start.20 = (f32[128,256]{1,0:T(8,128)}, f32[128,256]{1,0:T(8,128)S(1)}, u32[]{:S(2)}, u32[]{:S(2)}) collective-permute-start(f32[128,256]{1,0:T(8,128)} %shard_map.71.refs_0_), channel_id=1, source_target_pairs={{0,96},{1,97},{2,98},{3,99},{4,100},{5,101},{6,102},{7,103},{8,104... | collective-permute-start | bytes 393224 | tf_op jit(solution)/shard_map/ppermute | solution.py:40
  133.8 5.6 %collective-permute-start.21 = (f32[128,256]{1,0:T(8,128)}, f32[128,256]{1,0:T(8,128)S(1)}, u32[]{:S(2)}, u32[]{:S(2)}) collective-permute-start(f32[128,256]{1,0:T(8,128)} %shard_map.71.refs_0_), channel_id=1, source_target_pairs={{0,112},{1,113},{2,114},{3,115},{4,116},{5,117},{6,118},{7,119},{8... | collective-permute-start | bytes 393224 | tf_op jit(solution)/shard_map/ppermute | solution.py:40
  138.0 8.3 %copy-start.1 = (f32[8,64,256]{2,1,0:T(8,128)}, f32[8,64,256]{2,1,0:T(8,128)S(1)}, u32[]{:S(2)}) copy-start(f32[8,64,256]{2,1,0:T(8,128)S(1)} %pad_maximum_fusion.1.refs_9_.refs_1_) | copy-start | bytes 1572868
  138.0 14.8 %copy-start.20 = (f32[256]{0:T(256)S(1)}, f32[256]{0:T(256)}, u32[]{:S(2)}) copy-start(f32[256]{0:T(256)} %param.9) | copy-start | bytes 3076
  138.0 8.2 %copy-start.13 = (f32[128,256]{1,0:T(8,128)}, f32[128,256]{1,0:T(8,128)S(1)}, u32[]{:S(2)}) copy-start(f32[128,256]{1,0:T(8,128)S(1)} %collective-permute-done.18.refs_4_) | copy-start | bytes 393220
  138.0 8.2 %copy-start.14 = (f32[128,256]{1,0:T(8,128)}, f32[128,256]{1,0:T(8,128)S(1)}, u32[]{:S(2)}) copy-start(f32[128,256]{1,0:T(8,128)S(1)} %collective-permute-done.19.refs_5_) | copy-start | bytes 393220
  138.0 8.2 %copy-start.15 = (f32[128,256]{1,0:T(8,128)}, f32[128,256]{1,0:T(8,128)S(1)}, u32[]{:S(2)}) copy-start(f32[128,256]{1,0:T(8,128)S(1)} %collective-permute-done.20.refs_6_) | copy-start | bytes 393220
  139.4 6.9 %copy-start.16 = (f32[128,256]{1,0:T(8,128)}, f32[128,256]{1,0:T(8,128)S(1)}, u32[]{:S(2)}) copy-start(f32[128,256]{1,0:T(8,128)S(1)} %collective-permute-done.21.refs_7_) | copy-start | bytes 393220
  139.4 6.8 %collective-permute-start.22 = (f32[8,64,256]{2,1,0:T(8,128)S(1)}, f32[8,64,256]{2,1,0:T(8,128)S(1)}, u32[]{:S(2)}, u32[]{:S(2)}) collective-permute-start(f32[8,64,256]{2,1,0:T(8,128)S(1)} %pad_maximum_fusion.1.refs_9_.refs_1_), channel_id=1, source_target_pairs={{0,1},{1,0},{2,3},{3,2},{4,5},{5,4},{6,7},{7,6},{8,9},{9,8},{10,11... | collective-permute-start | bytes 1572872 | tf_op jit(solution)/shard_map/ppermute | solution.py:40
  146.3 0.8 copy-start.2
Sparse Core Ops, SparseCore 0:
  11.7 128.5 all-gather.3
  151.3 36.0 all-gather.5

commit v5 on v4

--- a/solution.py
+++ b/solution.py
@@ -98,7 +98,6 @@
             d[at], f[at, 0] = far[k - 1, :bs], far[k - 1, bs:]
             f[at, 1], f[at, 2] = near[k - 1, :bs], near[k - 1, bs:]
 
-    out_ref[...] = jnp.zeros_like(out_ref)
     columns = []
     for i in range(SIDE):
         above = []
@@ -115,18 +114,31 @@
             column = jnp.concatenate([-nt(jnp.concatenate(above, 0), d[i]), column], 0)
         columns.append(column)
         out_ref[: (i + 1) * bs, i * bs : (i + 1) * bs] = column
-
-
-def diagonal(place, d, f, near, far):
+        if i < SIDE - 1:
+            out_ref[(i + 1) * bs :, i * bs : (i + 1) * bs] = jnp.zeros(((SIDE - 1 - i) * bs, bs), F32)
+
+
+def diagonal(place, d, factor, near, far):
     bs = d.shape[0]
+    size = SIDE * bs
+    fixed = lambda shape: pl.BlockSpec(shape, lambda i, p: (0,) * len(shape))
     return pl.pallas_call(
         diagonal_kernel,
-        in_specs=[SMEM] + [VMEM] * 4,
-        out_specs=VMEM,
-        out_shape=jax.ShapeDtypeStruct((SIDE * bs, SIDE * bs), F32),
-        scratch_shapes=[pltpu.VMEM((SIDE, bs, bs), F32), pltpu.VMEM((SIDE, 3, bs, bs), F32)],
-        compiler_params=PARAMS,
-    )(place, d, f, near, far)
+        grid_spec=pltpu.PrefetchScalarGridSpec(
+            num_scalar_prefetch=1,
+            grid=(1,),
+            in_specs=[
+                fixed(d.shape),
+                pl.BlockSpec((bs, size), lambda i, p: (0, p[3])),
+                fixed(near.shape),
+                fixed(far.shape),
+            ],
+            out_specs=fixed((size, size)),
+            scratch_shapes=[pltpu.VMEM((SIDE, bs, bs), F32), pltpu.VMEM((SIDE, 3, bs, bs), F32)],
+        ),
+        out_shape=jax.ShapeDtypeStruct((size, size), F32),
+        compiler_params=PARAMS,
+    )(place, d, factor, near, far)
 
 
 def first_factor_kernel(place, s_ref, f_ref, out_ref):
@@ -365,7 +377,7 @@
     near = jnp.stack(
         [send(pair, lambda y, x, z, c: (y, (x + k) % SIDE, z, c) if c == 0 or x >= 2 else None) for k in (1, 2, 3)]
     )
-    st = diagonal(place, diag_inverse, square, near, swap_core(near))
+    st = diagonal(place, diag_inverse, factor, near, swap_core(near))
 
     m = size // (2 * ZS)
     sl = lax.dynamic_slice(st, (group * m, 0), (m, size))

time: 219 us -> 220 us (level)
  waiting for transfers between devices: 55.7 us -> 58.2 us
  local copies, waits for them, and re-layouts: 10.9 us -> 8.57 us
    ppermute x23, waiting for transfers between devices: 48.5 us -> 51.2 us  [send(): return lax.ppermute(value, AXES, moves(target))]
    dynamic_slice x1 -> x0, local copies, waits for them, and re-layouts: 2.31 us -> none  [shards(): square = lax.dynamic_slice(factor, (0, y * size), (bs, size))]
  transfers between devices with their start and end apart: 25 -> 25, of which waited for: 16 -> 14; matrix products, arithmetic and copies ran while one was open for 5% -> 4% of each run, Pallas kernels for 23% -> 23%
where the time goes in v5:
time: 220 us; the launch traced here: 219 us
  starting transfers between devices  60.4 us (27%)
  Pallas kernels  59.8 us (27%)
  waiting for transfers between devices  58.2 us (26%)
  between operations  14.4 us (7%)
  blocking collectives  12.8 us (6%)
  local copies, waits for them, and re-layouts  8.57 us (4%)
  other arithmetic  4.43 us (2%)
    ppermute x23, starting transfers between devices, send(): return lax.ppermute(value, AXES, moves(target))  60.4 us
    ppermute x23, waiting for transfers between devices, send(): return lax.ppermute(value, AXES, moves(target))  51.2 us
    pallas_call x2, Pallas kernels, apply(): pl.pallas_call(functools.partial(apply_kernel, last), grid_spec=pltpu.Pre...  18.3 us
    pallas_call x1, Pallas kernels, make_panel(): pl.pallas_call(functools.partial(panel_kernel, 0.5 * math.sqrt(e)), grid=...  17.5 us
    all_to_all x1, blocking collectives, shards(): lax.all_to_all(jnp.broadcast_to(mean, (CHAIN, n)), 'chain', 0, 0, tiled=T...  12.8 us
    pallas_call x1, Pallas kernels, diagonal(): pl.pallas_call(diagonal_kernel, grid_spec=pltpu.PrefetchScalarGridSpec(nu...  8.42 us
    all_gather x1, waiting for transfers between devices, shards(): m2_full = lax.all_gather(m2, ('z', 'c'), axis=0)  6.28 us
  transfers between devices with their start and end apart: 25, of which 14 were waited for; matrix products, arithmetic and copies ran while one was open for 4% of the time, Pallas kernels for 23%

profile of v5, /device:TPU:1, one launch (start us, length us, event | category | flops | bytes accessed | tf_op | source)
XLA Modules:
  0.0 218.6 jit_solution(334993647468817286)
XLA Ops:
  8.0 1.2 constant_dynamic-slice_fusion
  9.1 1.0 maximum_select_fusion
  10.2 1.3 collective-permute-start
  11.5 1.3 collective-permute-start.1
  13.5 11.3 %collective-permute-done = f32[512,256]{1,0:T(8,128)S(1)} collective-permute-done((f32[512,256]{1,0:T(8,128)S(1)}, f32[512,256]{1,0:T(8,128)S(1)}, u32[]{:S(2)}, u32[]{:S(2)}) %collective-permute-start) | collective-permute-done | bytes 524320 | tf_op jit(solution)/shard_map/ppermute | solution.py:40
  24.7 14.6 %collective-permute-done.1 = f32[512,256]{1,0:T(8,128)S(1)} collective-permute-done((f32[512,256]{1,0:T(8,128)S(1)}, f32[512,256]{1,0:T(8,128)S(1)}, u32[]{:S(2)}, u32[]{:S(2)}) %collective-permute-start.1) | collective-permute-done | bytes 524320 | tf_op jit(solution)/shard_map/ppermute | solution.py:40
  39.5 1.6 collective-permute-start.3
  41.7 2.4 %collective-permute-done.3.far = f32[3,512,256]{2,1,0:T(8,128)S(1)} collective-permute-done((f32[3,512,256]{2,1,0:T(8,128)S(1)}, f32[3,512,256]{2,1,0:T(8,128)S(1)}, u32[]{:S(2)}, u32[]{:S(2)}) %collective-permute-start.3) | collective-permute-done | bytes 1572896 | tf_op jit(solution)/shard_map/ppermute | solution.py:40
  44.2 1.1 copy-done.4
  45.3 8.4 %shard_map.68.st.refs_8_.refs_0_ = f32[1024,1024]{1,0:T(8,128)} custom-call(s32[4]{0:T(128)} %pad_add_fusion.place, f32[256,256]{1,0:T(8,128)} %d_ref.1, f32[256,4096]{1,0:T(8,128)} %f_ref.5, f32[3,512,256]{2,1,0:T(8,128)} %copy-done, f32[3,512,256]{2,1,0:T(8,128)} %copy-done.4), custom_call_target="tpu_custom_call" | custom-call | tf_op jit(solution)/shard_map/pallas_call | solution.py:125
  53.7 1.0 constant_dynamic-slice_fusion.2
  54.7 3.2 %collective-permute-start.4 = (f32[64,1024]{1,0:T(8,128)S(1)}, f32[64,1024]{1,0:T(8,128)S(1)}, u32[]{:S(2)}, u32[]{:S(2)}) collective-permute-start(f32[64,1024]{1,0:T(8,128)S(1)} %constant_dynamic-slice_fusion.2), channel_id=1, source_target_pairs={{0,64},{1,65},{2,66},{3,67},{4,68},{5,69},{6,70},{7,71},{8,72},{9,... | collective-permute-start | bytes 786440 | tf_op jit(solution)/shard_map/ppermute | solution.py:40
  57.9 4.5 %collective-permute-start.5 = (f32[64,1024]{1,0:T(8,128)S(1)}, f32[64,1024]{1,0:T(8,128)S(1)}, u32[]{:S(2)}, u32[]{:S(2)}) collective-permute-start(f32[64,1024]{1,0:T(8,128)S(1)} %constant_dynamic-slice_fusion.2), channel_id=1, source_target_pairs={{0,128},{1,129},{2,130},{3,131},{4,132},{5,133},{6,134},{7,135},{8... | collective-permute-start | bytes 786440 | tf_op jit(solution)/shard_map/ppermute | solution.py:40
  62.5 1.3 collective-permute-start.6
  64.5 3.2 %shard_map.69.t0.t1 = f32[64,256]{1,0:T(8,128)} custom-call(s32[4]{0:T(128)} %pad_add_fusion.place, f32[64,1024]{1,0:T(8,128)} %copy-done.9, f32[256,4096]{1,0:T(8,128)} %f_ref.5), custom_call_target="tpu_custom_call" | custom-call | tf_op jit(solution)/shard_map/pallas_call | solution.py:151
  67.7 1.6 collective-permute-done.5.s2
  69.3 4.3 %collective-permute-done.6.s3 = f32[64,1024]{1,0:T(8,128)S(1)} collective-permute-done((f32[64,1024]{1,0:T(8,128)S(1)}, f32[64,1024]{1,0:T(8,128)S(1)}, u32[]{:S(2)}, u32[]{:S(2)}) %collective-permute-start.6) | collective-permute-done | bytes 262176 | tf_op jit(solution)/shard_map/ppermute | solution.py:40
  73.5 1.2 collective-permute-start.7
  75.4 2.1 collective-permute-start.9
  78.3 1.4 collective-permute-done.8.t2
  79.7 1.1 collective-permute-done.9.t3
  81.4 4.0 %shard_map.70 = (f32[64,1024]{1,0:T(8,128)}, f32[64,256]{1,0:T(8,128)}) custom-call(s32[4]{0:T(128)} %pad_add_fusion.place, f32[64,256]{1,0:T(8,128)} %shard_map.69.t0.t1, f32[64,256]{1,0:T(8,128)} %copy-done.17, f32[64,256]{1,0:T(8,128)} %copy-done.18, f32[64,256]{1,0:T(8,128)} %copy-done.19, f32[1024,1024]{1,0:T(8,128)} %shard_map.68.st.refs_8_.refs_0_), custom_call_target="tpu_custom_call" | custom-call | tf_op jit(solution)/shard_map/pallas_call | solution.py:182
  85.4 1.3 collective-permute-start.11
  86.7 7.2 %collective-permute-start.12 = (f32[64,1024]{1,0:T(8,128)}, f32[64,1024]{1,0:T(8,128)S(1)}, u32[]{:S(2)}, u32[]{:S(2)}) collective-permute-start(f32[64,1024]{1,0:T(8,128)} %get-tuple-element.27), channel_id=1, source_target_pairs={{0,128},{1,129},{2,130},{3,131},{4,132},{5,133},{6,134},{7,135},{8... | collective-permute-start | bytes 786440 | tf_op jit(solution)/shard_map/ppermute | solution.py:40
  94.0 1.6 collective-permute-start.10
  95.6 1.9 collective-permute-done.10
  98.4 2.8 %collective-permute-start.13 = (f32[2,64,256]{2,1,0:T(8,128)S(1)}, f32[2,64,256]{2,1,0:T(8,128)S(1)}, u32[]{:S(2)}, u32[]{:S(2)}) collective-permute-start(f32[2,64,256]{2,1,0:T(8,128)S(1)} %pad_maximum_fusion.3), channel_id=1, source_target_pairs={{0,4},{1,5},{2,6},{3,7},{4,0},{5,1},{6,2},{7,3},{8,12},{9,13},{10,... | collective-permute-start | bytes 393224 | tf_op jit(solution)/shard_map/ppermute | solution.py:40
  101.2 4.3 %shard_map.71.refs_0_ = f32[128,256]{1,0:T(8,128)} custom-call(s32[4]{0:T(128)} %pad_add_fusion.place, f32[64,1024]{1,0:T(8,128)} %copy-done.5, f32[64,1024]{1,0:T(8,128)} %copy-done.6, f32[64,1024]{1,0:T(8,128)} %copy-done.7, f32[64,1024]{1,0:T(8,128)} %copy-done.8, f32[64,256]{1,0:T(8,128)} %shard_map.69.t0.t1, f32[256,4096]{1,0:T(8,128)} %f_ref.5), custom_call_target="tpu_custom_call" | custom-call | tf_op jit(solution)/shard_map/pallas_call | solution.py:206
  105.5 1.7 collective-permute-start.14
  107.2 1.5 collective-permute-start.15
  108.7 0.9 collective-permute-start.16
  109.6 2.6 %collective-permute-done.14.refs_1_ = f32[128,256]{1,0:T(8,128)S(1)} collective-permute-done((f32[128,256]{1,0:T(8,128)}, f32[128,256]{1,0:T(8,128)S(1)}, u32[]{:S(2)}, u32[]{:S(2)}) %collective-permute-start.14) | collective-permute-done | bytes 131104 | tf_op jit(solution)/shard_map/ppermute | solution.py:40
  112.2 5.6 %collective-permute-done.15.refs_2_ = f32[128,256]{1,0:T(8,128)S(1)} collective-permute-done((f32[128,256]{1,0:T(8,128)}, f32[128,256]{1,0:T(8,128)S(1)}, u32[]{:S(2)}, u32[]{:S(2)}) %collective-permute-start.15) | collective-permute-done | bytes 131104 | tf_op jit(solution)/shard_map/ppermute | solution.py:40
  117.9 7.0 %collective-permute-start.17 = (f32[4,64,256]{2,1,0:T(8,128)S(1)}, f32[4,64,256]{2,1,0:T(8,128)S(1)}, u32[]{:S(2)}, u32[]{:S(2)}) collective-permute-start(f32[4,64,256]{2,1,0:T(8,128)S(1)} %pad_maximum_fusion.2), channel_id=1, source_target_pairs={{0,8},{1,9},{2,10},{3,11},{4,12},{5,13},{6,14},{7,15},{8,0},{9,1},... | collective-permute-start | bytes 786440 | tf_op jit(solution)/shard_map/ppermute | solution.py:40
  124.8 1.3 collective-permute-start.18
  126.1 4.0 %collective-permute-start.19 = (f32[128,256]{1,0:T(8,128)}, f32[128,256]{1,0:T(8,128)S(1)}, u32[]{:S(2)}, u32[]{:S(2)}) collective-permute-start(f32[128,256]{1,0:T(8,128)} %shard_map.71.refs_0_), channel_id=1, source_target_pairs={{0,80},{1,81},{2,82},{3,83},{4,84},{5,85},{6,86},{7,87},{8,88},{9,... | collective-permute-start | bytes 393224 | tf_op jit(solution)/shard_map/ppermute | solution.py:40
  130.1 4.9 %collective-permute-start.20 = (f32[128,256]{1,0:T(8,128)}, f32[128,256]{1,0:T(8,128)S(1)}, u32[]{:S(2)}, u32[]{:S(2)}) collective-permute-start(f32[128,256]{1,0:T(8,128)} %shard_map.71.refs_0_), channel_id=1, source_target_pairs={{0,96},{1,97},{2,98},{3,99},{4,100},{5,101},{6,102},{7,103},{8,104... | collective-permute-start | bytes 393224 | tf_op jit(solution)/shard_map/ppermute | solution.py:40
  135.0 3.0 %collective-permute-start.21 = (f32[128,256]{1,0:T(8,128)}, f32[128,256]{1,0:T(8,128)S(1)}, u32[]{:S(2)}, u32[]{:S(2)}) collective-permute-start(f32[128,256]{1,0:T(8,128)} %shard_map.71.refs_0_), channel_id=1, source_target_pairs={{0,112},{1,113},{2,114},{3,115},{4,116},{5,117},{6,118},{7,119},{8... | collective-permute-start | bytes 393224 | tf_op jit(solution)/shard_map/ppermute | solution.py:40
  138.2 2.1 collective-permute-done.21.refs_7_
  140.3 5.2 %collective-permute-start.22 = (f32[8,64,256]{2,1,0:T(8,128)S(1)}, f32[8,64,256]{2,1,0:T(8,128)S(1)}, u32[]{:S(2)}, u32[]{:S(2)}) collective-permute-start(f32[8,64,256]{2,1,0:T(8,128)S(1)} %pad_maximum_fusion.1.refs_9_.refs_1_), channel_id=1, source_target_pairs={{0,1},{1,0},{2,3},{3,2},{4,5},{5,4},{6,7},{7,6},{8,9},{9,8},{10,11... | collective-permute-start | bytes 1572872 | tf_op jit(solution)/shard_map/ppermute | solution.py:40
  145.5 1.5 collective-permute-done.22.refs_10_.refs_2_
  147.9 4.1 %shard_map.72 = f32[128,256]{1,0:T(8,128)} custom-call(s32[4]{0:T(128)} %pad_add_fusion.place, f32[128,256]{1,0:T(8,128)} %shard_map.71.refs_0_, f32[128,256]{1,0:T(8,128)} %copy-done.10, f32[128,256]{1,0:T(8,128)} %copy-done.11, f32[128,256]{1,0:T(8,128)} %copy-done.12, f32[128,256]{1,0:T(8,128)} %copy-done.13, f32[128,256]{1,0:T(8,128)} %copy-done.14, ...), custom_call_target="tpu_custom_call" | custom-call | tf_op jit(solution)/shard_map/pallas_call | solution.py:247
  152.5 1.1 copy.11.scale_ref
  155.0 17.5 %shard_map.73 = (bf16[4,1024,1024]{2,1,0:T(8,128)(2,1)}, bf16[4,1024,1024]{2,1,0:T(8,128)(2,1)}) custom-call(bf16[4096,1024]{1,0:T(8,128)(2,1)} %all-gather.4.cloned.1.call-done.train_ref, bf16[1024,1024]{1,0:T(8,128)(2,1)} %cand_ref.1, f32[1024,1]{1,0:T(8,128)} %copy.11.scale_ref), custom_call_target="tpu_custom_call" | custom-call | flops 17179869184 | bytes 25165824 | tf_op jit(solution)/shard_map/pallas_call | solution.py:278
  172.5 9.0 %shard_map.74.refs_1_ = f32[1024,256]{1,0:T(8,128)} custom-call(s32[2]{0:T(128)} %pad_add_fusion.1.sup, s32[4]{0:T(128)} %pad_add_fusion.place, f32[1024,1024]{1,0:T(8,128)} %shard_map.68.st.refs_8_.refs_0_, f32[8,64,256]{2,1,0:T(8,128)} %copy-done.1, f32[8,64,256]{2,1,0:T(8,128)} %copy-done.2, ...), custom_call_target="tpu_custom_call" | custom-call | flops 6442450944 | bytes 8388608 | tf_op jit(solution)/shard_map/pallas_call | solution.py:344
  181.6 6.3 %all-gather.6.cloned.1.call-done = f32[2048,256]{1,0:T(8,128)} async-done(((f32[128,256]{1,0:T(8,128)}), f32[2048,256]{1,0:T(8,128)}) %all-gather.6.cloned.1.call-update) | async-done | bytes 2097168 | tf_op jit(solution)/shard_map/all_gather | solution.py:393
  188.4 9.3 %shard_map.75 = (f32[256,1024]{1,0:T(8,128)}, f32[1,1024]{1,0:T(1,128)}) custom-call(s32[2]{0:T(128)} %iota.3.sup, s32[4]{0:T(128)} %pad_add_fusion.place, f32[16,128,256]{2,1,0:T(8,128)} %bitcast.13, f32[1024,256]{1,0:T(8,128)} %shard_map.74.refs_1_, bf16[4,1024,1024]{2,1,0:T(8,128)(2,1)} %get-tuple-element.44.refs_3_.refs_5_.refs_2_.refs_4_, ...), custom_call_target="tpu_custom_call" | custom-call | flops 6442450944 | bytes 8388608 | tf_op jit(solution)/shard_map/pallas_call | solution.py:344
  198.3 12.8 %all_to_all.6 = f32[16,1,1024]{2,1,0:T(1,128)S(1)} all-to-all(f32[16,1,1024]{2,1,0:T(1,128)S(1)} %broadcast_in_dim.10), channel_id=1, replica_groups=mesh['chain'=16,'z'=8,'c'=2] {'chain'}, dimensions={0} | all-to-all | bytes 131072 | tf_op jit(solution)/shard_map/all_to_all | solution.py:402
  (71 shorter events, 10.6 us)
Async XLA Ops:
  7.2 147.8 %all-gather.4.cloned.1.call-start = ((), (), s32[]{:S(2)}) async-start(), calls=%async_computation.1 | async-start | bytes 8421376 | tf_op jit(solution)/shard_map/all_gather | solution.py:371
  7.9 179.9 %all-gather.6.cloned.1.call-start = ((), (), s32[]{:S(2)}) async-start(), calls=%async_computation.2 | async-start | bytes 2228224 | tf_op jit(solution)/shard_map/all_gather | solution.py:393
  10.2 14.6 %collective-permute-start = (f32[512,256]{1,0:T(8,128)S(1)}, f32[512,256]{1,0:T(8,128)S(1)}, u32[]{:S(2)}, u32[]{:S(2)}) collective-permute-start(f32[512,256]{1,0:T(8,128)S(1)} %maximum_select_fusion), channel_id=1, source_target_pairs={{0,16},{2,18},{4,20},{6,22},{8,24},{10,26},{12,28},{14,30},{16,32}... | collective-permute-start | bytes 1572872 | tf_op jit(solution)/shard_map/ppermute | solution.py:40
  11.5 27.9 %collective-permute-start.1 = (f32[512,256]{1,0:T(8,128)S(1)}, f32[512,256]{1,0:T(8,128)S(1)}, u32[]{:S(2)}, u32[]{:S(2)}) collective-permute-start(f32[512,256]{1,0:T(8,128)S(1)} %maximum_select_fusion), channel_id=1, source_target_pairs={{0,32},{2,34},{4,36},{6,38},{8,40},{10,42},{12,44},{14,46},{16,48}... | collective-permute-start | bytes 1572872 | tf_op jit(solution)/shard_map/ppermute | solution.py:40
  12.8 26.6 %collective-permute-start.2 = (f32[512,256]{1,0:T(8,128)S(1)}, f32[512,256]{1,0:T(8,128)S(1)}, u32[]{:S(2)}, u32[]{:S(2)}) collective-permute-start(f32[512,256]{1,0:T(8,128)S(1)} %maximum_select_fusion), channel_id=1, source_target_pairs={{0,48},{2,50},{4,52},{6,54},{8,56},{10,58},{12,60},{14,62},{16,0},... | collective-permute-start | bytes 1572872 | tf_op jit(solution)/shard_map/ppermute | solution.py:40
  39.5 4.7 %copy-start = (f32[3,512,256]{2,1,0:T(8,128)}, f32[3,512,256]{2,1,0:T(8,128)S(1)}, u32[]{:S(2)}) copy-start(f32[3,512,256]{2,1,0:T(8,128)S(1)} %pad_maximum_fusion.near) | copy-start | bytes 4718596
  39.5 4.7 %collective-permute-start.3 = (f32[3,512,256]{2,1,0:T(8,128)S(1)}, f32[3,512,256]{2,1,0:T(8,128)S(1)}, u32[]{:S(2)}, u32[]{:S(2)}) collective-permute-start(f32[3,512,256]{2,1,0:T(8,128)S(1)} %pad_maximum_fusion.near), channel_id=1, source_target_pairs={{0,1},{1,0},{2,3},{3,2},{4,5},{5,4},{6,7},{7,6},{8,9},{9,8},{10,11... | collective-permute-start | bytes 4718600 | tf_op jit(solution)/shard_map/ppermute | solution.py:40
  44.2 1.1 copy-start.4
  54.7 9.1 %collective-permute-start.4 = (f32[64,1024]{1,0:T(8,128)S(1)}, f32[64,1024]{1,0:T(8,128)S(1)}, u32[]{:S(2)}, u32[]{:S(2)}) collective-permute-start(f32[64,1024]{1,0:T(8,128)S(1)} %constant_dynamic-slice_fusion.2), channel_id=1, source_target_pairs={{0,64},{1,65},{2,66},{3,67},{4,68},{5,69},{6,70},{7,71},{8,72},{9,... | collective-permute-start | bytes 786440 | tf_op jit(solution)/shard_map/ppermute | solution.py:40
  57.9 11.4 %collective-permute-start.5 = (f32[64,1024]{1,0:T(8,128)S(1)}, f32[64,1024]{1,0:T(8,128)S(1)}, u32[]{:S(2)}, u32[]{:S(2)}) collective-permute-start(f32[64,1024]{1,0:T(8,128)S(1)} %constant_dynamic-slice_fusion.2), channel_id=1, source_target_pairs={{0,128},{1,129},{2,130},{3,131},{4,132},{5,133},{6,134},{7,135},{8... | collective-permute-start | bytes 786440 | tf_op jit(solution)/shard_map/ppermute | solution.py:40
  62.5 11.1 %collective-permute-start.6 = (f32[64,1024]{1,0:T(8,128)S(1)}, f32[64,1024]{1,0:T(8,128)S(1)}, u32[]{:S(2)}, u32[]{:S(2)}) collective-permute-start(f32[64,1024]{1,0:T(8,128)S(1)} %constant_dynamic-slice_fusion.2), channel_id=1, source_target_pairs={{0,192},{1,193},{2,194},{3,195},{4,196},{5,197},{6,198},{7,199},{8... | collective-permute-start | bytes 786440 | tf_op jit(solution)/shard_map/ppermute | solution.py:40
  63.8 0.7 copy-start.9
  69.3 16.1 %copy-start.5 = (f32[64,1024]{1,0:T(8,128)}, f32[64,1024]{1,0:T(8,128)S(1)}, u32[]{:S(2)}) copy-start(f32[64,1024]{1,0:T(8,128)S(1)} %collective-permute-done.5.s2) | copy-start | bytes 786436
  73.5 11.9 %copy-start.6 = (f32[64,1024]{1,0:T(8,128)}, f32[64,1024]{1,0:T(8,128)S(1)}, u32[]{:S(2)}) copy-start(f32[64,1024]{1,0:T(8,128)S(1)} %collective-permute-done.6.s3) | copy-start | bytes 786436
  73.5 4.7 %collective-permute-start.7 = (f32[64,256]{1,0:T(8,128)}, f32[64,256]{1,0:T(8,128)S(1)}, u32[]{:S(2)}, u32[]{:S(2)}) collective-permute-start(f32[64,256]{1,0:T(8,128)} %shard_map.69.t0.t1), channel_id=1, source_target_pairs={{0,16},{1,17},{2,18},{3,19},{4,20},{5,21},{6,22},{7,23},{8,24},{9,... | collective-permute-start | bytes 196616 | tf_op jit(solution)/shard_map/ppermute | solution.py:40
  74.7 4.9 %collective-permute-start.8 = (f32[64,256]{1,0:T(8,128)}, f32[64,256]{1,0:T(8,128)S(1)}, u32[]{:S(2)}, u32[]{:S(2)}) collective-permute-start(f32[64,256]{1,0:T(8,128)} %shard_map.69.t0.t1), channel_id=1, source_target_pairs={{0,32},{1,33},{2,34},{3,35},{4,36},{5,37},{6,38},{7,39},{8,40},{9,... | collective-permute-start | bytes 196616 | tf_op jit(solution)/shard_map/ppermute | solution.py:40
  75.4 5.4 %collective-permute-start.9 = (f32[64,256]{1,0:T(8,128)}, f32[64,256]{1,0:T(8,128)S(1)}, u32[]{:S(2)}, u32[]{:S(2)}) collective-permute-start(f32[64,256]{1,0:T(8,128)} %shard_map.69.t0.t1), channel_id=1, source_target_pairs={{0,48},{1,49},{2,50},{3,51},{4,52},{5,53},{6,54},{7,55},{8,56},{9,... | collective-permute-start | bytes 196616 | tf_op jit(solution)/shard_map/ppermute | solution.py:40
  78.3 2.5 %copy-start.17 = (f32[64,256]{1,0:T(8,128)}, f32[64,256]{1,0:T(8,128)S(1)}, u32[]{:S(2)}) copy-start(f32[64,256]{1,0:T(8,128)S(1)} %collective-permute-done.7.t1) | copy-start | bytes 196612
  79.7 1.1 copy-start.18
  80.8 0.6 copy-start.19
  85.4 12.9 %collective-permute-start.11 = (f32[64,1024]{1,0:T(8,128)}, f32[64,1024]{1,0:T(8,128)S(1)}, u32[]{:S(2)}, u32[]{:S(2)}) collective-permute-start(f32[64,1024]{1,0:T(8,128)} %get-tuple-element.27), channel_id=1, source_target_pairs={{0,64},{1,65},{2,66},{3,67},{4,68},{5,69},{6,70},{7,71},{8,72},{9,... | collective-permute-start | bytes 786440 | tf_op jit(solution)/shard_map/ppermute | solution.py:40
  86.7 11.6 %collective-permute-start.12 = (f32[64,1024]{1,0:T(8,128)}, f32[64,1024]{1,0:T(8,128)S(1)}, u32[]{:S(2)}, u32[]{:S(2)}) collective-permute-start(f32[64,1024]{1,0:T(8,128)} %get-tuple-element.27), channel_id=1, source_target_pairs={{0,128},{1,129},{2,130},{3,131},{4,132},{5,133},{6,134},{7,135},{8... | collective-permute-start | bytes 786440 | tf_op jit(solution)/shard_map/ppermute | solution.py:40
  94.0 3.5 %collective-permute-start.10 = (f32[1,64,256]{2,1,0:T(8,128)}, f32[1,64,256]{2,1,0:T(8,128)S(1)}, u32[]{:S(2)}, u32[]{:S(2)}) collective-permute-start(f32[1,64,256]{2,1,0:T(8,128)} %bitcast.17), channel_id=1, source_target_pairs={{0,2},{1,3},{2,0},{3,1},{4,6},{5,7},{6,4},{7,5},{8,10},{9,11},{10,... | collective-permute-start | bytes 196616 | tf_op jit(solution)/shard_map/ppermute | solution.py:40
  98.3 2.9 %copy-start.7 = (f32[64,1024]{1,0:T(8,128)}, f32[64,1024]{1,0:T(8,128)S(1)}, u32[]{:S(2)}) copy-start(f32[64,1024]{1,0:T(8,128)S(1)} %collective-permute-done.11.m1) | copy-start | bytes 786436
  98.4 2.9 %copy-start.8 = (f32[64,1024]{1,0:T(8,128)}, f32[64,1024]{1,0:T(8,128)S(1)}, u32[]{:S(2)}) copy-start(f32[64,1024]{1,0:T(8,128)S(1)} %collective-permute-done.12.m2) | copy-start | bytes 786436
  98.4 11.3 %collective-permute-start.13 = (f32[2,64,256]{2,1,0:T(8,128)S(1)}, f32[2,64,256]{2,1,0:T(8,128)S(1)}, u32[]{:S(2)}, u32[]{:S(2)}) collective-permute-start(f32[2,64,256]{2,1,0:T(8,128)S(1)} %pad_maximum_fusion.3), channel_id=1, source_target_pairs={{0,4},{1,5},{2,6},{3,7},{4,0},{5,1},{6,2},{7,3},{8,12},{9,13},{10,... | collective-permute-start | bytes 393224 | tf_op jit(solution)/shard_map/ppermute | solution.py:40
  105.5 6.7 %collective-permute-start.14 = (f32[128,256]{1,0:T(8,128)}, f32[128,256]{1,0:T(8,128)S(1)}, u32[]{:S(2)}, u32[]{:S(2)}) collective-permute-start(f32[128,256]{1,0:T(8,128)} %shard_map.71.refs_0_), channel_id=1, source_target_pairs={{0,16},{1,17},{2,18},{3,19},{4,20},{5,21},{6,22},{7,23},{8,24},{9,... | collective-permute-start | bytes 393224 | tf_op jit(solution)/shard_map/ppermute | solution.py:40
  107.2 10.6 %collective-permute-start.15 = (f32[128,256]{1,0:T(8,128)}, f32[128,256]{1,0:T(8,128)S(1)}, u32[]{:S(2)}, u32[]{:S(2)}) collective-permute-start(f32[128,256]{1,0:T(8,128)} %shard_map.71.refs_0_), channel_id=1, source_target_pairs={{0,32},{1,33},{2,34},{3,35},{4,36},{5,37},{6,38},{7,39},{8,40},{9,... | collective-permute-start | bytes 393224 | tf_op jit(solution)/shard_map/ppermute | solution.py:40
  108.7 9.1 %collective-permute-start.16 = (f32[128,256]{1,0:T(8,128)}, f32[128,256]{1,0:T(8,128)S(1)}, u32[]{:S(2)}, u32[]{:S(2)}) collective-permute-start(f32[128,256]{1,0:T(8,128)} %shard_map.71.refs_0_), channel_id=1, source_target_pairs={{0,48},{1,49},{2,50},{3,51},{4,52},{5,53},{6,54},{7,55},{8,56},{9,... | collective-permute-start | bytes 393224 | tf_op jit(solution)/shard_map/ppermute | solution.py:40
  112.2 34.8 %copy-start.10 = (f32[128,256]{1,0:T(8,128)}, f32[128,256]{1,0:T(8,128)S(1)}, u32[]{:S(2)}) copy-start(f32[128,256]{1,0:T(8,128)S(1)} %collective-permute-done.14.refs_1_) | copy-start | bytes 393220
  117.9 29.1 %copy-start.11 = (f32[128,256]{1,0:T(8,128)}, f32[128,256]{1,0:T(8,128)S(1)}, u32[]{:S(2)}) copy-start(f32[128,256]{1,0:T(8,128)S(1)} %collective-permute-done.15.refs_2_) | copy-start | bytes 393220
  117.9 29.1 %copy-start.12 = (f32[128,256]{1,0:T(8,128)}, f32[128,256]{1,0:T(8,128)S(1)}, u32[]{:S(2)}) copy-start(f32[128,256]{1,0:T(8,128)S(1)} %collective-permute-done.16.refs_3_) | copy-start | bytes 393220
  117.9 20.2 %collective-permute-start.17 = (f32[4,64,256]{2,1,0:T(8,128)S(1)}, f32[4,64,256]{2,1,0:T(8,128)S(1)}, u32[]{:S(2)}, u32[]{:S(2)}) collective-permute-start(f32[4,64,256]{2,1,0:T(8,128)S(1)} %pad_maximum_fusion.2), channel_id=1, source_target_pairs={{0,8},{1,9},{2,10},{3,11},{4,12},{5,13},{6,14},{7,15},{8,0},{9,1},... | collective-permute-start | bytes 786440 | tf_op jit(solution)/shard_map/ppermute | solution.py:40
  124.8 13.3 %collective-permute-start.18 = (f32[128,256]{1,0:T(8,128)}, f32[128,256]{1,0:T(8,128)S(1)}, u32[]{:S(2)}, u32[]{:S(2)}) collective-permute-start(f32[128,256]{1,0:T(8,128)} %shard_map.71.refs_0_), channel_id=1, source_target_pairs={{0,64},{1,65},{2,66},{3,67},{4,68},{5,69},{6,70},{7,71},{8,72},{9,... | collective-permute-start | bytes 393224 | tf_op jit(solution)/shard_map/ppermute | solution.py:40
  126.1 12.0 %collective-permute-start.19 = (f32[128,256]{1,0:T(8,128)}, f32[128,256]{1,0:T(8,128)S(1)}, u32[]{:S(2)}, u32[]{:S(2)}) collective-permute-start(f32[128,256]{1,0:T(8,128)} %shard_map.71.refs_0_), channel_id=1, source_target_pairs={{0,80},{1,81},{2,82},{3,83},{4,84},{5,85},{6,86},{7,87},{8,88},{9,... | collective-permute-start | bytes 393224 | tf_op jit(solution)/shard_map/ppermute | solution.py:40
  130.1 8.1 %collective-permute-start.20 = (f32[128,256]{1,0:T(8,128)}, f32[128,256]{1,0:T(8,128)S(1)}, u32[]{:S(2)}, u32[]{:S(2)}) collective-permute-start(f32[128,256]{1,0:T(8,128)} %shard_map.71.refs_0_), channel_id=1, source_target_pairs={{0,96},{1,97},{2,98},{3,99},{4,100},{5,101},{6,102},{7,103},{8,104... | collective-permute-start | bytes 393224 | tf_op jit(solution)/shard_map/ppermute | solution.py:40
  135.0 5.3 %collective-permute-start.21 = (f32[128,256]{1,0:T(8,128)}, f32[128,256]{1,0:T(8,128)S(1)}, u32[]{:S(2)}, u32[]{:S(2)}) collective-permute-start(f32[128,256]{1,0:T(8,128)} %shard_map.71.refs_0_), channel_id=1, source_target_pairs={{0,112},{1,113},{2,114},{3,115},{4,116},{5,117},{6,118},{7,119},{8... | collective-permute-start | bytes 393224 | tf_op jit(solution)/shard_map/ppermute | solution.py:40
  138.1 8.9 %copy-start.1 = (f32[8,64,256]{2,1,0:T(8,128)}, f32[8,64,256]{2,1,0:T(8,128)S(1)}, u32[]{:S(2)}) copy-start(f32[8,64,256]{2,1,0:T(8,128)S(1)} %pad_maximum_fusion.1.refs_9_.refs_1_) | copy-start | bytes 1572868
  138.1 13.9 %copy-start.3 = (bf16[1024,1024]{1,0:T(8,128)(2,1)S(1)}, bf16[1024,1024]{1,0:T(8,128)(2,1)}, u32[]{:S(2)}) copy-start(bf16[1024,1024]{1,0:T(8,128)(2,1)} %cand_ref.1) | copy-start | bytes 6291460
  138.1 8.9 %copy-start.13 = (f32[128,256]{1,0:T(8,128)}, f32[128,256]{1,0:T(8,128)S(1)}, u32[]{:S(2)}) copy-start(f32[128,256]{1,0:T(8,128)S(1)} %collective-permute-done.18.refs_4_) | copy-start | bytes 393220
  138.2 8.9 %copy-start.14 = (f32[128,256]{1,0:T(8,128)}, f32[128,256]{1,0:T(8,128)S(1)}, u32[]{:S(2)}) copy-start(f32[128,256]{1,0:T(8,128)S(1)} %collective-permute-done.19.refs_5_) | copy-start | bytes 393220
  138.2 8.8 %copy-start.15 = (f32[128,256]{1,0:T(8,128)}, f32[128,256]{1,0:T(8,128)S(1)}, u32[]{:S(2)}) copy-start(f32[128,256]{1,0:T(8,128)S(1)} %collective-permute-done.20.refs_6_) | copy-start | bytes 393220
  140.3 6.7 %copy-start.16 = (f32[128,256]{1,0:T(8,128)}, f32[128,256]{1,0:T(8,128)S(1)}, u32[]{:S(2)}) copy-start(f32[128,256]{1,0:T(8,128)S(1)} %collective-permute-done.21.refs_7_) | copy-start | bytes 393220
  140.3 6.7 %collective-permute-start.22 = (f32[8,64,256]{2,1,0:T(8,128)S(1)}, f32[8,64,256]{2,1,0:T(8,128)S(1)}, u32[]{:S(2)}, u32[]{:S(2)}) collective-permute-start(f32[8,64,256]{2,1,0:T(8,128)S(1)} %pad_maximum_fusion.1.refs_9_.refs_1_), channel_id=1, source_target_pairs={{0,1},{1,0},{2,3},{3,2},{4,5},{5,4},{6,7},{7,6},{8,9},{9,8},{10,11... | collective-permute-start | bytes 1572872 | tf_op jit(solution)/shard_map/ppermute | solution.py:40
  147.0 0.8 copy-start.2
  152.0 1.6 copy-start.20
Sparse Core Ops, SparseCore 0:
  11.7 126.6 all-gather.3
  152.1 35.6 all-gather.5
